TPU v7x, 32 devices: a whole 2x2x4 slice. The times are simulated.
32 devices in a mesh: dp: 8 (over z, y), seq: 4 (over x, core).
Axes of the slice: x: 2, y: 2, z: 4, core: 2. Of those that a mesh axis runs over, the one named last changes fastest.
Arguments:
- hidden_in: bfloat16 [128, 512, 768], P('dp', 'seq'), may hold values from -6 to 6
- segment_ids: int32 [128, 512], P('dp'), may hold values from 0 to 2, as said below
- cluster_perm: int32 [128, 12, 512], P('dp'), may hold values from 0 to 511, each once within a row
- w_qkv: bfloat16 [768, 2304], replicated, may hold values from -0.21875 to 0.21875
- bias_qv: float32 [1536], replicated, may hold values from -3 to 3
- w_out: bfloat16 [768, 768], replicated, may hold values from -0.875 to 0.875
- bias_out: float32 [768], replicated, may hold values from -2 to 2
- gain_attn: float32 [768], replicated, may hold values from 0.5 to 1.5
- shift_attn: float32 [768], replicated, may hold values from -2 to 2
- w_up: bfloat16 [768, 3072], replicated, may hold values from -0.21875 to 0.21875
- bias_up: float32 [3072], replicated, may hold values from -3 to 3
- w_down: bfloat16 [3072, 768], replicated, may hold values from -0.109375 to 0.109375
- bias_down: float32 [768], replicated, may hold values from -2 to 2
- gain_ffn: float32 [768], replicated, may hold values from 0.5 to 1.5
- shift_ffn: float32 [768], replicated, may hold values from -2 to 2
- grad_out: bfloat16 [128, 512, 768], P('dp', 'seq'), may hold values from -6 to 6
Outputs:
- out_hidden: bfloat16 [128, 512, 768], P('dp', 'seq')
- grad_in: bfloat16 [128, 512, 768], P('dp', 'seq')
- grad_w_qkv: float32 [768, 2304], P(('dp', 'seq'))
- grad_bias_qv: float32 [1536], P(('dp', 'seq'))
- grad_w_out: float32 [768, 768], P(('dp', 'seq'))
- grad_bias_out: float32 [768], P(('dp', 'seq'))
- grad_gain_attn: float32 [768], P(('dp', 'seq'))
- grad_shift_attn: float32 [768], P(('dp', 'seq'))
- grad_w_up: float32 [768, 3072], P(('dp', 'seq'))
- grad_bias_up: float32 [3072], P(('dp', 'seq'))
- grad_w_down: float32 [3072, 768], P(('dp', 'seq'))
- grad_bias_down: float32 [768], P(('dp', 'seq'))
- grad_gain_ffn: float32 [768], P(('dp', 'seq'))
- grad_shift_ffn: float32 [768], P(('dp', 'seq'))
Inputs may be any that keep to these rules, and one draw needn't show every extreme that they name: `cluster_perm`: for each row and head, a permutation of the row's 512 positions; a head's cluster c holds the tokens at its entries c * 128 to (c + 1) * 128 - 1. `segment_ids`: each row holds documents 0, 1, 2 in order; document 0 ends within the row's first 128 tokens and document 2 begins within its last 128 tokens.
All inputs are finite; a program needn't handle non-finite values.
Results may differ from a plain program's by a relative error of at most 0.015.
Values may be sent and summed in bfloat16 or wider, within the bound.
No kernel may reach another device: no remote copies, remote signals or barrier semaphores. Data moves between devices by JAX's collectives and lax.ppermute only.
A program may use at most 256 MiB of HBM per device.

v0:
```python
import math

import jax
import jax.numpy as jnp
from jax import lax
from jax.sharding import PartitionSpec as P

CL = 128


norm_eps = 1e-05
masked_value = -1e30


def layer_norm(values, gain_vec, shift_vec):
    center = values - jnp.mean(values, -1, keepdims=True)
    inverse = lax.rsqrt(jnp.mean(center * center, -1, keepdims=True) + norm_eps)
    normed = center * inverse
    return (normed * gain_vec + shift_vec, normed, inverse)


def norm_back(upstream, normed, inverse, gain_vec):
    scaled = upstream * gain_vec
    inner_term = (
        scaled
        - jnp.mean(scaled, -1, keepdims=True)
        - normed * jnp.mean(scaled * normed, -1, keepdims=True)
    )
    return (inverse * inner_term, jnp.sum(upstream * normed, 0), jnp.sum(upstream, 0))


def gelu_exact(values):
    return 0.5 * values * (1.0 + lax.erf(values * 0.7071067811865476))


def gelu_slope(values):
    return (
        0.5 * (1.0 + lax.erf(values * 0.7071067811865476))
        + values * jnp.exp(-0.5 * values * values) * 0.3989422804014327
    )


def cluster_table(order_table):
    row_count, head_count, length = order_table.shape
    member = jnp.arange(length, dtype=jnp.int32) // CL
    row_index = jnp.arange(row_count, dtype=jnp.int32)[:, None, None]
    head_index = jnp.arange(head_count, dtype=jnp.int32)[None, :, None]
    return (
        jnp.zeros(order_table.shape, jnp.int32)
        .at[row_index, head_index, order_table]
        .set(jnp.broadcast_to(member, order_table.shape))
    )


def split_heads(row_array, head_count):
    return row_array.reshape(row_array.shape[0], head_count, row_array.shape[1] // head_count)


def allowed_mask(own_cl, cluster_row, own_seg, segment_row):
    same_cluster = own_cl[:, :, None] == cluster_row[:, None, :]
    same_doc = own_seg[:, None] == segment_row[None, :]
    return same_cluster & same_doc[None, :, :]


def shards(
    hidden_in,
    segment_ids,
    cluster_perm,
    w_qkv,
    bias_qv,
    w_out,
    bias_out,
    gain_attn,
    shift_attn,
    w_up,
    bias_up,
    w_down,
    bias_down,
    gain_ffn,
    shift_ffn,
    grad_out,
):
    row_count, block_len, model_width = hidden_in.shape
    head_count = cluster_perm.shape[1]
    head_size = model_width // head_count
    score_scale = 1.0 / math.sqrt(head_size)
    tokens = row_count * block_len
    block_start = lax.axis_index("seq") * block_len
    clusters = cluster_table(cluster_perm)
    own_cluster = lax.dynamic_slice_in_dim(clusters, block_start, block_len, 2)
    own_segment = lax.dynamic_slice_in_dim(segment_ids, block_start, block_len, 1)
    inputs = hidden_in.reshape(tokens, model_width)
    bias_full = jnp.concatenate(
        [bias_qv[:model_width], jnp.zeros((model_width,), jnp.float32), bias_qv[model_width:]]
    )
    projected = (jnp.dot(inputs, w_qkv, preferred_element_type=jnp.float32) + bias_full).astype(
        jnp.bfloat16
    )
    queries = projected[:, :model_width].reshape(row_count, block_len, head_count, head_size)
    kv_local = projected[:, model_width:].reshape(row_count, block_len, 2 * model_width)
    kv_whole = lax.all_gather(kv_local, "seq", axis=1, tiled=True)

    def attend_row(item):
        query_row, kv_row, cluster_row, own_cl, own_seg, segment_row = item
        keys_row = split_heads(kv_row[:, :model_width], head_count)
        values_row = split_heads(kv_row[:, model_width:], head_count)
        scores = (
            jnp.einsum("ihd,jhd->hij", query_row, keys_row, preferred_element_type=jnp.float32)
            * score_scale
        )
        allowed = allowed_mask(own_cl, cluster_row, own_seg, segment_row)
        masked = jnp.where(allowed, scores, masked_value)
        row_peak = jnp.max(masked, -1, keepdims=True)
        exponent = jnp.exp(masked - row_peak)
        row_total = jnp.sum(exponent, -1, keepdims=True)
        prob_low = (exponent / row_total).astype(jnp.bfloat16)
        attended_row = jnp.einsum(
            "hij,jhd->ihd", prob_low, values_row, preferred_element_type=jnp.float32
        )
        return (attended_row, (row_peak + jnp.log(row_total))[..., 0])

    attended, logsum = lax.map(
        attend_row, (queries, kv_whole, clusters, own_cluster, own_segment, segment_ids)
    )
    attended_low = attended.reshape(tokens, model_width).astype(jnp.bfloat16)
    branch = jnp.dot(attended_low, w_out, preferred_element_type=jnp.float32) + bias_out
    first_norm, normed_one, inverse_one = layer_norm(
        inputs.astype(jnp.float32) + branch, gain_attn, shift_attn
    )
    first_low = first_norm.astype(jnp.bfloat16)
    pre_act = jnp.dot(first_low, w_up, preferred_element_type=jnp.float32) + bias_up
    act_low = gelu_exact(pre_act).astype(jnp.bfloat16)
    ffn_out = jnp.dot(act_low, w_down, preferred_element_type=jnp.float32) + bias_down
    final_norm, normed_two, inverse_two = layer_norm(
        first_low.astype(jnp.float32) + ffn_out, gain_ffn, shift_ffn
    )
    out_hidden = final_norm.astype(jnp.bfloat16).reshape(row_count, block_len, model_width)
    upstream = grad_out.reshape(tokens, model_width).astype(jnp.float32)
    grad_two, gain_ffn_grad, shift_ffn_grad = norm_back(upstream, normed_two, inverse_two, gain_ffn)
    grad_ffn_low = grad_two.astype(jnp.bfloat16)
    down_grad = jnp.dot(act_low.T, grad_ffn_low, preferred_element_type=jnp.float32)
    bias_down_grad = jnp.sum(grad_ffn_low.astype(jnp.float32), 0)
    grad_act = jnp.dot(grad_ffn_low, w_down.T, preferred_element_type=jnp.float32)
    grad_pre_low = (grad_act * gelu_slope(pre_act)).astype(jnp.bfloat16)
    up_grad = jnp.dot(first_low.T, grad_pre_low, preferred_element_type=jnp.float32)
    bias_up_grad = jnp.sum(grad_pre_low.astype(jnp.float32), 0)
    grad_first = jnp.dot(grad_pre_low, w_up.T, preferred_element_type=jnp.float32) + grad_two
    grad_one, gain_attn_grad, shift_attn_grad = norm_back(
        grad_first, normed_one, inverse_one, gain_attn
    )
    grad_branch_low = grad_one.astype(jnp.bfloat16)
    out_grad = jnp.dot(attended_low.T, grad_branch_low, preferred_element_type=jnp.float32)
    bias_out_grad = jnp.sum(grad_branch_low.astype(jnp.float32), 0)
    grad_att_low = (
        jnp.dot(grad_branch_low, w_out.T, preferred_element_type=jnp.float32)
        .astype(jnp.bfloat16)
        .reshape(row_count, block_len, head_count, head_size)
    )

    def query_back(item):
        query_row, kv_row, cluster_row, own_cl, own_seg, segment_row, logsum_row, grad_row = item
        keys_row = split_heads(kv_row[:, :model_width], head_count)
        values_row = split_heads(kv_row[:, model_width:], head_count)
        scores = (
            jnp.einsum("ihd,jhd->hij", query_row, keys_row, preferred_element_type=jnp.float32)
            * score_scale
        )
        allowed = allowed_mask(own_cl, cluster_row, own_seg, segment_row)
        attn_prob = jnp.exp(jnp.where(allowed, scores - logsum_row[..., None], masked_value))
        grad_prob = jnp.einsum(
            "ihd,jhd->hij", grad_row, values_row, preferred_element_type=jnp.float32
        )
        row_delta = jnp.sum(attn_prob * grad_prob, -1, keepdims=True)
        grad_score_low = (attn_prob * (grad_prob - row_delta)).astype(jnp.bfloat16)
        grad_query_row = (
            jnp.einsum("hij,jhd->ihd", grad_score_low, keys_row, preferred_element_type=jnp.float32)
            * score_scale
        )
        key_part = (
            jnp.einsum(
                "hij,ihd->jhd", grad_score_low, query_row, preferred_element_type=jnp.float32
            )
            * score_scale
        )
        value_part = jnp.einsum(
            "hij,ihd->jhd",
            attn_prob.astype(jnp.bfloat16),
            grad_row,
            preferred_element_type=jnp.float32,
        )
        length = kv_row.shape[0]
        partial_row = jnp.concatenate(
            [key_part.reshape(length, model_width), value_part.reshape(length, model_width)], -1
        )
        return (grad_query_row, row_delta[..., 0], partial_row)

    back_items = (
        queries,
        kv_whole,
        clusters,
        own_cluster,
        own_segment,
        segment_ids,
        logsum,
        grad_att_low,
    )
    grad_queries, row_delta, partial_grads = lax.map(lambda item: query_back(item), back_items)
    kv_grad = lax.psum_scatter(
        partial_grads.astype(jnp.bfloat16), "seq", scatter_dimension=1, tiled=True
    )
    kv_grad_low = kv_grad.reshape(tokens, 2 * model_width)
    grad_query_low = grad_queries.reshape(tokens, model_width).astype(jnp.bfloat16)
    grad_qkv_low = jnp.concatenate([grad_query_low, kv_grad_low], -1)
    qkv_grad = jnp.dot(inputs.T, grad_qkv_low, preferred_element_type=jnp.float32)
    bias_qv_grad = jnp.concatenate(
        [
            jnp.sum(grad_query_low.astype(jnp.float32), 0),
            jnp.sum(kv_grad_low[:, model_width:].astype(jnp.float32), 0),
        ]
    )
    grad_in = (
        (jnp.dot(grad_qkv_low, w_qkv.T, preferred_element_type=jnp.float32) + grad_one)
        .astype(jnp.bfloat16)
        .reshape(row_count, block_len, model_width)
    )
    summed = (
        lax.psum_scatter(qkv_grad, ("dp", "seq"), scatter_dimension=0, tiled=True),
        lax.psum_scatter(bias_qv_grad, ("dp", "seq"), scatter_dimension=0, tiled=True),
        lax.psum_scatter(out_grad, ("dp", "seq"), scatter_dimension=0, tiled=True),
        lax.psum_scatter(bias_out_grad, ("dp", "seq"), scatter_dimension=0, tiled=True),
        lax.psum_scatter(gain_attn_grad, ("dp", "seq"), scatter_dimension=0, tiled=True),
        lax.psum_scatter(shift_attn_grad, ("dp", "seq"), scatter_dimension=0, tiled=True),
        lax.psum_scatter(up_grad, ("dp", "seq"), scatter_dimension=0, tiled=True),
        lax.psum_scatter(bias_up_grad, ("dp", "seq"), scatter_dimension=0, tiled=True),
        lax.psum_scatter(down_grad, ("dp", "seq"), scatter_dimension=0, tiled=True),
        lax.psum_scatter(bias_down_grad, ("dp", "seq"), scatter_dimension=0, tiled=True),
        lax.psum_scatter(gain_ffn_grad, ("dp", "seq"), scatter_dimension=0, tiled=True),
        lax.psum_scatter(shift_ffn_grad, ("dp", "seq"), scatter_dimension=0, tiled=True),
    )
    return (out_hidden, grad_in) + tuple(summed)


def solution(mesh):
    return jax.shard_map(
        shards,
        mesh=mesh,
        in_specs=(
            P("dp", "seq", None),
            P("dp", None),
            P("dp", None, None),
            P(),
            P(),
            P(),
            P(),
            P(),
            P(),
            P(),
            P(),
            P(),
            P(),
            P(),
            P(),
            P("dp", "seq", None),
        ),
        out_specs=(
            P("dp", "seq", None),
            P("dp", "seq", None),
            P(("dp", "seq"), None),
            P(("dp", "seq")),
            P(("dp", "seq"), None),
            P(("dp", "seq")),
            P(("dp", "seq")),
            P(("dp", "seq")),
            P(("dp", "seq"), None),
            P(("dp", "seq")),
            P(("dp", "seq"), None),
            P(("dp", "seq")),
            P(("dp", "seq")),
            P(("dp", "seq")),
        ),
        check_vma=False,
    )
```

profile of v0, /device:TPU:0, one launch (start us, length us, event | category | flops | bytes accessed | tf_op | source)
XLA Modules:
  0.0 1776.7 jit_solution(15353957622133228554)
XLA Ops:
  9.2 9.8 add_convert_fusion
  19.1 3.5 slice.36
  24.5 8.6 copy.50
  33.2 3.8 slice.37
  44.3 360.3 %scatter_custom_fusion = s32[98304]{0:T(1024)} fusion(s32[98304]{0:T(1024)} %reshape.247, s32[98304]{0:T(1024)} %reshape.249, s32[]{:T(128)} %copy.128), kind=kCustom, calls=%fused_computation.107 | custom fusion | bytes 393728
  410.1 4.6 copy.52
  414.7 3.1 copy.87
  426.0 150.8 %while.24 = (s32[]{:T(128)}, bf16[16,128,12,64]{1,3,2,0:T(8,128)(2,1)}, f32[16,12,128]{2,1,0:T(8,128)}, bf16[16,512,1536]{1,2,0:T(8,128)(2,1)}, s32[16,12,128]{2...) while((s32[]{:T(128)}, ...), condition=%wide.region_4.5_spmd, body=%wide.region_1.4_spmd.sunk | while | flops 209254912 | bytes 18175096 | solution.py:122
  576.9 4.5 copy.56
  581.4 3.6 fusion.65
  586.0 17.8 %multiply_convert_fusion.1 = (bf16[2048,3072]{1,0:T(8,128)(2,1)}, f32[2048,3072]{1,0:T(8,128)}) fusion(f32[3072]{0:T(1024)S(1)} %copy-done.23, bf16[768,3072]{1,0:T(8,128)(2,1)S(1)} %bitcast.235, f32[2048,768]{1,0:T(8,128)S(1)} %get-tuple-element.298, f32[768]{0:T(1024)S(1)} %copy-done.26, f32[768]{0:T(1024)S(1)} %copy-done.18, ...), kind=kOutput, calls=%fused_computation.59 | convolution fusion | flops 9709289472 | bytes 48793600 | tf_op jit(solution)/shard_map/dot_general | solution.py:131
  603.9 15.3 fusion.66
  621.0 3.0 fusion.38
  624.1 4.5 convert_reduce_fusion.2
  628.6 24.1 %convert_reduce_fusion = (f32[3072]{0:T(1024)}, bf16[2048,3072]{1,0:T(8,128)(2,1)}) fusion(f32[2048,3072]{1,0:T(8,128)} %get-tuple-element.300, f32[3072]{0:T(1024)S(1)} %copy-done.23, bf16[3072,768]{1,0:T(8,128)(2,1)S(1)} %bitcast.233, f32[2048,768]{1,0:T(8,128)S(1)} %get-tuple-element.283), kind=kOutput, calls=%fused_computation.58 | convolution fusion | flops 9747035136 | bytes 48783360 | tf_op jit(solution)/shard_map/dot_general | solution.py:143
  652.7 21.1 %multiply_reduce_fusion.1 = (f32[768]{0:T(1024)}, f32[2048]{0:T(1024)S(1)}, f32[2048]{0:T(1024)S(1)}, f32[768]{0:T(1024)}, f32[2048,768]{1,0:T(8,128)}) fusion(f32[2048,768]{1,0:T(8,128)} %copy-done.5, f32[2048]{0:T(1024)S(1)} %add_rsqrt_fusion.1, f32[2048]{0:T(1024)S(1)} %broadcast_multiply_fusion.4, f32[768]{0:T(1024)S(1)} %copy-done.18, ...), kind=kOutput, calls=%fused_computation.75 | convolution fusion | flops 9679398912 | bytes 36217856 | tf_op jit(solution)/shard_map/dot_general | solution.py:147
  673.7 6.5 convert_reduce_fusion.3
  682.9 4.0 convolution_convert_fusion
  686.9 4.7 copy.57
  699.5 373.4 %while.25 = (s32[]{:T(128)}, bf16[16,128,12,64]{1,3,2,0:T(8,128)(2,1)}, bf16[16,512,1536]{2,1,0:T(8,128)(2,1)}, bf16[16,512,1536]{1,2,0:T(8,128)(2,1)}, s32[16,1...) while((s32[]{:T(128)}, ...), condition=%wide.region_15.16_spmd, body=%wide.region_13.15_spmd.sunk | while | flops 516061696 | bytes 54135492 | solution.py:207
  720.1 3.0 fusion.129
  766.7 3.0 fusion.129
  790.1 3.0 fusion.129
  813.4 3.0 fusion.129
  836.7 3.0 fusion.129
  883.4 3.0 fusion.129
  906.7 3.0 fusion.129
  930.0 3.0 fusion.129
  976.7 3.0 fusion.129
  1000.0 3.0 fusion.129
  1023.3 3.0 fusion.129
  1046.7 3.0 fusion.129
  1070.0 3.0 fusion.129
  1073.0 7.7 fusion.42
  1080.9 21.2 %fusion.67 = f32[768,3072]{1,0:T(8,128)} fusion(bf16[2048,3072]{1,0:T(8,128)(2,1)} %get-tuple-element.305, f32[2048,768]{1,0:T(8,128)} %copy-done.5, f32[768]{0:T(1024)} %param.28, f32[768]{0:T(1024)} %param.27, f32[2048]{0:T(1024)S(1)} %copy-done.13, f32[2048]{0:T(1024)S(1)} %broadcast_multiply_fusion.4), kind=kOutput, calls=%fused_computation.142 | convolution fusion | flops 9671540736 | bytes 28334080 | tf_op jit(solution)/shard_map/dot_general | solution.py:145
  1102.2 19.7 %fusion.57 = f32[3072,768]{1,0:T(8,128)} fusion(bf16[2048,3072]{1,0:T(8,128)(2,1)} %get-tuple-element.299, f32[2048,768]{1,0:T(8,128)} %copy-done.8), kind=kOutput, calls=%fused_computation.133 | convolution fusion | flops 9665249280 | bytes 28311552 | tf_op jit(solution)/shard_map/dot_general | solution.py:141
  1122.0 4.3 copy.62
  1126.3 3.0 copy.102
  1129.3 5.0 copy.64
  1134.4 122.2 %reduce-scatter.8.cloned.1.call-done = bf16[16,128,1536]{2,1,0:T(8,128)(2,1)} async-done(((bf16[16,512,1536]{2,1,0:T(8,128)(2,1)}), bf16[16,128,1536]{2,1,0:T(8,128)(2,1)}) %reduce-scatter.8.cloned.1.call-update) | async-done | bytes 6291472 | tf_op jit(solution)/shard_map/reduce_scatter | solution.py:208
  1256.5 13.2 fusion.41
  1269.8 8.1 copy.66
  1284.2 41.1 %all-reduce.8 = (f32[1536]{0:T(1024)}, f32[768]{0:T(1024)}, f32[768]{0:T(1024)}, f32[768]{0:T(1024)}, f32[3072]{0:T(1024)}, /*index=5*/f32[768]{0:T(1024)}, f32[768]{0:T(1024)}, f32[768]{0:T(1024)}) all-reduce(f32[1536]{0:T(1024)S(1)} %pad_maximum_fusion.8, ...), channel_id=4, replica_groups=mesh['dp'=8,'seq'=4] {'dp','seq'}, use_global_device_ids=true, to_apply=%region_20.21.clone | all-reduce | flops 9216 | bytes 73728
  1335.4 12.2 add_convert_fusion.1
  1347.6 14.7 reduce-scatter.10.cloned.1.call-done
  1362.3 141.0 %reduce-scatter.12.cloned.1.call-done = f32[24,3072]{1,0:T(8,128)} async-done(((f32[768,3072]{1,0:T(8,128)}), f32[24,3072]{1,0:T(8,128)}) %reduce-scatter.12.cloned.1.call-update) | async-done | bytes 294928 | tf_op jit(solution)/shard_map/reduce_scatter | solution.py:233
  1503.3 141.8 %reduce-scatter.14.cloned.1.call-done = f32[96,768]{1,0:T(8,128)} async-done(((f32[3072,768]{1,0:T(8,128)}), f32[96,768]{1,0:T(8,128)}) %reduce-scatter.14.cloned.1.call-update) | async-done | bytes 294928 | tf_op jit(solution)/shard_map/reduce_scatter | solution.py:235
  1645.1 124.4 %reduce-scatter.16.cloned.1.call-done = f32[24,2304]{1,0:T(8,128)} async-done(((f32[768,2304]{1,0:T(8,128)}), f32[24,2304]{1,0:T(8,128)}) %reduce-scatter.16.cloned.1.call-update) | async-done | bytes 221200
  (620 shorter events, 538.4 us)
Async XLA Ops:
  7.2 2.0 copy-start
  7.2 416.4 %all-gather.2.cloned.1.call-start = ((), (), s32[]{:S(2)}) async-start(), calls=%async_computation.5 | async-start | bytes 31457280 | tf_op jit(solution)/shard_map/all_gather | solution.py:101
  19.0 5.5 copy-start.6
  33.1 5.0 copy-start.20
  33.2 5.1 copy-start.19
  33.2 1223.4 %reduce-scatter.8.cloned.1.call-start = ((), (), s32[]{:S(2)}) async-start(), calls=%async_computation.6 | async-start | bytes 31457280 | tf_op jit(solution)/shard_map/reduce_scatter | solution.py:208
  414.7 6.2 copy-start.3
  414.7 6.2 copy-start.10
  576.8 8.2 copy-start.16
  576.8 4.6 copy-start.21
  576.8 4.6 copy-start.22
  576.8 4.5 copy-start.24
  581.3 3.7 copy-start.9
  581.4 4.6 slice-start.2
  581.4 4.6 slice-start.3
  585.0 18.8 %copy-start.5 = (f32[2048,768]{1,0:T(8,128)}, f32[2048,768]{1,0:T(8,128)S(1)}, u32[]{:S(2)}) copy-start(f32[2048,768]{1,0:T(8,128)S(1)} %get-tuple-element.298) | copy-start | bytes 18874372
  586.0 87.7 %copy-start.12 = (f32[2048]{0:T(1024)}, f32[2048]{0:T(1024)S(1)}, u32[]{:S(2)}) copy-start(f32[2048]{0:T(1024)S(1)} %add_rsqrt_fusion.1) | copy-start | bytes 24580
  586.0 17.8 %copy-start.25 = (f32[768]{0:T(1024)S(1)}, f32[768]{0:T(1024)}, u32[]{:S(2)}) copy-start(f32[768]{0:T(1024)} %param.32) | copy-start | bytes 9220
  619.1 1.9 copy-start.4
  620.0 4.1 copy-start.11
  620.0 4.1 copy-start.17
  621.0 7.6 slice-start
  624.1 4.5 slice-start.1
  628.6 24.1 %copy-start.8 = (f32[2048,768]{1,0:T(8,128)}, f32[2048,768]{1,0:T(8,128)S(1)}, u32[]{:S(2)}) copy-start(f32[2048,768]{1,0:T(8,128)S(1)} %get-tuple-element.283) | copy-start | bytes 18874372
  680.3 2.6 copy-start.7
  701.3 8.0 copy-start.2
  724.7 8.0 copy-start.2
  748.0 8.0 copy-start.2
  771.4 8.0 copy-start.2
  794.7 8.0 copy-start.2
  818.0 8.0 copy-start.2
  841.3 8.0 copy-start.2
  864.6 8.0 copy-start.2
  888.0 8.0 copy-start.2
  911.3 8.0 copy-start.2
  934.6 8.0 copy-start.2
  958.0 8.0 copy-start.2
  981.3 8.0 copy-start.2
  1004.6 8.0 copy-start.2
  1027.9 8.0 copy-start.2
  1051.3 8.0 copy-start.2
  1073.0 7.9 copy-start.13
  1073.0 289.3 %reduce-scatter.10.cloned.1.call-start = ((), (), s32[]{:S(2)}) async-start(), calls=%async_computation.7 | async-start | bytes 2433024 | tf_op jit(solution)/shard_map/reduce_scatter | solution.py:229
  1080.8 422.5 %reduce-scatter.12.cloned.1.call-start = ((), (), s32[]{:S(2)}) async-start(), calls=%async_computation.8 | async-start | bytes 9732096 | tf_op jit(solution)/shard_map/reduce_scatter | solution.py:233
  1102.1 543.0 %reduce-scatter.14.cloned.1.call-start = ((), (), s32[]{:S(2)}) async-start(), calls=%async_computation.9 | async-start | bytes 9732096 | tf_op jit(solution)/shard_map/reduce_scatter | solution.py:235
  1121.9 647.6 %reduce-scatter.16.cloned.1.call-start = ((), (), s32[]{:S(2)}) async-start(), calls=%async_computation.10 | async-start | bytes 7299072
  1277.9 6.3 copy-start.14
  1277.9 6.3 copy-start.15
  (19 other events, 21.9 us)
Sparse Core Ops, SparseCore 0:
  33.3 160.8 all-gather.1
  1073.1 183.3 reduce-scatter.7
  1263.3 98.9 reduce-scatter.9
  1368.6 134.6 reduce-scatter.11
  1510.7 134.4 reduce-scatter.13
  1651.3 118.2 reduce-scatter.15
where the time goes:
time: 1790 us; the launch traced here: 1780 us
  local copies, waits for them, and re-layouts  704 us (39%)
  waiting for transfers between devices  544 us (30%)
  matrix products  391 us (22%)
  other arithmetic  79.4 us (4%)
  blocking collectives  41.1 us (2%)
    unnamed x74, local copies, waits for them, and re-layouts  399 us
    reduce_scatter x1, waiting for transfers between devices, shards(): lax.psum_scatter(down_grad, ('dp', 'seq'), scatter_dimension=0, tiled=True)  142 us
    reduce_scatter x1, waiting for transfers between devices, shards(): lax.psum_scatter(up_grad, ('dp', 'seq'), scatter_dimension=0, tiled=True)  141 us
    unnamed x7, waiting for transfers between devices  125 us
    reduce_scatter x1, waiting for transfers between devices, shards(): lax.psum_scatter(partial_grads.astype(jnp.bfloat16), 'seq', scatter_dimen...  122 us
    dynamic_update_slice x32, local copies, waits for them, and re-layouts, shards(): lax.map(lambda item: query_back(item), back_items)  83.9 us
    squeeze x32, local copies, waits for them, and re-layouts, shards(): lax.map(attend_row, (queries, kv_whole, clusters, own_cluster, own_segmen...  48.4 us
    dot_general x16, matrix products, query_back(): jnp.einsum('hij,jhd->ihd', grad_score_low, keys_row, preferred_element_ty...  47.7 us
  transfers between devices with their start and end apart: 6, of which 5 were waited for; matrix products, arithmetic and copies ran while one was open for 28% of the time, Pallas kernels for 0%

commit v1 on v0

v1 whole, which is shorter than its diff:
```python
import functools
import math

import jax
import jax.numpy as jnp
from jax import lax
from jax.experimental import pallas as pl
from jax.experimental.pallas import tpu as pltpu
from jax.sharding import PartitionSpec as P

CL = 128
DOCS = 3
CODES = 16
NORM_EPS = 1e-05
BIG = 2.0**50
F32 = jnp.float32
BF16 = jnp.bfloat16
NN = (((1,), (0,)), ((), ()))
NT = (((1,), (1,)), ((), ()))
TN = (((0,), (0,)), ((), ()))
VMEM = 62 * 2**20


def mm(a, b, dims=NN):
    return lax.dot_general(a, b, dims, preferred_element_type=F32)


def whole(shape):
    return pl.BlockSpec(shape, lambda i: (0,) * len(shape), pipeline_mode=pl.Buffered(1))


def lead(shape):
    return pl.BlockSpec((1,) + shape, lambda i: (i,) + (0,) * len(shape))


def rows_of(tile, width):
    return pl.BlockSpec((tile, width), lambda i: (i, 0))


def shape_of(shape, dtype):
    return jax.ShapeDtypeStruct(shape, dtype)


def params():
    return pltpu.CompilerParams(vmem_limit_bytes=VMEM)


def cost(flops, nbytes):
    return pl.CostEstimate(flops=int(flops), bytes_accessed=int(nbytes), transcendentals=0)


def attend_kernel(
    x_ref, code_ref, wt_ref, bt_ref, wo_ref, bo_ref, ga_ref, sa_ref,
    qkv_ref, p_ref, il_ref, att_ref, first_ref, n_ref, s_ref, *, heads, hs,
):
    D = heads * hs
    x = x_ref[0]
    L = x.shape[0]
    qkv_ref[0] = (mm(wt_ref[...], x, NT) + bt_ref[...]).astype(BF16)
    it = lax.broadcasted_iota(jnp.int32, (CODES, L), 0)
    for h in range(heads):
        q = qkv_ref[0, h * hs : (h + 1) * hs, :]
        k = qkv_ref[0, D + h * hs : D + (h + 1) * hs, :]
        v = qkv_ref[0, 2 * D + h * hs : 2 * D + (h + 1) * hs, :]
        same = it == code_ref[0, h : h + 1, :]
        qa = jnp.concatenate([q, jnp.where(same, BIG, 0.0).astype(BF16)], 0)
        ka = jnp.concatenate([k, jnp.where(same, 0.0, -BIG).astype(BF16)], 0)
        s = mm(ka, qa, TN)
        e = jnp.exp(s - jnp.max(s, axis=0, keepdims=True))
        il = 1.0 / jnp.sum(e, axis=0, keepdims=True)
        p = e.astype(BF16)
        p_ref[0, h] = p
        il_ref[0, h : h + 1, :] = il
        att_ref[0, h * hs : (h + 1) * hs, :] = (mm(v, p) * il).astype(BF16)
    v1 = x.astype(F32) + mm(att_ref[0], wo_ref[...], TN) + bo_ref[...]
    c = v1 - jnp.mean(v1, -1, keepdims=True)
    s1 = lax.rsqrt(jnp.mean(c * c, -1, keepdims=True) + NORM_EPS)
    n1 = c * s1
    first_ref[0] = (n1 * ga_ref[...] + sa_ref[...]).astype(BF16)
    n_ref[0] = n1.astype(BF16)
    s_ref[0] = jnp.broadcast_to(s1, (L, 128))


def attend(x, code, wt, bt, wo, bo, ga, sa, heads, hs):
    R, L, D = x.shape
    return pl.pallas_call(
        functools.partial(attend_kernel, heads=heads, hs=hs),
        grid=(R,),
        in_specs=[
            lead((L, D)), lead((heads, L)), whole((3 * D, D)), whole((3 * D, 1)),
            whole((D, D)), whole((1, D)), whole((1, D)), whole((1, D)),
        ],
        out_specs=[
            lead((3 * D, L)), lead((heads, L, L)), lead((heads, L)), lead((D, L)),
            lead((L, D)), lead((L, D)), lead((L, 128)),
        ],
        out_shape=[
            shape_of((R, 3 * D, L), BF16), shape_of((R, heads, L, L), BF16),
            shape_of((R, heads, L), F32), shape_of((R, D, L), BF16),
            shape_of((R, L, D), BF16), shape_of((R, L, D), BF16), shape_of((R, L, 128), F32),
        ],
        compiler_params=params(),
        cost_estimate=cost(R * (8 * L * D * D + 4 * 4 * heads * L * L * hs), R * 2 * heads * L * L),
        name="attend",
    )(x, code, wt, bt, wo, bo, ga, sa)


def ffn_kernel(
    first_ref, gout_ref, wu_ref, bu_ref, wd_ref, bd_ref, gf_ref, sf_ref,
    out_ref, gffn_ref, act_ref, slope_ref, sums_ref,
):
    first = first_ref[...]
    u = mm(first, wu_ref[...]) + bu_ref[...]
    half = 0.5 * (1.0 + lax.erf(u * 0.7071067811865476))
    act = (u * half).astype(BF16)
    act_ref[...] = act
    slope_ref[...] = (half + u * jnp.exp(-0.5 * u * u) * 0.3989422804014327).astype(BF16)
    y = first.astype(F32) + mm(act, wd_ref[...]) + bd_ref[...]
    c = y - jnp.mean(y, -1, keepdims=True)
    s2 = lax.rsqrt(jnp.mean(c * c, -1, keepdims=True) + NORM_EPS)
    n2 = c * s2
    out_ref[...] = (n2 * gf_ref[...] + sf_ref[...]).astype(BF16)
    go = gout_ref[...].astype(F32)
    e = go * gf_ref[...]
    g2 = s2 * (e - jnp.mean(e, -1, keepdims=True) - n2 * jnp.mean(e * n2, -1, keepdims=True))
    gl = g2.astype(BF16)
    gffn_ref[...] = gl

    @pl.when(pl.program_id(0) == 0)
    def _():
        sums_ref[...] = jnp.zeros_like(sums_ref)

    sums_ref[0:1, :] += jnp.sum(gl.astype(F32), 0, keepdims=True)
    sums_ref[1:2, :] += jnp.sum(go * n2, 0, keepdims=True)
    sums_ref[2:3, :] += jnp.sum(go, 0, keepdims=True)


def ffn(first, gout, wu, bu, wd, bd, gf, sf, tile):
    T, D = first.shape
    FF = wu.shape[1]
    return pl.pallas_call(
        ffn_kernel,
        grid=(T // tile,),
        in_specs=[
            rows_of(tile, D), rows_of(tile, D), whole((D, FF)), whole((1, FF)),
            whole((FF, D)), whole((1, D)), whole((1, D)), whole((1, D)),
        ],
        out_specs=[
            rows_of(tile, D), rows_of(tile, D), rows_of(tile, FF), rows_of(tile, FF),
            pl.BlockSpec((8, D), lambda i: (0, 0)),
        ],
        out_shape=[
            shape_of((T, D), BF16), shape_of((T, D), BF16), shape_of((T, FF), BF16),
            shape_of((T, FF), BF16), shape_of((8, D), F32),
        ],
        compiler_params=params(),
        cost_estimate=cost(4 * T * D * FF * 1.3, 4 * T * FF + 4 * D * FF),
        name="ffn",
    )(first, gout, wu, bu, wd, bd, gf, sf)


def down_grad_kernel(act_ref, g_ref, o_ref):
    o_ref[...] = mm(act_ref[...], g_ref[...], TN).astype(BF16)


def down_grad(act, g, tile):
    T, FF = act.shape
    D = g.shape[1]
    return pl.pallas_call(
        down_grad_kernel,
        grid=(FF // tile,),
        in_specs=[pl.BlockSpec((T, tile), lambda i: (0, i)), whole((T, D))],
        out_specs=rows_of(tile, D),
        out_shape=shape_of((FF, D), BF16),
        compiler_params=params(),
        cost_estimate=cost(2 * T * D * FF * 1.3, 2 * T * FF + 2 * D * FF),
        name="down_grad",
    )(act, g)


def ffn_back_kernel(
    g_ref, slope_ref, wu_ref, wd_ref, wo_ref, n_ref, s_ref, ga_ref, att_ref, il_ref,
    gpre_ref, gone_ref, gbr_ref, do_ref, de_ref, sums_ref, bsum_ref, *, heads, hs,
):
    g = g_ref[...]
    gp = (mm(g, wd_ref[...], NT) * slope_ref[...].astype(F32)).astype(BF16)
    gpre_ref[...] = gp
    gfirst = mm(gp, wu_ref[...], NT) + g.astype(F32)
    n1 = n_ref[0].astype(F32)
    e = gfirst * ga_ref[...]
    g1 = s_ref[0, :, 0:1] * (
        e - jnp.mean(e, -1, keepdims=True) - n1 * jnp.mean(e * n1, -1, keepdims=True)
    )
    gl = g1.astype(BF16)
    gone_ref[0] = gl
    gbr_ref[...] = gl
    da = mm(wo_ref[...], gl, NT)
    for h in range(heads):
        il = il_ref[0, h : h + 1, :]
        piece = da[h * hs : (h + 1) * hs, :] * il
        do_ref[0, h * hs : (h + 1) * hs, :] = piece.astype(BF16)
        att = att_ref[0, h * hs : (h + 1) * hs, :].astype(F32)
        de_ref[0, h : h + 1, :] = jnp.sum(piece * att, axis=0, keepdims=True)

    @pl.when(pl.program_id(0) == 0)
    def _():
        sums_ref[...] = jnp.zeros_like(sums_ref)
        bsum_ref[...] = jnp.zeros_like(bsum_ref)

    sums_ref[0:1, :] += jnp.sum(gl.astype(F32), 0, keepdims=True)
    sums_ref[1:2, :] += jnp.sum(gfirst * n1, 0, keepdims=True)
    sums_ref[2:3, :] += jnp.sum(gfirst, 0, keepdims=True)
    bsum_ref[0:1, :] += jnp.sum(gp.astype(F32), 0, keepdims=True)


def ffn_back(g, slope, wu, wd, wo, n1, s1, ga, att, il, heads, hs):
    T, D = g.shape
    FF = wu.shape[1]
    R, L = n1.shape[:2]
    return pl.pallas_call(
        functools.partial(ffn_back_kernel, heads=heads, hs=hs),
        grid=(R,),
        in_specs=[
            rows_of(L, D), rows_of(L, FF), whole((D, FF)), whole((FF, D)), whole((D, D)),
            lead((L, D)), lead((L, 128)), whole((1, D)), lead((D, L)), lead((heads, L)),
        ],
        out_specs=[
            rows_of(L, FF), lead((L, D)), rows_of(L, D), lead((D, L)), lead((heads, L)),
            pl.BlockSpec((8, D), lambda i: (0, 0)), pl.BlockSpec((8, FF), lambda i: (0, 0)),
        ],
        out_shape=[
            shape_of((T, FF), BF16), shape_of((R, L, D), BF16), shape_of((T, D), BF16),
            shape_of((R, D, L), BF16), shape_of((R, heads, L), F32), shape_of((8, D), F32),
            shape_of((8, FF), F32),
        ],
        compiler_params=params(),
        cost_estimate=cost(4 * T * D * FF * 1.5, 4 * T * FF + 4 * D * FF),
        name="ffn_back",
    )(g, slope, wu, wd, wo, n1, s1, ga, att, il)


def up_grad_kernel(x_ref, g_ref, o_ref):
    o_ref[...] = mm(x_ref[...], g_ref[...], TN).astype(BF16)


def up_grad(x, g, tile):
    T, D = x.shape
    FF = g.shape[1]
    return pl.pallas_call(
        up_grad_kernel,
        grid=(FF // tile,),
        in_specs=[whole((T, D)), pl.BlockSpec((T, tile), lambda i: (0, i))],
        out_specs=pl.BlockSpec((D, tile), lambda i: (0, i)),
        out_shape=shape_of((D, FF), BF16),
        compiler_params=params(),
        cost_estimate=cost(2 * T * D * FF * 1.3, 2 * T * FF + 2 * D * FF),
        name="up_grad",
    )(x, g)


def out_grad_kernel(att_ref, g_ref, o_ref):
    total = mm(att_ref[0], g_ref[0])
    for r in range(1, att_ref.shape[0]):
        total = total + mm(att_ref[r], g_ref[r])
    o_ref[...] = total.astype(BF16)


def out_grad(att, g):
    R, D, L = att.shape
    tile = D // 3
    return pl.pallas_call(
        out_grad_kernel,
        grid=(3,),
        in_specs=[pl.BlockSpec((R, tile, L), lambda i: (0, i, 0)), whole((R, L, D))],
        out_specs=rows_of(tile, D),
        out_shape=shape_of((D, D), BF16),
        compiler_params=params(),
        cost_estimate=cost(2 * R * L * D * D * 1.3, 4 * R * L * D),
        name="out_grad",
    )(att, g)


def attend_back_kernel(
    qkv_ref, p_ref, do_ref, de_ref, gone_ref, wt_ref, g_ref, gin_ref, sums_ref, *, heads, hs, scale
):
    D = heads * hs
    for h in range(heads):
        q = qkv_ref[0, h * hs : (h + 1) * hs, :]
        k = qkv_ref[0, D + h * hs : D + (h + 1) * hs, :]
        v = qkv_ref[0, 2 * D + h * hs : 2 * D + (h + 1) * hs, :]
        do = do_ref[0, h * hs : (h + 1) * hs, :]
        p = p_ref[0, h]
        dp = mm(v, do, TN)
        ds = (p.astype(F32) * (dp - de_ref[0, h : h + 1, :])).astype(BF16)
        g_ref[0, h * hs : (h + 1) * hs, :] = (mm(k, ds) * scale).astype(BF16)
        g_ref[0, D + h * hs : D + (h + 1) * hs, :] = mm(q, ds, NT).astype(BF16)
        g_ref[0, 2 * D + h * hs : 2 * D + (h + 1) * hs, :] = mm(do, p, NT).astype(BF16)
    g = g_ref[0]
    gin_ref[0] = (mm(g, wt_ref[...], TN) + gone_ref[0].astype(F32)).astype(BF16)

    @pl.when(pl.program_id(0) == 0)
    def _():
        sums_ref[...] = jnp.zeros_like(sums_ref)

    ones = jnp.ones((8, g.shape[1]), BF16)
    sums_ref[...] += mm(ones, g, NT)


def attend_back(qkv, p, do, de, gone, wt, heads, hs, scale):
    R, D3, L = qkv.shape
    D = D3 // 3
    return pl.pallas_call(
        functools.partial(attend_back_kernel, heads=heads, hs=hs, scale=scale),
        grid=(R,),
        in_specs=[
            lead((D3, L)), lead((heads, L, L)), lead((D, L)), lead((heads, L)), lead((L, D)),
            whole((D3, D)),
        ],
        out_specs=[lead((D3, L)), lead((L, D)), pl.BlockSpec((8, D3), lambda i: (0, 0))],
        out_shape=[
            shape_of((R, D3, L), BF16), shape_of((R, L, D), BF16), shape_of((8, D3), F32),
        ],
        compiler_params=params(),
        cost_estimate=cost(R * (6 * L * D * D + 4 * 8 * heads * L * L * hs), R * 2 * heads * L * L),
        name="attend_back",
    )(qkv, p, do, de, gone, wt)


def qkv_grad_kernel(x_ref, g_ref, o_ref):
    total = mm(x_ref[0], g_ref[0], (((0,), (1,)), ((), ())))
    for r in range(1, x_ref.shape[0]):
        total = total + mm(x_ref[r], g_ref[r], (((0,), (1,)), ((), ())))
    o_ref[...] = total.astype(BF16)


def qkv_grad(x, g):
    R, L, D = x.shape
    D3 = g.shape[1]
    tile = 768
    return pl.pallas_call(
        qkv_grad_kernel,
        grid=(D3 // tile,),
        in_specs=[whole((R, L, D)), pl.BlockSpec((R, tile, L), lambda i: (0, i, 0))],
        out_specs=pl.BlockSpec((D, tile), lambda i: (0, i)),
        out_shape=shape_of((D, D3), BF16),
        compiler_params=params(),
        cost_estimate=cost(2 * R * L * D * D3 * 1.3, 2 * R * L * (D + D3)),
        name="qkv_grad",
    )(x, g)


def bits_of(size):
    return [b for b in range(size.bit_length() - 1)]


def flip(x, axis, size, bit):
    return lax.ppermute(x, axis, [(i, i ^ (1 << bit)) for i in range(size)])


def my_bit(axis, bit):
    return (lax.axis_index(axis) >> bit) & 1


def pick(x, index, axis):
    return lax.dynamic_index_in_dim(x, index, axis, keepdims=False)


def block_order(size):
    order = [0]
    for bit in reversed(bits_of(size)):
        order = order + [o ^ (1 << bit) for o in order]
    return order


def to_rows(x, axis, size):
    held = x
    for bit in reversed(bits_of(size)):
        mine = my_bit(axis, bit)
        split = held.reshape((2, held.shape[0] // 2) + held.shape[1:])
        other = flip(pick(split, 1 - mine, 0), axis, size, bit)
        held = jnp.concatenate([pick(split, mine, 0), other], 2)
    return held[0]


def to_blocks(x, axis, size):
    held = x[None]
    for bit in bits_of(size):
        mine = my_bit(axis, bit)
        half = held.shape[2] // 2
        own = held[:, :, :half]
        other = flip(held[:, :, half:], axis, size, bit)
        low = jnp.where(mine == 0, own, other)
        high = jnp.where(mine == 0, other, own)
        held = jnp.concatenate([low, high], 0)
    return held


def reduce_rows(x, sizes, order):
    (dp, seq) = sizes
    names = [("dp", b) for b in reversed(bits_of(dp))] + [("seq", b) for b in reversed(bits_of(seq))]
    held = x.reshape((2,) * len(names) + (x.shape[0] // (dp * seq),) + x.shape[1:])
    left = list(names)
    for name, bit in order:
        axis = left.index((name, bit))
        mine = my_bit(name, bit)
        size = dp if name == "dp" else seq
        other = flip(pick(held, 1 - mine, axis), name, size, bit)
        held = (pick(held, mine, axis).astype(F32) + other.astype(F32)).astype(BF16)
        left.pop(axis)
    return held


def shards(
    dp, seq, hidden_in, segment_ids, cluster_perm, w_qkv, bias_qv, w_out, bias_out, gain_attn,
    shift_attn, w_up, bias_up, w_down, bias_down, gain_ffn, shift_ffn, grad_out,
):
    row_count, block_len, D = hidden_in.shape
    heads = cluster_perm.shape[1]
    hs = D // heads
    L = segment_ids.shape[1]
    FF = w_up.shape[1]
    R = row_count // seq
    T = R * L
    scale = 1.0 / math.sqrt(hs)
    me = lax.axis_index("seq")

    x = to_rows(hidden_in.reshape(seq, R, block_len, D), "seq", seq)
    gout = to_rows(grad_out.reshape(seq, R, block_len, D), "seq", seq)

    perm = lax.dynamic_slice_in_dim(cluster_perm, me * R, R, 0)
    segs = lax.dynamic_slice_in_dim(segment_ids, me * R, R, 0)
    member = (jnp.arange(L, dtype=jnp.int32) // CL).astype(BF16)
    hi = (perm[:, :, None, :] // CL == jnp.arange(L // CL)[:, None]).astype(BF16) * member
    lo = (perm[:, :, None, :] % CL == jnp.arange(CL)[:, None]).astype(BF16)
    cluster = jnp.einsum("rhaj,rhbj->rhab", hi, lo, preferred_element_type=F32)
    code = cluster.reshape(R, heads, L).astype(jnp.int32) * DOCS + segs[:, None, :]
    code = code.reshape(R, heads, seq, block_len)
    code = jnp.concatenate([pick(code, me ^ o, 2) for o in block_order(seq)], -1)

    col = jnp.concatenate([jnp.full((D,), scale, F32), jnp.ones((2 * D,), F32)])
    wt = w_qkv.T
    wts = (wt.astype(F32) * col[:, None]).astype(BF16)
    bias_full = jnp.concatenate([bias_qv[:D] * scale, jnp.zeros((D,), F32), bias_qv[D:]])
    row = lambda v: v.reshape(1, -1)

    qkv, p, il, att, first, n1, s1 = attend(
        x, code, wts, bias_full.reshape(-1, 1), w_out, row(bias_out), row(gain_attn),
        row(shift_attn), heads, hs,
    )
    first = first.reshape(T, D)
    out, gffn, act, slope, sums_ffn = ffn(
        first, gout.reshape(T, D), w_up, row(bias_up), w_down, row(bias_down), row(gain_ffn),
        row(shift_ffn), L,
    )
    out_hidden = to_blocks(out.reshape(R, L, D), "seq", seq).reshape(row_count, block_len, D)
    d_down = down_grad(act, gffn, 512)
    gpre, gone, gbr, do, de, sums_attn, sums_up = ffn_back(
        gffn, slope, w_up, w_down, w_out, n1, s1, row(gain_attn), att, il, heads, hs
    )
    d_up = up_grad(first, gpre, 512)
    d_out = out_grad(att, gbr.reshape(R, L, D))
    g, gin, sums_qkv = attend_back(qkv, p, do, de, gone, wt, heads, hs, scale)
    grad_in = to_blocks(gin, "seq", seq).reshape(row_count, block_len, D)
    d_qkv = qkv_grad(x, g)

    n = dp * seq
    small = [
        sums_qkv[0, :D], sums_qkv[0, 2 * D :], sums_attn[0], sums_attn[1], sums_attn[2],
        sums_up[0], sums_ffn[0], sums_ffn[1], sums_ffn[2],
    ]
    small = [jnp.concatenate(small[:2])] + small[2:]
    per = [v.size // n for v in small]
    packed = jnp.concatenate([v.reshape(n, -1) for v in small], -1)
    pad = 8 * D - packed.shape[1] if packed.shape[1] <= 8 * D else 0
    packed = jnp.pad(packed, ((0, 0), (0, pad))).reshape(n * 8, D).astype(BF16)

    bits = lambda name, size: [(name, b) for b in bits_of(size)]
    order = [("seq", 0)] + bits("dp", dp) + bits("seq", seq)[1:]
    reduce = lambda v: reduce_rows(v, (dp, seq), order)
    r_down = reduce(d_down).astype(F32)
    r_up = reduce(d_up).astype(F32)
    r_out = reduce(jnp.concatenate([d_out.reshape(n, -1, D), packed.reshape(n, 8, D)], 1).reshape(-1, D))
    r_out = r_out.astype(F32)
    r_qkv = reduce(d_qkv).astype(F32)
    vec = r_out[D // n :].reshape(-1)
    cuts, at = [], 0
    for width in per:
        cuts.append(vec[at : at + width])
        at += width
    b_qv, b_out, g_attn, s_attn, b_up, b_down, g_ffn, s_ffn = cuts
    return (
        out_hidden, grad_in, r_qkv, b_qv, r_out[: D // n], b_out, g_attn, s_attn, r_up, b_up,
        r_down, b_down, g_ffn, s_ffn,
    )


def solution(mesh):
    tok = P("dp", "seq", None)
    both = ("dp", "seq")
    return jax.shard_map(
        functools.partial(shards, mesh.shape["dp"], mesh.shape["seq"]),
        mesh=mesh,
        in_specs=(tok, P("dp", None), P("dp", None, None)) + (P(),) * 12 + (tok,),
        out_specs=(
            tok, tok, P(both, None), P(both), P(both, None), P(both), P(both), P(both),
            P(both, None), P(both), P(both, None), P(both), P(both), P(both),
        ),
        check_vma=False,
    )
```

time: 1790 us -> 479 us (0.27)
  local copies, waits for them, and re-layouts: 704 us -> 43.7 us
  waiting for transfers between devices: 544 us -> 142 us
  matrix products: 391 us -> 2 us
  Pallas kernels: 0 us -> 221 us
  blocking collectives: 41.1 us -> 0 us
  other arithmetic: 79.4 us -> 39.7 us
  starting transfers between devices: 0.25 us -> 24.9 us
    reduce_scatter x4 -> x0, waiting for transfers between devices: 420 us -> none  [the longest x1 142 us: shards(): lax.psum_scatter(down_grad, ('dp', 'seq'), scatter_dimension=0, tiled=True)]
    unnamed x74 -> x41, local copies, waits for them, and re-layouts: 399 us -> 7.85 us
    dot_general x124 -> x1, matrix products: 391 us -> 2 us  [shards(): cluster = jnp.einsum('rhaj,rhbj->rhab', hi, lo, preferred_element_type=F32)]
    pallas_call x0 -> x8, Pallas kernels: none -> 221 us  [the longest x1 52.4 us: attend_back(): pl.pallas_call(functools.partial(attend_back_kernel, heads=heads, hs=hs,...]
    ppermute x0 -> x28, waiting for transfers between devices: none -> 142 us  [flip(): return lax.ppermute(x, axis, [(i, i ^ 1 << bit) for i in range(size)])]
    unnamed x7 -> x0, waiting for transfers between devices: 125 us -> none
    dynamic_update_slice x32 -> x0, local copies, waits for them, and re-layouts: 83.9 us -> none  [shards(): lax.map(lambda item: query_back(item), back_items)]
    eq x96 -> x0, local copies, waits for them, and re-layouts: 58 us -> none  [the longest x64 46.9 us: allowed_mask(): same_cluster = own_cl[:, :, None] == cluster_row[:, None, :]]
  transfers between devices with their start and end apart: 6 -> 28, of which waited for: 5 -> 12; matrix products, arithmetic and copies ran while one was open for 28% -> 15% of each run, Pallas kernels for 0% -> 18%
where the time goes in v1:
time: 479 us; the launch traced here: 474 us
  Pallas kernels  221 us (46%)
  waiting for transfers between devices  142 us (30%)
  local copies, waits for them, and re-layouts  43.7 us (9%)
  other arithmetic  39.7 us (8%)
  starting transfers between devices  24.9 us (5%)
    ppermute x28, waiting for transfers between devices, flip(): return lax.ppermute(x, axis, [(i, i ^ 1 << bit) for i in range(size)])  142 us
    pallas_call x1, Pallas kernels, attend_back(): pl.pallas_call(functools.partial(attend_back_kernel, heads=heads, hs=hs,...  52.4 us
    pallas_call x1, Pallas kernels, attend(): pl.pallas_call(functools.partial(attend_kernel, heads=heads, hs=hs), grid...  44 us
    pallas_call x1, Pallas kernels, ffn_back(): pl.pallas_call(functools.partial(ffn_back_kernel, heads=heads, hs=hs), gr...  40.9 us
    pallas_call x1, Pallas kernels, ffn(): pl.pallas_call(ffn_kernel, grid=(T // tile,), in_specs=[rows_of(tile, D),...  35.3 us
    ppermute x28, starting transfers between devices, flip(): return lax.ppermute(x, axis, [(i, i ^ 1 << bit) for i in range(size)])  24.9 us
    pallas_call x1, Pallas kernels, up_grad(): pl.pallas_call(up_grad_kernel, grid=(FF // tile,), in_specs=[whole((T, D)...  15 us
    pallas_call x1, Pallas kernels, down_grad(): pl.pallas_call(down_grad_kernel, grid=(FF // tile,), in_specs=[pl.BlockSp...  14.6 us
  transfers between devices with their start and end apart: 28, of which 12 were waited for; matrix products, arithmetic and copies ran while one was open for 15% of the time, Pallas kernels for 18%

profile of v1, /device:TPU:0, one launch (start us, length us, event | category | flops | bytes accessed | tf_op | source)
XLA Modules:
  0.0 474.2 jit_solution(16297583627042397275)
XLA Ops:
  0.7 3.5 dynamic-slice_bitcast_fusion.2
  4.1 2.9 collective-permute-start
  7.1 1.9 dynamic-slice_bitcast_fusion
  9.4 2.0 fusion.19
  12.8 29.8 %collective-permute-done = bf16[2,4,128,768]{3,2,1,0:T(8,128)(2,1)} collective-permute-done((bf16[2,4,128,768]{3,2,1,0:T(8,128)(2,1)}, bf16[2,4,128,768]{3,2,1,0:T(8,128)(2,1)}, u32[]{:S(2)}, u32[]{:S(2)}) %collective-permute-start) | collective-permute-done | bytes 1572896 | tf_op jit(solution)/shard_map/ppermute | solution.py:357
  42.6 3.2 fusion.13
  48.5 5.0 %copy.50 = bf16[768,2304]{0,1:T(8,128)(2,1)S(1)} copy(bf16[768,2304]{1,0:T(8,128)(2,1)} %param.19) | data formatting | bytes 7077888 | tf_op args[3]
  62.1 2.4 multiply_convert_fusion.wt_ref
  64.5 11.0 %collective-permute-done.2 = bf16[2,4,128,768]{3,2,1,0:T(8,128)(2,1)} collective-permute-done((bf16[2,4,128,768]{3,2,1,0:T(8,128)(2,1)}, bf16[2,4,128,768]{3,2,1,0:T(8,128)(2,1)}, u32[]{:S(2)}, u32[]{:S(2)}) %collective-permute-start.2) | collective-permute-done | bytes 1572896 | tf_op jit(solution)/shard_map/ppermute | solution.py:357
  75.5 2.9 fusion.11
  78.4 3.3 maximum_bitcast_fusion.x_ref
  81.6 44.0 %attend.1 = (bf16[4,2304,512]{2,1,0:T(8,128)(2,1)}, bf16[4,12,512,512]{3,2,1,0:T(8,128)(2,1)}, f32[4,12,512]{2,1,0:T(8,128)}, bf16[4,768,512]{2,1,0:T(8,128)(2,1...) custom-call(bf16[4,512,768]{2,1,0:T(8,128)(2,1)} %maximum_bitcast_fusion.x_ref, ...), custom_call_target="tpu_custom_call" | custom-call | flops 22548578304 | bytes 25165824 | tf_op jit(solution)/shard_map/attend/pallas_call | solution.py:86
  125.6 3.2 pad_maximum_fusion
  128.9 35.3 %ffn.1 = (bf16[2048,768]{1,0:T(8,128)(2,1)}, bf16[2048,768]{1,0:T(8,128)(2,1)}, bf16[2048,3072]{1,0:T(8,128)(2,1)}, bf16[2048,3072]{1,0:T(8,128)(2,1)}, f32[8,768]{1,0:T(8,128)}) custom-call(bf16[2048,768]{1,0:T(8,128)(2,1)} %bitcast.169, bf16[2048,768]{1,0:T(8,128)(2,1)} %bitcast.157, bf16[768,3072]{1,0:T(8,128)(2,1)} %wu_ref.3, f32[1,3072]{1,0:T(1,128)} %bitcast.168, ...), custom_call_target="tpu_custom_call" | custom-call | flops 25125558272 | bytes 34603008 | tf_op jit(solution)/shard_map/ffn/pallas_call | solution.py:141
  164.1 40.9 %ffn_back.1 = (bf16[2048,3072]{1,0:T(8,128)(2,1)}, bf16[4,512,768]{2,1,0:T(8,128)(2,1)}, bf16[2048,768]{1,0:T(8,128)(2,1)}, bf16[4,768,512]{2,1,0:T(8,128)(2,1)}...) custom-call(bf16[2048,768]{1,0:T(8,128)(2,1)} %get-tuple-element.40.g_ref, ...), custom_call_target="tpu_custom_call" | custom-call | flops 28991029248 | bytes 34603008 | tf_op jit(solution)/shard_map/ffn_back/pallas_call | solution.py:220
  205.0 52.4 %attend_back.1 = (bf16[4,2304,512]{2,1,0:T(8,128)(2,1)}, bf16[4,512,768]{2,1,0:T(8,128)(2,1)}, f32[8,2304]{1,0:T(8,128)}) custom-call(bf16[4,2304,512]{2,1,0:T(8,128)(2,1)} %get-tuple-element.38.qkv_ref, bf16[4,12,512,512]{3,2,1,0:T(8,128)(2,1)} %get-tuple-element.39.p_ref, bf16[4,768,512]{2,1,0:T(8,128)(2,1)} %get-tuple-element.46.do_ref, ...), custom_call_target="tpu_custom_call" | custom-call | flops 33017561088 | bytes 25165824 | tf_op jit(solution)/shard_map/attend_back/pallas_call | solution.py:312
  260.5 6.3 %out_grad.1 = bf16[768,768]{1,0:T(8,128)(2,1)} custom-call(bf16[4,768,512]{2,1,0:T(8,128)(2,1)} %get-tuple-element.44.att_ref, bf16[4,512,768]{2,1,0:T(8,128)(2,1)} %bitcast.171), custom_call_target="tpu_custom_call" | custom-call | flops 3140694784 | bytes 6291456 | tf_op jit(solution)/shard_map/out_grad/pallas_call | solution.py:271
  268.8 14.6 %down_grad.1 = bf16[3072,768]{1,0:T(8,128)(2,1)} custom-call(bf16[2048,3072]{1,0:T(8,128)(2,1)} %get-tuple-element.57.act_ref, bf16[2048,768]{1,0:T(8,128)(2,1)} %get-tuple-element.40.g_ref), custom_call_target="tpu_custom_call" | custom-call | flops 12562779136 | bytes 17301504 | tf_op jit(solution)/shard_map/down_grad/pallas_call | solution.py:169
  283.4 4.1 constant_dynamic-slice_fusion.1
  287.5 1.6 copy.87
  290.5 1.9 collective-permute-start.14
  292.4 15.0 %up_grad.1 = bf16[768,3072]{1,0:T(8,128)(2,1)} custom-call(bf16[2048,768]{1,0:T(8,128)(2,1)} %bitcast.170, bf16[2048,3072]{1,0:T(8,128)(2,1)} %get-tuple-element.56.g_ref), custom_call_target="tpu_custom_call" | custom-call | flops 12562779136 | bytes 17301504 | tf_op jit(solution)/shard_map/up_grad/pallas_call | solution.py:249
  307.6 1.6 collective-permute-start.15
  309.2 12.0 %qkv_grad.1 = bf16[768,2304]{1,0:T(8,128)(2,1)} custom-call(bf16[4,512,768]{2,1,0:T(8,128)(2,1)} %maximum_bitcast_fusion.x_ref, bf16[4,2304,512]{2,1,0:T(8,128)(2,1)} %get-tuple-element.50.g_ref), custom_call_target="tpu_custom_call" | custom-call | flops 9422084096 | bytes 12582912 | tf_op jit(solution)/shard_map/qkv_grad/pallas_call | solution.py:340
  321.2 2.8 slice.130
  324.1 2.6 collective-permute-start.16
  329.8 2.5 collective-permute-done.16
  332.3 1.5 collective-permute-start.17
  334.2 1.6 copy.88
  340.6 2.1 broadcast_select_fusion.1
  344.1 2.1 fusion.4
  346.9 1.6 broadcast_select_fusion.3
  350.2 2.4 fusion.2
  352.7 1.5 collective-permute-start.24
  354.2 14.6 %collective-permute-done.9 = bf16[2,2,2,24,2304]{4,3,2,0,1:T(8,128)(2,1)S(1)} collective-permute-done((bf16[2,2,2,24,2304]{4,3,2,0,1:T(8,128)(2,1)S(1)}, bf16[2,2,2,24,2304]{4,3,2,0,1:T(8,128)(2,1)S(1)}, u32[]{:S(2)}, u32[]{:S(2)}) %collective-permute-start.9) | collective-permute-done | bytes 884768 | tf_op jit(solution)/shard_map/ppermute | solution.py:357
  369.1 2.6 fusion.3
  372.5 8.1 %collective-permute-done.10 = bf16[2,2,24,2304]{3,2,1,0:T(8,128)(2,1)S(1)} collective-permute-done((bf16[2,2,24,2304]{3,2,1,0:T(8,128)(2,1)S(1)}, bf16[2,2,24,2304]{3,2,1,0:T(8,128)(2,1)S(1)}, u32[]{:S(2)}, u32[]{:S(2)}) %collective-permute-start.10) | collective-permute-done | bytes 442400 | tf_op jit(solution)/shard_map/ppermute | solution.py:357
  380.7 1.5 collective-permute-start.11
  382.4 30.9 %collective-permute-done.5 = bf16[2,4,128,768]{3,2,1,0:T(8,128)(2,1)S(1)} collective-permute-done((bf16[2,4,128,768]{3,2,1,0:T(8,128)(2,1)S(1)}, bf16[2,4,128,768]{3,2,1,0:T(8,128)(2,1)S(1)}, u32[]{:S(2)}, u32[]{:S(2)}) %collective-permute-start.5) | collective-permute-done | bytes 1572896 | tf_op jit(solution)/shard_map/ppermute | solution.py:357
  413.8 1.9 pad_maximum_fusion.2
  415.7 1.9 pad_maximum_fusion.1
  419.4 1.9 collective-permute-start.20
  423.3 11.8 %collective-permute-done.25 = bf16[2,2,96,768]{3,2,1,0:T(8,128)(2,1)S(1)} collective-permute-done((bf16[2,2,96,768]{3,2,1,0:T(8,128)(2,1)S(1)}, bf16[2,2,96,768]{3,2,1,0:T(8,128)(2,1)S(1)}, u32[]{:S(2)}, u32[]{:S(2)}) %collective-permute-start.25) | collective-permute-done | bytes 589856 | tf_op jit(solution)/shard_map/ppermute | solution.py:357
  436.4 16.0 %collective-permute-done.20 = bf16[2,2,24,3072]{3,2,1,0:T(8,128)(2,1)S(1)} collective-permute-done((bf16[2,2,24,3072]{3,2,1,0:T(8,128)(2,1)S(1)}, bf16[2,2,24,3072]{3,2,1,0:T(8,128)(2,1)S(1)}, u32[]{:S(2)}, u32[]{:S(2)}) %collective-permute-start.20) | collective-permute-done | bytes 589856 | tf_op jit(solution)/shard_map/ppermute | solution.py:357
  453.5 1.6 collective-permute-start.27
  455.1 12.2 %collective-permute-done.21 = bf16[2,24,3072]{2,1,0:T(8,128)(2,1)S(1)} collective-permute-done((bf16[2,24,3072]{2,1,0:T(8,128)(2,1)S(1)}, bf16[2,24,3072]{2,1,0:T(8,128)(2,1)S(1)}, u32[]{:S(2)}, u32[]{:S(2)}) %collective-permute-start.21) | collective-permute-done | bytes 294944 | tf_op jit(solution)/shard_map/ppermute | solution.py:357
  467.4 1.6 collective-permute-start.22
  469.7 3.5 collective-permute-done.22
  (169 shorter events, 40.9 us)
Async XLA Ops:
  0.6 8.7 %copy-start = (s32[16,512]{1,0:T(8,128)S(1)}, s32[16,512]{1,0:T(8,128)}, u32[]{:S(2)}) copy-start(s32[16,512]{1,0:T(8,128)} %param.17) | copy-start | bytes 98308
  0.7 6.4 %copy-start.10 = (bf16[16,128,768]{2,1,0:T(8,128)(2,1)S(1)}, bf16[16,128,768]{2,1,0:T(8,128)(2,1)}, u32[]{:S(2)}) copy-start(bf16[16,128,768]{2,1,0:T(8,128)(2,1)} %param.31) | copy-start | bytes 9437188
  4.1 38.5 %collective-permute-start = (bf16[2,4,128,768]{3,2,1,0:T(8,128)(2,1)}, bf16[2,4,128,768]{3,2,1,0:T(8,128)(2,1)}, u32[]{:S(2)}, u32[]{:S(2)}) collective-permute-start(bf16[2,4,128,768]{3,2,1,0:T(8,128)(2,1)} %get-tuple-element.88), channel_id=1, source_target_pairs={{0,2},{1,3},{2,0},{3,1},{4,6},{5,7},{6,4},{7,5},{8,10},{9,11},{10,... | collective-permute-start | bytes 4718600 | tf_op jit(solution)/shard_map/ppermute | solution.py:357
  7.1 1.9 copy-start.11
  9.0 66.5 %collective-permute-start.2 = (bf16[2,4,128,768]{3,2,1,0:T(8,128)(2,1)}, bf16[2,4,128,768]{3,2,1,0:T(8,128)(2,1)}, u32[]{:S(2)}, u32[]{:S(2)}) collective-permute-start(bf16[2,4,128,768]{3,2,1,0:T(8,128)(2,1)} %get-tuple-element.84), channel_id=1, source_target_pairs={{0,2},{1,3},{2,0},{3,1},{4,6},{5,7},{6,4},{7,5},{8,10},{9,11},{10,... | collective-permute-start | bytes 4718600 | tf_op jit(solution)/shard_map/ppermute | solution.py:357
  42.6 4.5 copy-start.15
  45.9 32.5 %collective-permute-start.1 = (bf16[1,4,256,768]{3,2,1,0:T(8,128)(2,1)}, bf16[1,4,256,768]{3,2,1,0:T(8,128)(2,1)}, u32[]{:S(2)}, u32[]{:S(2)}) collective-permute-start(bf16[1,4,256,768]{3,2,1,0:T(8,128)(2,1)} %get-tuple-element.87), channel_id=1, source_target_pairs={{0,1},{1,0},{2,3},{3,2},{4,5},{5,4},{6,7},{7,6},{8,9},{9,8},{10,11... | collective-permute-start | bytes 4718600 | tf_op jit(solution)/shard_map/ppermute | solution.py:357
  48.5 5.0 %copy-start.16 = (f32[768]{0:T(1024)S(1)}, f32[768]{0:T(1024)}, u32[]{:S(2)}) copy-start(f32[768]{0:T(1024)} %param.23) | copy-start | bytes 9220
  48.5 13.5 %copy-start.14 = (f32[2304]{0:T(1024)S(1)}, f32[2304]{0:T(1024)}, u32[]{:S(2)}) copy-start(f32[2304]{0:T(1024)} %constant.220.clone.1) | copy-start | bytes 27652
  53.6 10.9 %copy-start.2 = (bf16[768,2304]{0,1:T(8,128)(2,1)}, bf16[768,2304]{0,1:T(8,128)(2,1)S(1)}, u32[]{:S(2)}) copy-start(bf16[768,2304]{0,1:T(8,128)(2,1)S(1)} %copy.50) | copy-start | bytes 10616836
  62.1 13.4 %copy-start.6 = (bf16[2,4,128,768]{3,2,1,0:T(8,128)(2,1)S(1)}, bf16[2,4,128,768]{3,2,1,0:T(8,128)(2,1)}, u32[]{:S(2)}) copy-start(bf16[2,4,128,768]{3,2,1,0:T(8,128)(2,1)} %get-tuple-element.85) | copy-start | bytes 4718596
  75.5 2.9 copy-start.5
  78.3 47.3 %collective-permute-start.3 = (bf16[1,4,256,768]{3,2,1,0:T(8,128)(2,1)}, bf16[1,4,256,768]{3,2,1,0:T(8,128)(2,1)}, u32[]{:S(2)}, u32[]{:S(2)}) collective-permute-start(bf16[1,4,256,768]{3,2,1,0:T(8,128)(2,1)} %get-tuple-element.83), channel_id=1, source_target_pairs={{0,1},{1,0},{2,3},{3,2},{4,5},{5,4},{6,7},{7,6},{8,9},{9,8},{10,11... | collective-permute-start | bytes 4718600 | tf_op jit(solution)/shard_map/ppermute | solution.py:357
  205.0 53.5 %copy-start.13 = (f32[8,768]{1,0:T(8,128)S(1)}, f32[8,768]{1,0:T(8,128)}, u32[]{:S(2)}) copy-start(f32[8,768]{1,0:T(8,128)} %get-tuple-element.53) | copy-start | bytes 73732
  205.0 54.9 %copy-start.12 = (f32[8,768]{1,0:T(8,128)S(1)}, f32[8,768]{1,0:T(8,128)}, u32[]{:S(2)}) copy-start(f32[8,768]{1,0:T(8,128)} %get-tuple-element.55) | copy-start | bytes 73732
  268.3 20.8 %collective-permute-start.13 = (bf16[2,2,2,2,32,768]{5,4,3,0,1,2:T(8,128)(2,1)S(1)}, bf16[2,2,2,2,32,768]{5,4,3,0,1,2:T(8,128)(2,1)}, u32[]{:S(2)}, u32[]{:S(2)}) collective-permute-start(bf16[2,2,2,2,32,768]{5,4,3,0,1,2:T(8,128)(2,1)S(1)} %bitcast.167), channel_id=1, source_target_pairs={{0,1},{1,0},{2,3},{3,2},{4,5},{5,4},{6,7},{7,6},{8,9},{9,8},{10,11... | collective-permute-start | bytes 2359304 | tf_op jit(solution)/shard_map/ppermute | solution.py:357
  289.1 60.4 %collective-permute-start.23 = (bf16[2,2,2,2,96,768]{5,4,3,0,1,2:T(8,128)(2,1)}, bf16[2,2,2,2,96,768]{5,4,3,0,1,2:T(8,128)(2,1)}, u32[]{:S(2)}, u32[]{:S(2)}) collective-permute-start(bf16[2,2,2,2,96,768]{5,4,3,0,1,2:T(8,128)(2,1)} %bitcast.145), channel_id=1, source_target_pairs={{0,1},{1,0},{2,3},{3,2},{4,5},{5,4},{6,7},{7,6},{8,9},{9,8},{10,11... | collective-permute-start | bytes 7077896 | tf_op jit(solution)/shard_map/ppermute | solution.py:357
  290.5 16.9 %collective-permute-start.14 = (bf16[2,2,2,32,768]{4,3,2,0,1:T(8,128)(2,1)S(1)}, bf16[2,2,2,32,768]{4,3,2,0,1:T(8,128)(2,1)S(1)}, u32[]{:S(2)}, u32[]{:S(2)}) collective-permute-start(bf16[2,2,2,32,768]{4,3,2,0,1:T(8,128)(2,1)S(1)} %dynamic-slice_bitcast_fusion.10), channel_id=1, source_target_pairs={{0,4},{4,0},{8,12},{12,8},{16,20},{20,16},{24,28},{28,24},{1,5},{5... | collective-permute-start | bytes 1179656 | tf_op jit(solution)/shard_map/ppermute | solution.py:357
  307.6 16.5 %collective-permute-start.15 = (bf16[2,2,32,768]{3,2,1,0:T(8,128)(2,1)S(1)}, bf16[2,2,32,768]{3,2,1,0:T(8,128)(2,1)S(1)}, u32[]{:S(2)}, u32[]{:S(2)}) collective-permute-start(bf16[2,2,32,768]{3,2,1,0:T(8,128)(2,1)S(1)} %dynamic-slice_bitcast_fusion.14), channel_id=1, source_target_pairs={{0,8},{4,12},{8,0},{12,4},{16,24},{20,28},{24,16},{28,20},{1,9},{5... | collective-permute-start | bytes 589832 | tf_op jit(solution)/shard_map/ppermute | solution.py:357
  321.2 5.5 %copy-start.7 = (bf16[768,2304]{1,0:T(8,128)(2,1)S(1)}, bf16[768,2304]{1,0:T(8,128)(2,1)}, u32[]{:S(2)}) copy-start(bf16[768,2304]{1,0:T(8,128)(2,1)} %qkv_grad.1) | copy-start | bytes 10616836
  324.0 16.5 %collective-permute-start.6 = (bf16[1,4,256,768]{3,2,1,0:T(8,128)(2,1)}, bf16[1,4,256,768]{3,2,1,0:T(8,128)(2,1)}, u32[]{:S(2)}, u32[]{:S(2)}) collective-permute-start(bf16[1,4,256,768]{3,2,1,0:T(8,128)(2,1)} %slice.130), channel_id=1, source_target_pairs={{0,1},{1,0},{2,3},{3,2},{4,5},{5,4},{6,7},{7,6},{8,9},{9,8},{10,11... | collective-permute-start | bytes 4718600 | tf_op jit(solution)/shard_map/ppermute | solution.py:357
  324.1 8.2 %collective-permute-start.16 = (bf16[2,32,768]{2,1,0:T(8,128)(2,1)S(1)}, bf16[2,32,768]{2,1,0:T(8,128)(2,1)S(1)}, u32[]{:S(2)}, u32[]{:S(2)}) collective-permute-start(bf16[2,32,768]{2,1,0:T(8,128)(2,1)S(1)} %dynamic-slice_bitcast_fusion.18), channel_id=1, source_target_pairs={{0,16},{4,20},{8,24},{12,28},{16,0},{20,4},{24,8},{28,12},{1,17},{... | collective-permute-start | bytes 294920 | tf_op jit(solution)/shard_map/ppermute | solution.py:357
  326.7 7.1 %slice-start = ((s8[4718592]{0:T(1024)(128)(4,1)}), s8[4194304]{0:T(1024)(128)(4,1)S(1)}, s32[]{:S(2)}) async-start(s8[4718592]{0:T(1024)(128)(4,1)} %bitcast.150), calls=%async_computation | async-start | bytes 8388608
  326.7 7.1 %slice-start.1 = ((s8[4718592]{0:T(1024)(128)(4,1)}), s8[524288]{0:T(1024)(128)(4,1)S(1)}, s32[]{:S(2)}) async-start(s8[4718592]{0:T(1024)(128)(4,1)} %bitcast.150), calls=%async_computation.1 | async-start | bytes 1048576
  329.6 13.8 %collective-permute-start.8 = (bf16[2,2,2,2,24,2304]{5,4,3,0,1,2:T(8,128)(2,1)}, bf16[2,2,2,2,24,2304]{5,4,3,0,1,2:T(8,128)(2,1)}, u32[]{:S(2)}, u32[]{:S(2)}) collective-permute-start(bf16[2,2,2,2,24,2304]{5,4,3,0,1,2:T(8,128)(2,1)} %bitcast.147), channel_id=1, source_target_pairs={{0,1},{1,0},{2,3},{3,2},{4,5},{5,4},{6,7},{7,6},{8,9},{9,8},{10,11... | collective-permute-start | bytes 5308424 | tf_op jit(solution)/shard_map/ppermute | solution.py:357
  332.3 5.9 %collective-permute-start.17 = (bf16[32,768]{1,0:T(8,128)(2,1)S(1)}, bf16[32,768]{1,0:T(8,128)(2,1)S(1)}, u32[]{:S(2)}, u32[]{:S(2)}) collective-permute-start(bf16[32,768]{1,0:T(8,128)(2,1)S(1)} %dynamic-slice_bitcast_fusion.19), channel_id=1, source_target_pairs={{0,2},{1,3},{2,0},{3,1},{4,6},{5,7},{6,4},{7,5},{8,10},{9,11},{10,... | collective-permute-start | bytes 147464 | tf_op jit(solution)/shard_map/ppermute | solution.py:357
  334.2 2.7 copy-start.8
  335.8 33.4 %collective-permute-start.18 = (bf16[2,2,2,2,24,3072]{5,4,3,0,1,2:T(8,128)(2,1)}, bf16[2,2,2,2,24,3072]{5,4,3,0,1,2:T(8,128)(2,1)}, u32[]{:S(2)}, u32[]{:S(2)}) collective-permute-start(bf16[2,2,2,2,24,3072]{5,4,3,0,1,2:T(8,128)(2,1)} %bitcast.146), channel_id=1, source_target_pairs={{0,1},{1,0},{2,3},{3,2},{4,5},{5,4},{6,7},{7,6},{8,9},{9,8},{10,11... | collective-permute-start | bytes 7077896 | tf_op jit(solution)/shard_map/ppermute | solution.py:357
  338.2 8.7 %collective-permute-start.4 = (bf16[1,4,256,768]{3,2,1,0:T(8,128)(2,1)}, bf16[1,4,256,768]{3,2,1,0:T(8,128)(2,1)}, u32[]{:S(2)}, u32[]{:S(2)}) collective-permute-start(bf16[1,4,256,768]{3,2,1,0:T(8,128)(2,1)} %slice.126), channel_id=1, source_target_pairs={{0,1},{1,0},{2,3},{3,2},{4,5},{5,4},{6,7},{7,6},{8,9},{9,8},{10,11... | collective-permute-start | bytes 4718600 | tf_op jit(solution)/shard_map/ppermute | solution.py:357
  342.7 1.5 copy-start.4
  342.8 39.4 %collective-permute-start.7 = (bf16[2,4,128,768]{3,2,1,0:T(8,128)(2,1)S(1)}, bf16[2,4,128,768]{3,2,1,0:T(8,128)(2,1)S(1)}, u32[]{:S(2)}, u32[]{:S(2)}) collective-permute-start(bf16[2,4,128,768]{3,2,1,0:T(8,128)(2,1)S(1)} %pad_maximum_fusion.3), channel_id=1, source_target_pairs={{0,2},{1,3},{2,0},{3,1},{4,6},{5,7},{6,4},{7,5},{8,10},{9,11},{10,... | collective-permute-start | bytes 4718600 | tf_op jit(solution)/shard_map/ppermute | solution.py:357
  344.1 2.8 copy-start.9
  346.3 22.5 %collective-permute-start.9 = (bf16[2,2,2,24,2304]{4,3,2,0,1:T(8,128)(2,1)S(1)}, bf16[2,2,2,24,2304]{4,3,2,0,1:T(8,128)(2,1)S(1)}, u32[]{:S(2)}, u32[]{:S(2)}) collective-permute-start(bf16[2,2,2,24,2304]{4,3,2,0,1:T(8,128)(2,1)S(1)} %dynamic-slice_bitcast_fusion.6), channel_id=1, source_target_pairs={{0,4},{4,0},{8,12},{12,8},{16,20},{20,16},{24,28},{28,24},{1,5},{5... | collective-permute-start | bytes 2654216 | tf_op jit(solution)/shard_map/ppermute | solution.py:357
  348.5 1.7 copy-start.3
  348.7 64.7 %collective-permute-start.5 = (bf16[2,4,128,768]{3,2,1,0:T(8,128)(2,1)S(1)}, bf16[2,4,128,768]{3,2,1,0:T(8,128)(2,1)S(1)}, u32[]{:S(2)}, u32[]{:S(2)}) collective-permute-start(bf16[2,4,128,768]{3,2,1,0:T(8,128)(2,1)S(1)} %pad_maximum_fusion.4), channel_id=1, source_target_pairs={{0,2},{1,3},{2,0},{3,1},{4,6},{5,7},{6,4},{7,5},{8,10},{9,11},{10,... | collective-permute-start | bytes 4718600 | tf_op jit(solution)/shard_map/ppermute | solution.py:357
  352.7 65.7 %collective-permute-start.24 = (bf16[2,2,2,96,768]{4,3,2,0,1:T(8,128)(2,1)S(1)}, bf16[2,2,2,96,768]{4,3,2,0,1:T(8,128)(2,1)S(1)}, u32[]{:S(2)}, u32[]{:S(2)}) collective-permute-start(bf16[2,2,2,96,768]{4,3,2,0,1:T(8,128)(2,1)S(1)} %dynamic-slice_bitcast_fusion.4), channel_id=1, source_target_pairs={{0,4},{4,0},{8,12},{12,8},{16,20},{20,16},{24,28},{28,24},{1,5},{5... | collective-permute-start | bytes 3538952 | tf_op jit(solution)/shard_map/ppermute | solution.py:357
  369.1 11.5 %collective-permute-start.10 = (bf16[2,2,24,2304]{3,2,1,0:T(8,128)(2,1)S(1)}, bf16[2,2,24,2304]{3,2,1,0:T(8,128)(2,1)S(1)}, u32[]{:S(2)}, u32[]{:S(2)}) collective-permute-start(bf16[2,2,24,2304]{3,2,1,0:T(8,128)(2,1)S(1)} %dynamic-slice_bitcast_fusion.9), channel_id=1, source_target_pairs={{0,8},{4,12},{8,0},{12,4},{16,24},{20,28},{24,16},{28,20},{1,9},{5... | collective-permute-start | bytes 1327112 | tf_op jit(solution)/shard_map/ppermute | solution.py:357
  371.8 47.1 %collective-permute-start.19 = (bf16[2,2,2,24,3072]{4,3,2,0,1:T(8,128)(2,1)S(1)}, bf16[2,2,2,24,3072]{4,3,2,0,1:T(8,128)(2,1)S(1)}, u32[]{:S(2)}, u32[]{:S(2)}) collective-permute-start(bf16[2,2,2,24,3072]{4,3,2,0,1:T(8,128)(2,1)S(1)} %dynamic-slice_bitcast_fusion.5), channel_id=1, source_target_pairs={{0,4},{4,0},{8,12},{12,8},{16,20},{20,16},{24,28},{28,24},{1,5},{5... | collective-permute-start | bytes 3538952 | tf_op jit(solution)/shard_map/ppermute | solution.py:357
  380.7 37.0 %collective-permute-start.11 = (bf16[2,24,2304]{2,1,0:T(8,128)(2,1)S(1)}, bf16[2,24,2304]{2,1,0:T(8,128)(2,1)S(1)}, u32[]{:S(2)}, u32[]{:S(2)}) collective-permute-start(bf16[2,24,2304]{2,1,0:T(8,128)(2,1)S(1)} %dynamic-slice_bitcast_fusion.13), channel_id=1, source_target_pairs={{0,16},{4,20},{8,24},{12,28},{16,0},{20,4},{24,8},{28,12},{1,17},{... | collective-permute-start | bytes 663560 | tf_op jit(solution)/shard_map/ppermute | solution.py:357
  417.7 4.8 %collective-permute-start.12 = (bf16[24,2304]{1,0:T(8,128)(2,1)S(1)}, bf16[24,2304]{1,0:T(8,128)(2,1)S(1)}, u32[]{:S(2)}, u32[]{:S(2)}) collective-permute-start(bf16[24,2304]{1,0:T(8,128)(2,1)S(1)} %dynamic-slice_bitcast_fusion.17), channel_id=1, source_target_pairs={{0,2},{1,3},{2,0},{3,1},{4,6},{5,7},{6,4},{7,5},{8,10},{9,11},{10,... | collective-permute-start | bytes 331784 | tf_op jit(solution)/shard_map/ppermute | solution.py:357
  418.7 16.3 %collective-permute-start.25 = (bf16[2,2,96,768]{3,2,1,0:T(8,128)(2,1)S(1)}, bf16[2,2,96,768]{3,2,1,0:T(8,128)(2,1)S(1)}, u32[]{:S(2)}, u32[]{:S(2)}) collective-permute-start(bf16[2,2,96,768]{3,2,1,0:T(8,128)(2,1)S(1)} %dynamic-slice_bitcast_fusion.7), channel_id=1, source_target_pairs={{0,8},{4,12},{8,0},{12,4},{16,24},{20,28},{24,16},{28,20},{1,9},{5... | collective-permute-start | bytes 1769480 | tf_op jit(solution)/shard_map/ppermute | solution.py:357
  419.4 33.0 %collective-permute-start.20 = (bf16[2,2,24,3072]{3,2,1,0:T(8,128)(2,1)S(1)}, bf16[2,2,24,3072]{3,2,1,0:T(8,128)(2,1)S(1)}, u32[]{:S(2)}, u32[]{:S(2)}) collective-permute-start(bf16[2,2,24,3072]{3,2,1,0:T(8,128)(2,1)S(1)} %dynamic-slice_bitcast_fusion.8), channel_id=1, source_target_pairs={{0,8},{4,12},{8,0},{12,4},{16,24},{20,28},{24,16},{28,20},{1,9},{5... | collective-permute-start | bytes 1769480 | tf_op jit(solution)/shard_map/ppermute | solution.py:357
  435.3 18.1 %collective-permute-start.26 = (bf16[2,96,768]{2,1,0:T(8,128)(2,1)S(1)}, bf16[2,96,768]{2,1,0:T(8,128)(2,1)S(1)}, u32[]{:S(2)}, u32[]{:S(2)}) collective-permute-start(bf16[2,96,768]{2,1,0:T(8,128)(2,1)S(1)} %dynamic-slice_bitcast_fusion.11), channel_id=1, source_target_pairs={{0,16},{4,20},{8,24},{12,28},{16,0},{20,4},{24,8},{28,12},{1,17},{... | collective-permute-start | bytes 884744 | tf_op jit(solution)/shard_map/ppermute | solution.py:357
  452.6 21.4 %copy-start.1 = (s32[16,512]{1,0:T(8,128)S(1)}, s32[16,512]{1,0:T(8,128)}, u32[]{:S(2)}) copy-start(s32[16,512]{1,0:T(8,128)} %param.17) | copy-start | bytes 98308
  452.6 14.6 %collective-permute-start.21 = (bf16[2,24,3072]{2,1,0:T(8,128)(2,1)S(1)}, bf16[2,24,3072]{2,1,0:T(8,128)(2,1)S(1)}, u32[]{:S(2)}, u32[]{:S(2)}) collective-permute-start(bf16[2,24,3072]{2,1,0:T(8,128)(2,1)S(1)} %dynamic-slice_bitcast_fusion.12), channel_id=1, source_target_pairs={{0,16},{4,20},{8,24},{12,28},{16,0},{20,4},{24,8},{28,12},{1,17},{... | collective-permute-start | bytes 884744 | tf_op jit(solution)/shard_map/ppermute | solution.py:357
  453.5 15.5 %collective-permute-start.27 = (bf16[96,768]{1,0:T(8,128)(2,1)S(1)}, bf16[96,768]{1,0:T(8,128)(2,1)S(1)}, u32[]{:S(2)}, u32[]{:S(2)}) collective-permute-start(bf16[96,768]{1,0:T(8,128)(2,1)S(1)} %dynamic-slice_bitcast_fusion.15), channel_id=1, source_target_pairs={{0,2},{1,3},{2,0},{3,1},{4,6},{5,7},{6,4},{7,5},{8,10},{9,11},{10,... | collective-permute-start | bytes 442376 | tf_op jit(solution)/shard_map/ppermute | solution.py:357
  467.4 5.8 %collective-permute-start.22 = (bf16[24,3072]{1,0:T(8,128)(2,1)S(1)}, bf16[24,3072]{1,0:T(8,128)(2,1)S(1)}, u32[]{:S(2)}, u32[]{:S(2)}) collective-permute-start(bf16[24,3072]{1,0:T(8,128)(2,1)S(1)} %dynamic-slice_bitcast_fusion.16), channel_id=1, source_target_pairs={{0,2},{1,3},{2,0},{3,1},{4,6},{5,7},{6,4},{7,5},{8,10},{9,11},{10,... | collective-permute-start | bytes 442376 | tf_op jit(solution)/shard_map/ppermute | solution.py:357

commit v2 on v1

v2 whole, which is shorter than its diff:
```python
import functools
import math

import jax
import jax.numpy as jnp
from jax import lax
from jax.experimental import pallas as pl
from jax.experimental.pallas import tpu as pltpu
from jax.sharding import PartitionSpec as P

CL = 128
DOCS = 3
CODES = 16
NORM_EPS = 1e-05
BIG = 2.0**50
F32 = jnp.float32
BF16 = jnp.bfloat16
NN = (((1,), (0,)), ((), ()))
NT = (((1,), (1,)), ((), ()))
TN = (((0,), (0,)), ((), ()))
MIB = 2**20
VMEM = 48 * MIB
ATTEND_VMEM = 40 * MIB
FFN_VMEM = 48 * MIB
BACK_VMEM = 48 * MIB
ATTEND_BACK_VMEM = 40 * MIB
WHOLE = pl.BlockSpec(memory_space=pltpu.VMEM)
TICK = jax.ShapeDtypeStruct((1, 1), jnp.float32)
TICK1 = pl.BlockSpec((1, 1), lambda i: (0, 0))
TICK2 = pl.BlockSpec((1, 1), lambda i, g: (0, 0))
TICK3 = pl.BlockSpec((1, 1), lambda i, g, me: (0, 0))
ANY = pl.BlockSpec(memory_space=pl.ANY)


def mm(a, b, dims=NN):
    return lax.dot_general(a, b, dims, preferred_element_type=F32)


def whole(shape):
    return pl.BlockSpec(shape, lambda i: (0,) * len(shape), pipeline_mode=pl.Buffered(1))


def lead(shape):
    return pl.BlockSpec((1,) + shape, lambda i: (i,) + (0,) * len(shape))


def rows_of(tile, width):
    return pl.BlockSpec((tile, width), lambda i: (i, 0))


def shape_of(shape, dtype):
    return jax.ShapeDtypeStruct(shape, dtype)


def params(limit=VMEM):
    return pltpu.CompilerParams(vmem_limit_bytes=limit)


def cost(flops, nbytes):
    return pl.CostEstimate(flops=int(flops), bytes_accessed=int(nbytes), transcendentals=0)


def part_specs(parts, R, at, block_len, D):
    own = pl.BlockSpec((1, block_len, D), lambda i, g, me: (me[0] * R + at + i, 0, 0))
    specs = [own]
    for bit, (part, base) in enumerate(parts[1:]):
        shape = (1, 1) + part.shape[2:]
        place = lambda bit, base, i, g, me: (me[0] >> (bit + 1), at + i - base, 0, 0)
        specs.append(pl.BlockSpec(shape, functools.partial(place, bit, base)))
    return specs


def arrays_of(parts):
    return [parts[0]] + [part for part, _ in parts[1:]]


def merge(refs):
    return jnp.concatenate([refs[0][0]] + [ref[0, 0] for ref in refs[1:]], 0)


def attend_kernel(me_ref, *refs, nparts, heads, hs, group, scale, nio):
    parts, (code_ref, wt_ref, bt_ref, wo_ref, vec_ref) = refs[:nparts], refs[nparts : nparts + 5]
    x_ref, qkv_ref, p_ref, il_ref, att_ref, first_ref, n_ref, s_ref, tick_ref = refs[nparts + 5 + nio :]
    tick_ref[...] = jnp.zeros_like(tick_ref)
    D = heads * hs
    L = x_ref.shape[1]
    step = pl.program_id(1)

    @pl.when(step == 0)
    def _():
        x_ref[0] = merge(parts)
        f = mm(wt_ref[...], x_ref[0], NT) + bt_ref[:, 0:1]
        qkv_ref[0, :D, :] = (f[:D].astype(BF16).astype(F32) * scale).astype(BF16)
        qkv_ref[0, D:, :] = f[D:].astype(BF16)

    it = lax.broadcasted_iota(jnp.int32, (CODES, L), 0)
    for i in range(group):
        at = pl.multiple_of((step * group + i) * hs, hs)
        q = qkv_ref[0, pl.ds(at, hs), :]
        k = qkv_ref[0, pl.ds(D + at, hs), :]
        v = qkv_ref[0, pl.ds(2 * D + at, hs), :]
        same = it == code_ref[0, 0, i : i + 1, :]
        qa = jnp.concatenate([q, jnp.where(same, BIG, 0.0).astype(BF16)], 0)
        ka = jnp.concatenate([k, jnp.where(same, 0.0, -BIG).astype(BF16)], 0)
        s = mm(ka, qa, TN)
        e = jnp.exp(s - jnp.max(s, axis=0, keepdims=True))
        il = 1.0 / jnp.sum(e, axis=0, keepdims=True)
        p = e.astype(BF16)
        p_ref[0, i] = p
        il_ref[0, 0, i : i + 1, :] = il
        att_ref[0, pl.ds(at, hs), :] = (mm(v, p) * il).astype(BF16)

    @pl.when(step == heads // group - 1)
    def _():
        v1 = x_ref[0].astype(F32) + mm(att_ref[0], wo_ref[...], TN) + vec_ref[0:1, :]
        c = v1 - jnp.mean(v1, -1, keepdims=True)
        s1 = lax.rsqrt(jnp.mean(c * c, -1, keepdims=True) + NORM_EPS)
        n1 = c * s1
        first_ref[0] = (n1 * vec_ref[1:2, :] + vec_ref[2:3, :]).astype(BF16)
        n_ref[0] = n1.astype(BF16)
        s_ref[0] = jnp.broadcast_to(s1, (L, 128))


def attend(me, parts, at, r, R, code, wt, bt, wo, vec, heads, hs, scale, group, deps, held):
    D = wo.shape[0]
    L = code.shape[-1]
    here = lambda shape: pl.BlockSpec((1,) + shape, lambda i, g, me: (at + i,) + (0,) * len(shape))
    grouped = lambda shape: pl.BlockSpec((1, 1) + shape, lambda i, g, me: (at + i, g, 0, 0))
    shapes = [
        shape_of((R, L, D), BF16),
        shape_of((R, 3 * D, L), BF16), shape_of((R, heads, L, L), BF16),
        shape_of((R, heads // group, group, L), F32), shape_of((R, D, L), BF16),
        shape_of((R, L, D), BF16), shape_of((R, L, D), BF16), shape_of((R, L, 128), F32),
        TICK,
    ]
    nio = len(held) + len(deps)
    np_ = len(parts)
    return pl.pallas_call(
        functools.partial(
            attend_kernel, nparts=np_, heads=heads, hs=hs, group=group, scale=scale, nio=nio
        ),
        grid_spec=pltpu.PrefetchScalarGridSpec(
            num_scalar_prefetch=1,
            grid=(r, heads // group),
            in_specs=part_specs(parts, R, at, parts[0].shape[1], D) + [
                grouped((group, L)), WHOLE, WHOLE, WHOLE, WHOLE,
            ] + [ANY] * nio,
            out_specs=[
                here((L, D)),
                here((3 * D, L)), pl.BlockSpec((1, group, L, L), lambda i, g, me: (at + i, g, 0, 0)),
                grouped((group, L)), here((D, L)), here((L, D)), here((L, D)), here((L, 128)),
                TICK3,
            ],
        ),
        out_shape=shapes,
        input_output_aliases={1 + np_ + 5 + len(deps) + i: i for i in range(len(held))},
        compiler_params=params(ATTEND_VMEM),
        cost_estimate=cost(r * (8 * L * D * D + 4 * 4 * heads * L * L * hs), r * 2 * heads * L * L),
        name="attend",
    )(me, *arrays_of(parts), code, wt, bt, wo, vec, *deps, *held)


def prepare_kernel(me_ref, w_ref, b_ref, perm_ref, seg_ref, *rest, seq):
    wt_ref, bt_ref, code_ref = rest[-3:]
    wt_ref[...] = w_ref[...].T
    bt_ref[...] = b_ref[...].T
    R, heads, L = perm_ref.shape
    group = code_ref.shape[2]
    me = me_ref[0]
    block = L // seq
    high = lax.broadcasted_iota(jnp.int32, (8, L), 0)
    low = lax.broadcasted_iota(jnp.int32, (128, L), 0)
    member = (lax.broadcasted_iota(jnp.int32, (8, L), 1) // CL).astype(F32)
    for r in range(R):
        seg = seg_ref[pl.ds(me * R + r, 1), :]
        for bit in bits_of(seq):
            blocks = [seg[:, i * block : (i + 1) * block] for i in range(seq)]
            turned = jnp.concatenate([blocks[i ^ (1 << bit)] for i in range(seq)], 1)
            seg = jnp.where(((me >> bit) & 1) == 1, turned, seg)
        for h in range(heads):
            place = perm_ref[r, h : h + 1, :] ^ (me * block)
            a = jnp.where((place >> 7) == high, member, 0.0).astype(BF16)
            b = ((place & 127) == low).astype(BF16)
            table = mm(a, b, NT)
            row = jnp.concatenate([table[i : i + 1, :] for i in range(L // 128)], 1)
            code_ref[r, h // group, h % group : h % group + 1, :] = row.astype(jnp.int32) * DOCS + seg


def prepare(me, seq, w, b, perm, segs, group, deps):
    rows, heads, L = perm.shape
    R = rows // seq
    D, D3 = w.shape
    full = lambda shape: pl.BlockSpec(shape, lambda i, me: (0,) * len(shape))
    codes = (R, heads // group, group, L)
    return pl.pallas_call(
        functools.partial(prepare_kernel, seq=seq),
        grid_spec=pltpu.PrefetchScalarGridSpec(
            num_scalar_prefetch=1,
            grid=(1,),
            in_specs=[
                full((D, D3)), full((8, D3)), pl.BlockSpec((R, heads, L), lambda i, me: (me[0], 0, 0)),
                full(segs.shape),
            ] + [ANY] * len(deps),
            out_specs=[full((D3, D)), full((D3, 8)), full(codes)],
        ),
        out_shape=[shape_of((D3, D), BF16), shape_of((D3, 8), F32), shape_of(codes, jnp.int32)],
        compiler_params=params(32 * MIB),
        cost_estimate=cost(4e9, 8e6),
        name="prepare",
    )(me, w, b, perm, segs, *deps)


def join_kernel(*refs):
    refs[-1][...] = jnp.zeros_like(refs[-1])


def join(*after):
    return pl.pallas_call(
        join_kernel,
        in_specs=[ANY] * len(after),
        out_specs=WHOLE,
        out_shape=TICK,
        compiler_params=params(4 * MIB),
        cost_estimate=cost(1, 1),
        name="join",
    )(*after)


def ffn_kernel(me_ref, *refs, nparts, nio):
    parts, (first_ref, wu_ref, bu_ref, wd_ref, vec_ref) = refs[:nparts], refs[nparts : nparts + 5]
    lo_ref, hi_ref, gffn_ref, act_ref, slope_ref, sums_ref, tick_ref = refs[nparts + 5 + nio :]
    tick_ref[...] = jnp.zeros_like(tick_ref)
    first = first_ref[...]
    u = mm(first, wu_ref[...]) + bu_ref[...]
    half = 0.5 * (1.0 + lax.erf(u * 0.7071067811865476))
    act = (u * half).astype(BF16)
    act_ref[...] = act
    slope_ref[...] = (half + u * jnp.exp(-0.5 * u * u) * 0.3989422804014327).astype(BF16)
    y = first.astype(F32) + mm(act, wd_ref[...]) + vec_ref[3:4, :]
    c = y - jnp.mean(y, -1, keepdims=True)
    s2 = lax.rsqrt(jnp.mean(c * c, -1, keepdims=True) + NORM_EPS)
    n2 = c * s2
    out = (n2 * vec_ref[4:5, :] + vec_ref[5:6, :]).astype(BF16)
    half_len = out.shape[0] // 2
    lo_ref[0] = out[:half_len]
    hi_ref[0] = out[half_len:]
    go = merge(parts).astype(F32)
    e = go * vec_ref[4:5, :]
    g2 = s2 * (e - jnp.mean(e, -1, keepdims=True) - n2 * jnp.mean(e * n2, -1, keepdims=True))
    gl = g2.astype(BF16)
    gffn_ref[...] = gl

    @pl.when(pl.program_id(0) == 0)
    def _():
        sums_ref[...] = jnp.zeros_like(sums_ref)

    sums_ref[0:1, :] += jnp.sum(gl.astype(F32), 0, keepdims=True)
    sums_ref[1:2, :] += jnp.sum(go * n2, 0, keepdims=True)
    sums_ref[2:3, :] += jnp.sum(go, 0, keepdims=True)


def ffn(me, first, parts, at, r, R, wu, bu, wd, vec, deps, held):
    T, D = first.shape
    L = T // R
    FF = wu.shape[1]
    here = lambda width: pl.BlockSpec((L, width), lambda i, g, me: (at + i, 0))
    nio = len(held) + len(deps)
    np_ = len(parts)
    half = pl.BlockSpec((1, L // 2, D), lambda i, g, me: (i, 0, 0))
    return pl.pallas_call(
        functools.partial(ffn_kernel, nparts=np_, nio=nio),
        grid_spec=pltpu.PrefetchScalarGridSpec(
            num_scalar_prefetch=1,
            grid=(r, 1),
            in_specs=part_specs(parts, R, at, parts[0].shape[1], D) + [
                here(D), WHOLE, WHOLE, WHOLE, WHOLE,
            ] + [ANY] * nio,
            out_specs=[
                half, half, here(D), here(FF), here(FF),
                pl.BlockSpec((8, D), lambda i, g, me: (0, 0)), TICK3,
            ],
        ),
        out_shape=[
            shape_of((r, L // 2, D), BF16), shape_of((r, L // 2, D), BF16), shape_of((T, D), BF16),
            shape_of((T, FF), BF16), shape_of((T, FF), BF16), shape_of((8, D), F32),
            TICK,
        ],
        input_output_aliases={1 + np_ + 5 + len(deps) + i: 2 + i for i in range(len(held))},
        compiler_params=params(FFN_VMEM),
        cost_estimate=cost(4 * r * L * D * FF * 1.3, 4 * r * L * FF + 4 * D * FF),
        name="ffn",
    )(me, *arrays_of(parts), first, wu, bu, wd, vec, *deps, *held)


def down_grad_kernel(act_ref, g_ref, o_ref):
    o_ref[...] = mm(act_ref[...], g_ref[...], TN).astype(BF16)


def down_grad(act, g, tile):
    T, FF = act.shape
    D = g.shape[1]
    return pl.pallas_call(
        down_grad_kernel,
        grid=(FF // tile,),
        in_specs=[pl.BlockSpec((T, tile), lambda i: (0, i)), whole((T, D))],
        out_specs=rows_of(tile, D),
        out_shape=shape_of((FF, D), BF16),
        compiler_params=params(),
        cost_estimate=cost(2 * T * D * FF * 1.3, 2 * T * FF + 2 * D * FF),
        name="down_grad",
    )(act, g)


def ffn_back_kernel(
    g_ref, slope_ref, wu_ref, wd_ref, wo_ref, n_ref, s_ref, vec_ref, att_ref, il_ref, *rest,
    heads, hs,
):
    gpre_ref, gbr_ref, do_ref, de_ref, sums_ref, bsum_ref, tick_ref = rest[-7:]
    tick_ref[...] = jnp.zeros_like(tick_ref)
    g = g_ref[...]
    gp = (mm(g, wd_ref[...], NT) * slope_ref[...].astype(F32)).astype(BF16)
    gpre_ref[...] = gp
    gfirst = mm(gp, wu_ref[...], NT) + g.astype(F32)
    n1 = n_ref[0].astype(F32)
    e = gfirst * vec_ref[1:2, :]
    g1 = s_ref[0, :, 0:1] * (
        e - jnp.mean(e, -1, keepdims=True) - n1 * jnp.mean(e * n1, -1, keepdims=True)
    )
    gl = g1.astype(BF16)
    gbr_ref[0] = gl
    da = mm(wo_ref[...], gl, NT)
    for h in range(heads):
        il = il_ref[0, h : h + 1, :]
        piece = da[h * hs : (h + 1) * hs, :] * il
        do_ref[0, h * hs : (h + 1) * hs, :] = piece.astype(BF16)
        att = att_ref[0, h * hs : (h + 1) * hs, :].astype(F32)
        de_ref[0, h : h + 1, :] = jnp.sum(piece * att, axis=0, keepdims=True)

    @pl.when(pl.program_id(0) == 0)
    def _():
        sums_ref[...] = jnp.zeros_like(sums_ref)
        bsum_ref[...] = jnp.zeros_like(bsum_ref)

    sums_ref[0:1, :] += jnp.sum(gl.astype(F32), 0, keepdims=True)
    sums_ref[1:2, :] += jnp.sum(gfirst * n1, 0, keepdims=True)
    sums_ref[2:3, :] += jnp.sum(gfirst, 0, keepdims=True)
    bsum_ref[0:1, :] += jnp.sum(gp.astype(F32), 0, keepdims=True)


def ffn_back(at, r, g, slope, wu, wd, wo, n1, s1, vec, att, il, heads, hs, deps, held):
    T, D = g.shape
    FF = wu.shape[1]
    R, L = n1.shape[:2]
    flat = lambda width: pl.BlockSpec((L, width), lambda i: (at + i, 0))
    here = lambda shape: pl.BlockSpec((1,) + shape, lambda i: (at + i,) + (0,) * len(shape))
    extra = list(deps) + list(held)
    return pl.pallas_call(
        functools.partial(ffn_back_kernel, heads=heads, hs=hs),
        grid=(r,),
        in_specs=[
            flat(D), flat(FF), WHOLE, WHOLE, WHOLE, here((L, D)), here((L, 128)), WHOLE,
            here((D, L)), here((heads, L)),
        ] + [ANY] * len(extra),
        out_specs=[
            flat(FF), here((L, D)), here((D, L)), here((heads, L)),
            pl.BlockSpec((8, D), lambda i: (0, 0)), pl.BlockSpec((8, FF), lambda i: (0, 0)),
            TICK1,
        ],
        out_shape=[
            shape_of((T, FF), BF16), shape_of((R, L, D), BF16), shape_of((R, D, L), BF16),
            shape_of((R, heads, L), F32), shape_of((8, D), F32), shape_of((8, FF), F32),
            TICK,
        ],
        input_output_aliases={10 + len(deps) + i: i for i in range(len(held))},
        compiler_params=params(BACK_VMEM),
        cost_estimate=cost(4 * r * L * D * FF * 1.5, 4 * r * L * FF + 4 * D * FF),
        name="ffn_back",
    )(g, slope, wu, wd, wo, n1, s1, vec, att, il, *extra)


def up_grad_kernel(x_ref, g_ref, *rest):
    o_ref, tick_ref = rest[-2:]
    tick_ref[...] = jnp.zeros_like(tick_ref)
    o_ref[...] = mm(x_ref[...], g_ref[...], TN).astype(BF16)


def up_grad(x, g, tile, deps):
    T, D = x.shape
    FF = g.shape[1]
    return pl.pallas_call(
        up_grad_kernel,
        grid=(FF // tile,),
        in_specs=[whole((T, D)), pl.BlockSpec((T, tile), lambda i: (0, i))] + [ANY] * len(deps),
        out_specs=[pl.BlockSpec((D, tile), lambda i: (0, i)), TICK1],
        out_shape=[shape_of((D, FF + D), BF16), TICK],
        compiler_params=params(),
        cost_estimate=cost(2 * T * D * FF * 1.3, 2 * T * FF + 2 * D * FF),
        name="up_grad",
    )(x, g, *deps)


def out_grad_kernel(att_ref, g_ref, *rest):
    o_ref, tick_ref = rest[-2:]
    tick_ref[...] = jnp.zeros_like(tick_ref)
    total = mm(att_ref[0], g_ref[0])
    for r in range(1, att_ref.shape[0]):
        total = total + mm(att_ref[r], g_ref[r])
    o_ref[...] = total.astype(BF16)


def out_grad(att, g, deps, held):
    R, D, L = att.shape
    tile = D // 3
    last = held.shape[1] // D - 1
    return pl.pallas_call(
        out_grad_kernel,
        grid=(3,),
        in_specs=[pl.BlockSpec((R, tile, L), lambda i: (0, i, 0)), whole((R, L, D))]
        + [ANY] * (len(deps) + 1),
        out_specs=[pl.BlockSpec((tile, D), lambda i: (i, last)), TICK1],
        out_shape=[shape_of(held.shape, BF16), TICK],
        input_output_aliases={2 + len(deps): 0},
        compiler_params=params(),
        cost_estimate=cost(2 * R * L * D * D * 1.3, 4 * R * L * D),
        name="out_grad",
    )(att, g, *deps, held)


def attend_back_kernel(
    qkv_ref, p_ref, do_ref, de_ref, gone_ref, wt_ref, *rest, heads, hs, scale, group
):
    g_ref, lo_ref, hi_ref, sums_ref, tick_ref = rest[-5:]
    tick_ref[...] = jnp.zeros_like(tick_ref)
    D = heads * hs
    step = pl.program_id(1)
    for i in range(group):
        at = pl.multiple_of((step * group + i) * hs, hs)
        q = qkv_ref[0, pl.ds(at, hs), :]
        k = qkv_ref[0, pl.ds(D + at, hs), :]
        v = qkv_ref[0, pl.ds(2 * D + at, hs), :]
        do = do_ref[0, pl.ds(at, hs), :]
        p = p_ref[0, i]
        dp = mm(v, do, TN)
        ds = (p.astype(F32) * (dp - de_ref[0, 0, i : i + 1, :])).astype(BF16)
        g_ref[0, pl.ds(at, hs), :] = (mm(k, ds) * scale).astype(BF16)
        g_ref[0, pl.ds(D + at, hs), :] = mm(q, ds, NT).astype(BF16)
        g_ref[0, pl.ds(2 * D + at, hs), :] = mm(do, p, NT).astype(BF16)

    @pl.when(step == heads // group - 1)
    def _():
        g = g_ref[0]
        gin = (mm(g, wt_ref[...], TN) + gone_ref[0].astype(F32)).astype(BF16)
        half_len = gin.shape[0] // 2
        lo_ref[0] = gin[:half_len]
        hi_ref[0] = gin[half_len:]

        @pl.when(pl.program_id(0) == 0)
        def _():
            sums_ref[...] = jnp.zeros_like(sums_ref)

        ones = jnp.ones((8, g.shape[1]), BF16)
        sums_ref[...] += mm(ones, g, NT)


def attend_back(at, r, of, place, qkv, p, do, de, gone, wt, heads, hs, scale, group, deps, held):
    R, D3, L = qkv.shape
    D = D3 // 3
    here = lambda shape: pl.BlockSpec((1,) + shape, lambda i, g: (at + i,) + (0,) * len(shape))
    extra = list(deps) + [v for v in held if v is not None]
    aliases = {}
    for i, v in enumerate(held):
        if v is not None:
            aliases[6 + len(deps) + len(aliases)] = i
    half = pl.BlockSpec((1, L // 2, D), lambda i, g: (place + i, 0, 0))
    return pl.pallas_call(
        functools.partial(attend_back_kernel, heads=heads, hs=hs, scale=scale, group=group),
        grid=(r, heads // group),
        in_specs=[
            here((D3, L)), pl.BlockSpec((1, group, L, L), lambda i, g: (at + i, g, 0, 0)),
            here((D, L)), pl.BlockSpec((1, 1, group, L), lambda i, g: (at + i, g, 0, 0)),
            here((L, D)), WHOLE,
        ] + [ANY] * len(extra),
        out_specs=[
            here((D3, L)), half, half, pl.BlockSpec((8, D3), lambda i, g: (0, 0)),
            TICK2,
        ],
        out_shape=[
            shape_of((R, D3, L), BF16), shape_of((of, L // 2, D), BF16),
            shape_of((of, L // 2, D), BF16), shape_of((8, D3), F32), TICK,
        ],
        input_output_aliases=aliases,
        compiler_params=params(ATTEND_BACK_VMEM),
        cost_estimate=cost(r * (6 * L * D * D + 4 * 8 * heads * L * L * hs), r * 2 * heads * L * L),
        name="attend_back",
    )(qkv, p, do, de, gone, wt, *extra)


def qkv_grad_kernel(x_ref, g_ref, *rest):
    o_refs, tick_ref = rest[-3:-1], rest[-1]
    tick_ref[...] = jnp.zeros_like(tick_ref)
    total = mm(x_ref[0], g_ref[0], (((0,), (1,)), ((), ())))
    for r in range(1, x_ref.shape[0]):
        total = total + mm(x_ref[r], g_ref[r], (((0,), (1,)), ((), ())))
    half = pl.num_programs(0) // 2

    @pl.when(pl.program_id(0) < half)
    def _():
        o_refs[0][...] = total.astype(BF16)

    @pl.when(pl.program_id(0) >= half)
    def _():
        o_refs[1][...] = total.astype(BF16)


def qkv_grad(x, g, deps):
    R, L, D = x.shape
    D3 = g.shape[1]
    tile = 384
    half = D3 // 2 // tile
    return pl.pallas_call(
        qkv_grad_kernel,
        grid=(2 * half,),
        in_specs=[whole((R, L, D)), pl.BlockSpec((R, tile, L), lambda i: (0, i, 0))] + [ANY] * len(deps),
        out_specs=[
            pl.BlockSpec((D, tile), lambda i: (0, jnp.minimum(i, half - 1))),
            pl.BlockSpec((D, tile), lambda i: (0, jnp.maximum(i - half, 0))), TICK1,
        ],
        out_shape=[shape_of((D, D3 // 2), BF16), shape_of((D, D3 // 2), BF16), TICK],
        compiler_params=params(),
        cost_estimate=cost(2 * R * L * D * D3 * 1.3, 2 * R * L * (D + D3)),
        name="qkv_grad",
    )(x, g, *deps)


def bits_of(size):
    return [b for b in range(size.bit_length() - 1)]


def flip(x, axis, size, bit):
    return lax.ppermute(x, axis, [(i, i ^ (1 << bit)) for i in range(size)])


def my_bit(axis, bit):
    return (lax.axis_index(axis) >> bit) & 1


def pick(x, index, axis):
    return lax.dynamic_index_in_dim(x, index, axis, keepdims=False)


def late(x, tick):
    return x if tick is None else x + tick.reshape(()).astype(x.dtype)


class Rows:
    def __init__(self, x, axis, size):
        self.x, self.axis, self.size = x, axis, size
        self.bits = bits_of(size)
        self.R = x.shape[0] // size
        self.came = [[] for _ in self.bits]
        self.sent = []

    def own(self, bit, start, stop):
        cut = self.x.reshape((2,) * len(self.bits) + (self.R,) + self.x.shape[1:])[..., start:stop, :, :]
        held = [cut]
        for done in range(bit):
            mine = my_bit(self.axis, done)
            held = [pick(v, mine, v.ndim - 4) for v in held]
            got, base = self.find(done, start)
            held.append(got[..., start - base : stop - base, :, :])
        return held

    def find(self, bit, start):
        return [(v, base) for v, base in self.came[bit] if base <= start][-1]

    def come(self, bit, start, stop):
        held = self.own(bit, start, stop)
        mine = my_bit(self.axis, bit)
        send = [pick(v, 1 - mine, v.ndim - 4) for v in held]
        send = send[0] if len(send) == 1 else jnp.concatenate(send, -2)
        self.came[bit].append((flip(send, self.axis, self.size, bit), start))
        return send

    def all_high(self, start, stop):
        return [self.come(bit, start, stop) for bit in self.bits[1:]]

    def parts(self, start):
        out = [self.x]
        for bit in self.bits:
            got, base = self.find(bit, start)
            out.append((got.reshape((-1,) + got.shape[-3:]), base))
        return out


class Blocks:
    def __init__(self, axis, size):
        self.axis, self.size, self.chunks = axis, size, []

    def send(self, lo, hi):
        self.chunks.append((lo, flip(hi, self.axis, self.size, bits_of(self.size)[-1])))

    def result(self, tick=None):
        bits = bits_of(self.size)
        axis, size = self.axis, self.size
        join = lambda vs: jnp.concatenate(vs, 0) if len(vs) > 1 else vs[0]
        pieces = {0: join([lo for lo, _ in self.chunks]), 1 << bits[-1]: late(join([hi for _, hi in self.chunks]), tick)}
        for bit in reversed(bits[:-1]):
            names = list(pieces)
            half = pieces[0].shape[1] // 2
            came = flip(jnp.stack([pieces[name][:, half:] for name in names], 0), axis, size, bit)
            for i, name in enumerate(names):
                pieces[name | (1 << bit)] = came[i]
                pieces[name] = pieces[name][:, :half]
        R, B, D = pieces[0].shape
        me = lax.axis_index(axis)
        out = jnp.zeros((size * R, B, D), BF16)
        for name, piece in pieces.items():
            out = lax.dynamic_update_slice_in_dim(out, piece, (me ^ name) * R, 0)
        return out


class Sum:
    def __init__(self, x, dp, seq, order):
        self.sizes = {"dp": dp, "seq": seq}
        self.left = [("dp", b) for b in reversed(bits_of(dp))] + [("seq", b) for b in reversed(bits_of(seq))]
        self.order = list(order)
        self.terms = [x.reshape((2,) * len(self.left) + (x.shape[0] // (dp * seq),) + x.shape[1:])]
        self.came = []

    def total(self, terms, tick):
        if len(terms) == 1:
            return terms[0]
        sum_ = terms[0].astype(F32) + terms[1].astype(F32)
        return (sum_ if tick is None else sum_ + tick.reshape(())).astype(BF16)

    def step(self, tick=None, split=1):
        name, bit = self.order.pop(0)
        axis = self.left.index((name, bit))
        self.left.pop(axis)
        mine = my_bit(name, bit)
        terms = self.terms
        if self.came:
            terms = terms + [self.came[0] if len(self.came) == 1 else jnp.concatenate(self.came, -1)]
        send = self.total([pick(term, 1 - mine, axis) for term in terms], tick)
        self.terms = [self.total([pick(term, mine, axis) for term in terms], tick)]
        width = send.shape[-1] // split
        sends = [send[..., i * width : (i + 1) * width] for i in range(split)] if split > 1 else [send]
        self.came = [flip(v, name, self.sizes[name], bit) for v in sends]
        return sends

    def result(self, tick=None):
        while self.order:
            self.step(tick)
        out = self.terms[0].astype(F32) + self.came[0].astype(F32)
        return out if tick is None else out + tick.reshape(())


def chunks_of(count, sizes):
    out, at = [], 0
    for size in sizes:
        stop = min(count, at + size)
        if stop > at:
            out.append((at, stop))
        at = stop
    return out + ([(at, count)] if at < count else [])


def shards(
    dp, seq, hidden_in, segment_ids, cluster_perm, w_qkv, bias_qv, w_out, bias_out, gain_attn,
    shift_attn, w_up, bias_up, w_down, bias_down, gain_ffn, shift_ffn, grad_out,
):
    row_count, block_len, D = hidden_in.shape
    heads = cluster_perm.shape[1]
    hs = D // heads
    L = segment_ids.shape[1]
    FF = w_up.shape[1]
    R = row_count // seq
    T = R * L
    group = 4
    scale = 1.0 / math.sqrt(hs)
    mine = lax.axis_index("seq")
    me = mine.reshape(1).astype(jnp.int32)

    hidden, gout = Rows(hidden_in, "seq", seq), Rows(grad_out, "seq", seq)
    halves = chunks_of(R, (R // 2,))
    hidden.come(0, 0, R)
    sent = [hidden.all_high(row, row + 1) for row in range(R)]
    gout_core = gout.come(0, 0, R)
    gout_sent = [gout.all_high(*half) for half in halves]

    bias = jnp.concatenate([bias_qv[:D], jnp.zeros((D,), F32), bias_qv[D:]])
    bias = jnp.broadcast_to(bias, (8, 3 * D))
    none = jnp.zeros((D,), F32)
    vec = jnp.stack([bias_out, gain_attn, shift_attn, bias_down, gain_ffn, shift_ffn, none, none])
    wt, bt, code = prepare(me, seq, w_qkv, bias, cluster_perm, segment_ids, group, sent[0])

    held = ()
    for row in range(R):
        deps = sent[row + 1] if row + 1 < R else []
        if row == min(1, R - 1):
            deps = deps + [gout_core]
        if row >= R - 2:
            deps = deps + gout_sent[min(row - R + 2, len(halves) - 1)]
        *held, tick = attend(
            me, hidden.parts(row), row, 1, R, code, wt, bt, w_out, vec, heads, hs, scale, group, deps, held
        )
    x, qkv, p, il, att, first, n1, s1 = held
    il = il.reshape(R, heads, L)
    first = first.reshape(T, D)

    held, out_blocks, sums_ffn = (), Blocks("seq", seq), []
    for start, stop in halves:
        lo, hi, *held, sums, tick = ffn(
            me, first, gout.parts(start), start, stop - start, R, w_up, bias_up.reshape(1, -1), w_down,
            vec, [], held,
        )
        out_blocks.send(lo, hi)
        sums_ffn.append(sums)
    gffn, act, slope = held

    low = [("dp", b) for b in bits_of(dp)]
    high = [("seq", b) for b in bits_of(seq)[1:]]
    core = [("seq", 0)]
    turned = low[1:2] + low[:1] + high + low[2:]

    d_down = down_grad(act, gffn, 512)
    down = Sum(d_down, dp, seq, core + low + high)
    tick, held, sums_attn, sums_up = None, (), [], []
    for i, (start, stop) in enumerate(halves):
        deps = down.step(tick)
        *held, sums1, sums2, tick = ffn_back(
            start, stop - start, gffn, slope, w_up, w_down, w_out, n1, s1, vec, att, il, heads, hs,
            deps, held,
        )
        tick = join(tick, *down.came)
        sums_attn.append(sums1)
        sums_up.append(sums2)
    gpre, gbr, do, de = held
    deps = down.step(tick)
    d_up, tick = up_grad(first, gpre, 512, deps)
    d_up, tick = out_grad(att, gbr, [], d_up)
    up = Sum(d_up, dp, seq, core + low + high)
    tick = join(tick, *down.came)
    deps = down.step(tick) + up.step()
    de = de.reshape(R, heads // group, group, L)
    g, in_blocks, sums_qkv = None, Blocks("seq", seq), []
    for start, stop in halves:
        lo = hi = None
        for row in range(start, stop):
            if row == 1:
                tick = join(tick, *down.came, *up.came)
                last = down.step(tick) if len(down.order) == 1 else []
                sends = up.step(tick, 2)
                deps = last + sends[:1]
            elif row == 2:
                tick = join(tick, *down.came, up.came[0])
                deps = sends[1:]
            elif row == 3:
                tick = join(tick, *up.came)
                deps = up.step(tick)
            elif row:
                deps = []
            g, lo, hi, sums, tick = attend_back(
                row, 1, stop - start, row - start, qkv, p, do, de, gbr, wt, heads, hs, scale, group,
                deps, (g, lo, hi),
            )
            sums_qkv.append(sums)
        in_blocks.send(lo, hi)
    if R > 3:
        tick = join(tick, *up.came, *[came for _, came in in_blocks.chunks[:1]])
    d_qkv0, d_qkv1, tick = qkv_grad(x, g, up.step(tick))
    qkv0 = Sum(d_qkv0, dp, seq, core + low + high)

    n = dp * seq
    add = lambda vs: late(functools.reduce(jnp.add, vs), tick)
    sums_qkv, sums_attn, sums_up, sums_ffn = add(sums_qkv), add(sums_attn), add(sums_up), add(sums_ffn)
    small = [
        jnp.concatenate([sums_qkv[0, :D], sums_qkv[0, 2 * D :]]),
        sums_attn[0], sums_attn[1], sums_attn[2], sums_up[0], sums_ffn[0], sums_ffn[1], sums_ffn[2],
    ]
    per = [v.size // n for v in small]
    packed = jnp.concatenate([v.reshape(n, -1) for v in small], -1)
    lanes = 128 * -(-packed.shape[1] // (128 * (D // n)))
    packed = jnp.pad(packed, ((0, 0), (0, lanes * (D // n) - packed.shape[1])))
    packed = packed.reshape(D, lanes).astype(BF16)

    qkv1 = Sum(jnp.concatenate([d_qkv1, packed], 1), dp, seq, core + turned)
    while qkv0.order or qkv1.order or up.order:
        for s in (qkv0, qkv1, up):
            if s.order:
                s.step()
    grad_in = in_blocks.result(tick)
    out_hidden = out_blocks.result(tick)
    r_down, r_up, r_qkv0, r_qkv1 = down.result(tick), up.result(tick), qkv0.result(), qkv1.result()
    vec = r_qkv1[:, 3 * D // 2 :].reshape(-1)
    cuts, at = [], 0
    for width in per:
        cuts.append(vec[at : at + width])
        at += width
    b_qv, b_out, g_attn, s_attn, b_up, b_down, g_ffn, s_ffn = cuts
    return (
        out_hidden, grad_in, jnp.concatenate([r_qkv0, r_qkv1[:, : 3 * D // 2]], 1), b_qv,
        r_up[:, FF:], b_out, g_attn, s_attn, r_up[:, :FF], b_up, r_down, b_down, g_ffn, s_ffn,
    )


def solution(mesh):
    tok = P("dp", "seq", None)
    both = ("dp", "seq")
    return jax.shard_map(
        functools.partial(shards, mesh.shape["dp"], mesh.shape["seq"]),
        mesh=mesh,
        in_specs=(tok, P("dp", None), P("dp", None, None)) + (P(),) * 12 + (tok,),
        out_specs=(
            tok, tok, P(both, None), P(both), P(both, None), P(both), P(both), P(both),
            P(both, None), P(both), P(both, None), P(both), P(both), P(both),
        ),
        check_vma=False,
    )
```

time: 479 us -> 428 us (0.89)
  waiting for transfers between devices: 142 us -> 31 us
  Pallas kernels: 221 us -> 270 us
  starting transfers between devices: 24.9 us -> 35.9 us
  other arithmetic: 39.7 us -> 30.3 us
  local copies, waits for them, and re-layouts: 43.7 us -> 53 us
    ppermute x28 -> x35, waiting for transfers between devices: 142 us -> 31 us  [flip(): return lax.ppermute(x, axis, [(i, i ^ 1 << bit) for i in range(size)])]
    pallas_call x3 -> x14, Pallas kernels: 91.3 us -> 129 us  [the longest x4 61.5 us: attend(): pl.pallas_call(functools.partial(attend_kernel, nparts=np_, heads=heads,...]
    concatenate x11 -> x10, other arithmetic: 16.2 us -> 3.94 us  [the longest x1 3 us: shards(): qkv1 = Sum(jnp.concatenate([d_qkv1, packed], 1), dp, seq, core + turned)]
    ppermute x28 -> x35, starting transfers between devices: 24.9 us -> 35.9 us  [flip(): return lax.ppermute(x, axis, [(i, i ^ 1 << bit) for i in range(size)])]
    dynamic_slice x7 -> x1, local copies, waits for them, and re-layouts: 10.5 us -> 0.08 us  [pick(): return lax.dynamic_index_in_dim(x, index, axis, keepdims=False)]
    unnamed x41 -> x110, local copies, waits for them, and re-layouts: 7.85 us -> 16.4 us
    reshape x8 -> x3, local copies, waits for them, and re-layouts: 8.4 us -> 0.08 us  [the longest x1 0.04 us: shards(): de = de.reshape(R, heads // group, group, L)]
    pallas_call x1 -> x2, Pallas kernels: 40.9 us -> 48.5 us  [ffn_back(): pl.pallas_call(functools.partial(ffn_back_kernel, heads=heads, hs=hs), gr...]
  transfers between devices with their start and end apart: 28 -> 35, of which waited for: 12 -> 10; matrix products, arithmetic and copies ran while one was open for 15% -> 12% of each run, Pallas kernels for 18% -> 50%
where the time goes in v2:
time: 428 us; the launch traced here: 423 us
  Pallas kernels  270 us (63%)
  local copies, waits for them, and re-layouts  53 us (12%)
  starting transfers between devices  35.9 us (8%)
  waiting for transfers between devices  31 us (7%)
  other arithmetic  30.3 us (7%)
    pallas_call x4, Pallas kernels, attend(): pl.pallas_call(functools.partial(attend_kernel, nparts=np_, heads=heads,...  61.5 us
    pallas_call x4, Pallas kernels, attend_back(): pl.pallas_call(functools.partial(attend_back_kernel, heads=heads, hs=hs,...  58.7 us
    pallas_call x2, Pallas kernels, ffn_back(): pl.pallas_call(functools.partial(ffn_back_kernel, heads=heads, hs=hs), gr...  48.5 us
    pallas_call x2, Pallas kernels, ffn(): pl.pallas_call(functools.partial(ffn_kernel, nparts=np_, nio=nio), grid_s...  44.3 us
    ppermute x35, starting transfers between devices, flip(): return lax.ppermute(x, axis, [(i, i ^ 1 << bit) for i in range(size)])  35.9 us
    ppermute x35, waiting for transfers between devices, flip(): return lax.ppermute(x, axis, [(i, i ^ 1 << bit) for i in range(size)])  31 us
    unnamed x110, local copies, waits for them, and re-layouts  16.4 us
    pallas_call x1, Pallas kernels, qkv_grad(): pl.pallas_call(qkv_grad_kernel, grid=(2 * half,), in_specs=[whole((R, L,...  14.7 us
  transfers between devices with their start and end apart: 35, of which 10 were waited for; matrix products, arithmetic and copies ran while one was open for 12% of the time, Pallas kernels for 50%

profile of v2, /device:TPU:0, one launch (start us, length us, event | category | flops | bytes accessed | tf_op | source)
XLA Modules:
  0.0 422.7 jit_solution(5221430198147658153)
XLA Ops:
  0.7 2.8 dynamic-slice_bitcast_fusion
  4.3 2.3 copy.82.perm_ref
  6.8 2.2 fusion.57
  10.3 2.7 collective-permute-start.6
  19.2 1.8 prepare.1
  21.0 1.8 copy-done
  22.8 2.1 collective-permute-start.7
  24.9 15.6 %attend.4 = (bf16[4,512,768]{2,1,0:T(8,128)(2,1)S(1)}, bf16[4,2304,512]{2,1,0:T(8,128)(2,1)}, bf16[4,12,512,512]{3,2,1,0:T(8,128)(2,1)}, f32[4,3,4,512]{3,2,1,0:...) custom-call(s32[1]{0:T(128)} %bitcast.me_ref, ...), custom_call_target="tpu_custom_call" | custom-call | flops 5637144576 | bytes 6291456 | tf_op jit(solution)/shard_map/attend/pallas_call | solution.py:138
  40.5 15.2 %attend.5 = (bf16[4,512,768]{2,1,0:T(8,128)(2,1)S(1)}, bf16[4,2304,512]{2,1,0:T(8,128)(2,1)}, bf16[4,12,512,512]{3,2,1,0:T(8,128)(2,1)}, f32[4,3,4,512]{3,2,1,0:...) custom-call(s32[1]{0:T(128)} %bitcast.me_ref, ...), custom_call_target="tpu_custom_call", output_to_operand_aliasing={{0}: (11, {}), {1}: (12, {}), {2}: (13, {}), {3}: (14, {}),... | custom-call | flops 5637144576 | bytes 6291456 | tf_op jit(solution)/shard_map/attend/pallas_call | solution.py:138
  55.6 15.7 %attend.6 = (bf16[4,512,768]{2,1,0:T(8,128)(2,1)S(1)}, bf16[4,2304,512]{2,1,0:T(8,128)(2,1)}, bf16[4,12,512,512]{3,2,1,0:T(8,128)(2,1)}, f32[4,3,4,512]{3,2,1,0:...) custom-call(s32[1]{0:T(128)} %bitcast.me_ref, ...), custom_call_target="tpu_custom_call", output_to_operand_aliasing={{0}: (11, {}), {1}: (12, {}), {2}: (13, {}), {3}: (14, {}),... | custom-call | flops 5637144576 | bytes 6291456 | tf_op jit(solution)/shard_map/attend/pallas_call | solution.py:138
  71.3 15.2 %attend.7 = (bf16[4,512,768]{2,1,0:T(8,128)(2,1)S(1)}, bf16[4,2304,512]{2,1,0:T(8,128)(2,1)}, bf16[4,12,512,512]{3,2,1,0:T(8,128)(2,1)}, f32[4,3,4,512]{3,2,1,0:...) custom-call(s32[1]{0:T(128)} %bitcast.me_ref, ...), custom_call_target="tpu_custom_call", output_to_operand_aliasing={{0}: (10, {}), {1}: (11, {}), {2}: (12, {}), {3}: (13, {}),... | custom-call | flops 5637144576 | bytes 6291456 | tf_op jit(solution)/shard_map/attend/pallas_call | solution.py:138
  87.5 23.1 %ffn.2 = (bf16[2,256,768]{2,1,0:T(8,128)(2,1)S(1)}, bf16[2,256,768]{2,1,0:T(8,128)(2,1)}, bf16[2048,768]{1,0:T(8,128)(2,1)}, bf16[2048,3072]{1,0:T(8,128)(2,1)},...) custom-call(s32[1]{0:T(128)} %bitcast.me_ref, bf16[16,128,768]{2,1,0:T(8,128)(2,1)} %refs_0_.11, ...), custom_call_target="tpu_custom_call" | custom-call | flops 12562779136 | bytes 22020096 | tf_op jit(solution)/shard_map/ffn/pallas_call | solution.py:270
  110.6 21.2 %ffn.3 = (bf16[2,256,768]{2,1,0:T(8,128)(2,1)S(1)}, bf16[2,256,768]{2,1,0:T(8,128)(2,1)}, bf16[2048,768]{1,0:T(8,128)(2,1)}, bf16[2048,3072]{1,0:T(8,128)(2,1)},...) custom-call(s32[1]{0:T(128)} %bitcast.me_ref, ...), custom_call_target="tpu_custom_call", output_to_operand_aliasing={{2}: (9, {}), {3}: (10, {}), {4}: (11, {})} | custom-call | flops 12562779136 | bytes 22020096 | tf_op jit(solution)/shard_map/ffn/pallas_call | solution.py:270
  131.9 1.9 copy-done.16
  133.8 13.7 %down_grad.1 = bf16[3072,768]{1,0:T(8,128)(2,1)} custom-call(bf16[2048,3072]{1,0:T(8,128)(2,1)} %get-tuple-element.144.act_ref, bf16[2048,768]{1,0:T(8,128)(2,1)S(1)} %copy-done.16), custom_call_target="tpu_custom_call" | custom-call | flops 12562779136 | bytes 17301504 | tf_op jit(solution)/shard_map/down_grad/pallas_call | solution.py:302
  147.4 3.2 copy_bitcast_fusion.1
  150.8 2.0 fusion.65.rest_0_
  153.1 24.2 %ffn_back.2 = (bf16[2048,3072]{1,0:T(8,128)(2,1)}, bf16[4,512,768]{2,1,0:T(8,128)(2,1)}, bf16[4,768,512]{2,1,0:T(8,128)(2,1)}, f32[4,12,512]{2,1,0:T(8,128)S(1)}...) custom-call(bf16[2048,768]{1,0:T(8,128)(2,1)} %get-tuple-element.138.g_ref, ...), custom_call_target="tpu_custom_call" | custom-call | flops 14495514624 | bytes 22020096 | tf_op jit(solution)/shard_map/ffn_back/pallas_call | solution.py:357
  178.0 1.8 copy.88.refs_1_
  181.0 3.0 fusion.5
  185.6 24.2 %ffn_back.3 = (bf16[2048,3072]{1,0:T(8,128)(2,1)}, bf16[4,512,768]{2,1,0:T(8,128)(2,1)}, bf16[4,768,512]{2,1,0:T(8,128)(2,1)}, f32[4,12,512]{2,1,0:T(8,128)S(1)}...) custom-call(bf16[2048,768]{1,0:T(8,128)(2,1)} %get-tuple-element.138, ...), custom_call_target="tpu_custom_call", output_to_operand_aliasing={{0}: (11, {}), {1}: (12, {}), {2}: (13, {}), {3}: (14, {})} | custom-call | flops 14495514624 | bytes 22020096 | tf_op jit(solution)/shard_map/ffn_back/pallas_call | solution.py:357
  214.8 13.8 %up_grad.1 = (bf16[768,3840]{1,0:T(8,128)(2,1)}, f32[1,1]{1,0:T(1,128)}) custom-call(bf16[2048,768]{1,0:T(8,128)(2,1)S(1)} %bitcast.251, bf16[2048,3072]{1,0:T(8,128)(2,1)} %get-tuple-element.153.g_ref, bf16[2,2,96,768]{3,2,1,0:T(8,128)(2,1)S(1)} %get-tuple-element.209.rest_0_), custom_call_target="tpu_custom_call" | custom-call | flops 12562779136 | bytes 17301504 | tf_op jit(solution)/shard_map/up_grad/pallas_call | solution.py:390
  228.5 5.8 %out_grad.1 = (bf16[768,3840]{1,0:T(8,128)(2,1)}, f32[1,1]{1,0:T(1,128)}) custom-call(bf16[4,768,512]{2,1,0:T(8,128)(2,1)S(1)} %copy-done.4, bf16[4,512,768]{2,1,0:T(8,128)(2,1)} %get-tuple-element.152.g_ref.gone_ref, bf16[768,3840]{1,0:T(8,128)(2,1)} %get-tuple-element.155.rest_0_), custom_call_target="tpu_custom_call", output_to_operand_aliasing={{0}: (2, {})} | custom-call | flops 3140694784 | bytes 6291456 | tf_op jit(solution)/shard_map/out_grad/pallas_call | solution.py:415
  234.4 3.6 copy_bitcast_fusion
  238.3 1.7 collective-permute-start.8
  243.3 2.6 copy-done.30
  246.1 9.3 %collective-permute-done.13.refs_1_ = bf16[2,2,96,768]{3,2,1,0:T(8,128)(2,1)S(1)} collective-permute-done((bf16[2,2,96,768]{3,2,1,0:T(8,128)(2,1)S(1)}, bf16[2,2,96,768]{3,2,1,0:T(8,128)(2,1)S(1)}, u32[]{:S(2)}, u32[]{:S(2)}) %collective-permute-start.13) | collective-permute-done | bytes 589856 | tf_op jit(solution)/shard_map/ppermute | solution.py:540
  257.4 2.7 collective-permute-start.14
  260.1 15.5 %attend_back.4 = (bf16[4,2304,512]{2,1,0:T(8,128)(2,1)}, bf16[2,256,768]{2,1,0:T(8,128)(2,1)S(1)}, bf16[2,256,768]{2,1,0:T(8,128)(2,1)S(1)}, f32[8,2304]{1,0:T(8,128)S(1)}, f32[1,1]{1,0:T(1,128)}) custom-call(bf16[4,2304,512]{2,1,0:T(8,128)(2,1)} %get-tuple-element.136.qkv_ref, bf16[4,12,512,512]{3,2,1,0:T(8,128)(2,1)} %get-tuple-element.137.p_ref, ...), custom_call_target="tpu_custom_call" | custom-call | flops 8254390272 | bytes 6291456 | tf_op jit(solution)/shard_map/attend_back/pallas_call | solution.py:475
  275.5 2.0 copy.96.refs_2_
  278.7 3.6 fusion.3
  285.9 14.3 %attend_back.5 = (bf16[4,2304,512]{2,1,0:T(8,128)(2,1)}, bf16[2,256,768]{2,1,0:T(8,128)(2,1)S(1)}, bf16[2,256,768]{2,1,0:T(8,128)(2,1)S(1)}, f32[8,2304]{1,0:T(8,128)S(1)}, f32[1,1]{1,0:T(1,128)}) custom-call(bf16[4,2304,512]{2,1,0:T(8,128)(2,1)} %get-tuple-element.136.qkv_ref, ...), custom_call_target="tpu_custom_call", output_to_operand_aliasing={{0}: (8, {}), {1}: (9, {}), {2}: (10, {})} | custom-call | flops 8254390272 | bytes 6291456 | tf_op jit(solution)/shard_map/attend_back/pallas_call | solution.py:475
  300.2 14.4 %attend_back.6 = (bf16[4,2304,512]{2,1,0:T(8,128)(2,1)}, bf16[2,256,768]{2,1,0:T(8,128)(2,1)S(1)}, bf16[2,256,768]{2,1,0:T(8,128)(2,1)}, f32[8,2304]{1,0:T(8,128)S(1)}, f32[1,1]{1,0:T(1,128)}) custom-call(bf16[4,2304,512]{2,1,0:T(8,128)(2,1)} %get-tuple-element.136.qkv_ref, ...), custom_call_target="tpu_custom_call", output_to_operand_aliasing={{0}: (7, {})} | custom-call | flops 8254390272 | bytes 6291456 | tf_op jit(solution)/shard_map/attend_back/pallas_call | solution.py:475
  318.6 1.6 collective-permute-start.17
  320.3 14.6 %attend_back.7 = (bf16[4,2304,512]{2,1,0:T(8,128)(2,1)}, bf16[2,256,768]{2,1,0:T(8,128)(2,1)S(1)}, bf16[2,256,768]{2,1,0:T(8,128)(2,1)}, f32[8,2304]{1,0:T(8,128)S(1)}, f32[1,1]{1,0:T(1,128)}) custom-call(bf16[4,2304,512]{2,1,0:T(8,128)(2,1)} %get-tuple-element.136.qkv_ref, ...), custom_call_target="tpu_custom_call", output_to_operand_aliasing={{0}: (7, {}), {1}: (8, {}), {2}: (9, {})} | custom-call | flops 8254390272 | bytes 6291456 | tf_op jit(solution)/shard_map/attend_back/pallas_call | solution.py:475
  340.2 14.7 %qkv_grad.1 = (bf16[768,1152]{1,0:T(8,128)(2,1)S(1)}, bf16[768,1152]{1,0:T(8,128)(2,1)S(1)}, f32[1,1]{1,0:T(1,128)}) custom-call(bf16[4,512,768]{2,1,0:T(8,128)(2,1)} %copy-done.6, bf16[4,2304,512]{2,1,0:T(8,128)(2,1)} %get-tuple-element.167.g_ref, bf16[2,24,3840]{2,1,0:T(8,128)(2,1)S(1)} %get-tuple-element.227.rest_0_), custom_call_target="tpu_custom_call" | custom-call | flops 9422084096 | bytes 12582912 | tf_op jit(solution)/shard_map/qkv_grad/pallas_call | solution.py:520
  366.9 1.7 convert_element_type.584
  368.6 3.0 pad_maximum_fusion
  373.4 3.2 fusion.31
  378.4 2.1 maximum_add_fusion
  388.9 2.8 collective-permute-done.33
  394.7 4.0 collective-permute-done.23
  399.4 2.5 collective-permute-done.28
  402.1 3.9 collective-permute-done.24
  406.1 2.7 collective-permute-start.25
  409.8 3.4 collective-permute-done.25
  414.2 2.4 collective-permute-start.31
  417.5 2.5 collective-permute-done.31
  (272 shorter events, 69.9 us)
Async XLA Ops:
  3.5 6.6 %collective-permute-start.2 = (bf16[2,4,128,768]{3,2,1,0:T(8,128)(2,1)}, bf16[2,4,128,768]{3,2,1,0:T(8,128)(2,1)S(1)}, u32[]{:S(2)}, u32[]{:S(2)}) collective-permute-start(bf16[2,4,128,768]{3,2,1,0:T(8,128)(2,1)} %dynamic-slice_bitcast_fusion), channel_id=1, source_target_pairs={{0,1},{1,0},{2,3},{3,2},{4,5},{5,4},{6,7},{7,6},{8,9},{9,8},{10,11... | collective-permute-start | bytes 4718600 | tf_op jit(solution)/shard_map/ppermute | solution.py:540
  4.1 11.1 %collective-permute-start = (bf16[2,4,128,768]{3,2,1,0:T(8,128)(2,1)S(1)}, bf16[2,4,128,768]{3,2,1,0:T(8,128)(2,1)}, u32[]{:S(2)}, u32[]{:S(2)}) collective-permute-start(bf16[2,4,128,768]{3,2,1,0:T(8,128)(2,1)S(1)} %dynamic-slice_bitcast_fusion.1.refs_9_), channel_id=1, source_target_pairs={{0,1},{1,0},{2,3},{3,2},{4,5},{5,4},{6,7},{7,6},{8,9},{9,8},{10,11... | collective-permute-start | bytes 4718600 | tf_op jit(solution)/shard_map/ppermute | solution.py:540
  10.3 12.6 %collective-permute-start.6 = (bf16[1,256,768]{2,1,0:T(8,128)(2,1)S(1)}, bf16[1,256,768]{2,1,0:T(8,128)(2,1)S(1)}, u32[]{:S(2)}, u32[]{:S(2)}) collective-permute-start(bf16[1,256,768]{2,1,0:T(8,128)(2,1)S(1)} %pad_maximum_fusion.6.rest_0_), channel_id=1, source_target_pairs={{0,2},{1,3},{2,0},{3,1},{4,6},{5,7},{6,4},{7,5},{8,10},{9,11},{10,... | collective-permute-start | bytes 1179656 | tf_op jit(solution)/shard_map/ppermute | solution.py:540
  13.0 27.4 %collective-permute-start.5 = (bf16[1,256,768]{2,1,0:T(8,128)(2,1)S(1)}, bf16[1,256,768]{2,1,0:T(8,128)(2,1)S(1)}, u32[]{:S(2)}, u32[]{:S(2)}) collective-permute-start(bf16[1,256,768]{2,1,0:T(8,128)(2,1)S(1)} %pad_maximum_fusion.8.refs_8_), channel_id=1, source_target_pairs={{0,2},{1,3},{2,0},{3,1},{4,6},{5,7},{6,4},{7,5},{8,10},{9,11},{10,... | collective-permute-start | bytes 1179656 | tf_op jit(solution)/shard_map/ppermute | solution.py:540
  14.0 41.6 %collective-permute-start.4 = (bf16[1,256,768]{2,1,0:T(8,128)(2,1)S(1)}, bf16[1,256,768]{2,1,0:T(8,128)(2,1)S(1)}, u32[]{:S(2)}, u32[]{:S(2)}) collective-permute-start(bf16[1,256,768]{2,1,0:T(8,128)(2,1)S(1)} %pad_maximum_fusion.7.refs_8_), channel_id=1, source_target_pairs={{0,2},{1,3},{2,0},{3,1},{4,6},{5,7},{6,4},{7,5},{8,10},{9,11},{10,... | collective-permute-start | bytes 1179656 | tf_op jit(solution)/shard_map/ppermute | solution.py:540
  16.9 54.5 %collective-permute-start.3 = (bf16[1,256,768]{2,1,0:T(8,128)(2,1)S(1)}, bf16[1,256,768]{2,1,0:T(8,128)(2,1)S(1)}, u32[]{:S(2)}, u32[]{:S(2)}) collective-permute-start(bf16[1,256,768]{2,1,0:T(8,128)(2,1)S(1)} %pad_maximum_fusion.5.refs_8_), channel_id=1, source_target_pairs={{0,2},{1,3},{2,0},{3,1},{4,6},{5,7},{6,4},{7,5},{8,10},{9,11},{10,... | collective-permute-start | bytes 1179656 | tf_op jit(solution)/shard_map/ppermute | solution.py:540
  17.9 69.6 %collective-permute-start.1 = (bf16[2,256,768]{2,1,0:T(8,128)(2,1)S(1)}, bf16[2,256,768]{2,1,0:T(8,128)(2,1)S(1)}, u32[]{:S(2)}, u32[]{:S(2)}) collective-permute-start(bf16[2,256,768]{2,1,0:T(8,128)(2,1)S(1)} %pad_maximum_fusion.3.refs_9_), channel_id=1, source_target_pairs={{0,2},{1,3},{2,0},{3,1},{4,6},{5,7},{6,4},{7,5},{8,10},{9,11},{10,... | collective-permute-start | bytes 2359304 | tf_op jit(solution)/shard_map/ppermute | solution.py:540
  22.8 87.8 %collective-permute-start.7 = (bf16[2,256,768]{2,1,0:T(8,128)(2,1)S(1)}, bf16[2,256,768]{2,1,0:T(8,128)(2,1)S(1)}, u32[]{:S(2)}, u32[]{:S(2)}) collective-permute-start(bf16[2,256,768]{2,1,0:T(8,128)(2,1)S(1)} %pad_maximum_fusion.4.refs_8_), channel_id=1, source_target_pairs={{0,2},{1,3},{2,0},{3,1},{4,6},{5,7},{6,4},{7,5},{8,10},{9,11},{10,... | collective-permute-start | bytes 2359304 | tf_op jit(solution)/shard_map/ppermute | solution.py:540
  24.9 15.6 %copy-start.15 = (bf16[2,4,128,768]{3,2,1,0:T(8,128)(2,1)S(1)}, bf16[2,4,128,768]{3,2,1,0:T(8,128)(2,1)}, u32[]{:S(2)}) copy-start(bf16[2,4,128,768]{3,2,1,0:T(8,128)(2,1)} %copy-done.14) | copy-start | bytes 4718596
  71.3 16.2 %copy-start.29 = (f32[3072]{0:T(1024)S(1)}, f32[3072]{0:T(1024)}, u32[]{:S(2)}) copy-start(f32[3072]{0:T(1024)} %param.26) | copy-start | bytes 36868
  87.5 23.1 %copy-start.3 = (bf16[4,768,512]{2,1,0:T(8,128)(2,1)}, bf16[4,768,512]{2,1,0:T(8,128)(2,1)S(1)}, u32[]{:S(2)}) copy-start(bf16[4,768,512]{2,1,0:T(8,128)(2,1)S(1)} %get-tuple-element.142.att_ref) | copy-start | bytes 9437188
  87.5 23.1 %copy-start.6 = (bf16[4,512,768]{2,1,0:T(8,128)(2,1)}, bf16[4,512,768]{2,1,0:T(8,128)(2,1)S(1)}, u32[]{:S(2)}) copy-start(bf16[4,512,768]{2,1,0:T(8,128)(2,1)S(1)} %get-tuple-element.135.x_ref) | copy-start | bytes 9437188
  131.9 15.6 %copy-start.21 = (f32[8,768]{1,0:T(8,128)}, f32[8,768]{1,0:T(8,128)S(1)}, u32[]{:S(2)}) copy-start(f32[8,768]{1,0:T(8,128)S(1)} %get-tuple-element.185) | copy-start | bytes 73732
  150.7 27.3 %collective-permute-start.10 = (bf16[2,2,2,2,96,768]{5,4,3,1,0,2:T(8,128)(2,1)}, bf16[2,2,2,2,96,768]{5,4,3,1,0,2:T(8,128)(2,1)}, u32[]{:S(2)}, u32[]{:S(2)}) collective-permute-start(bf16[2,2,2,2,96,768]{5,4,3,1,0,2:T(8,128)(2,1)} %copy_bitcast_fusion.1), channel_id=1, source_target_pairs={{0,1},{1,0},{2,3},{3,2},{4,5},{5,4},{6,7},{7,6},{8,9},{9,8},{10,11... | collective-permute-start | bytes 7077896 | tf_op jit(solution)/shard_map/ppermute | solution.py:540
  150.8 30.2 %slice-start = ((s8[4718592]{0:T(1024)(128)(4,1)}), s8[4194304]{0:T(1024)(128)(4,1)S(1)}, s32[]{:S(2)}) async-start(s8[4718592]{0:T(1024)(128)(4,1)} %bitcast.269), calls=%async_computation | async-start | bytes 8388608
  153.1 27.9 %slice-start.1 = ((s8[4718592]{0:T(1024)(128)(4,1)}), s8[524288]{0:T(1024)(128)(4,1)S(1)}, s32[]{:S(2)}) async-start(s8[4718592]{0:T(1024)(128)(4,1)} %bitcast.269), calls=%async_computation.1 | async-start | bytes 1048576
  184.0 28.4 %collective-permute-start.11 = (bf16[2,2,2,96,768]{4,3,2,1,0:T(8,128)(2,1)S(1)}, bf16[2,2,2,96,768]{4,3,2,1,0:T(8,128)(2,1)S(1)}, u32[]{:S(2)}, u32[]{:S(2)}) collective-permute-start(bf16[2,2,2,96,768]{4,3,2,1,0:T(8,128)(2,1)S(1)} %get-tuple-element.197.rest_0_), channel_id=1, source_target_pairs={{0,4},{4,0},{8,12},{12,8},{16,20},{20,16},{24,28},{28,24},{1,5},{5... | collective-permute-start | bytes 3538952 | tf_op jit(solution)/shard_map/ppermute | solution.py:540
  238.0 37.5 %collective-permute-start.12 = (bf16[2,2,2,2,24,3840]{5,4,3,1,0,2:T(8,128)(2,1)}, bf16[2,2,2,2,24,3840]{5,4,3,1,0,2:T(8,128)(2,1)}, u32[]{:S(2)}, u32[]{:S(2)}) collective-permute-start(bf16[2,2,2,2,24,3840]{5,4,3,1,0,2:T(8,128)(2,1)} %copy_bitcast_fusion), channel_id=1, source_target_pairs={{0,1},{1,0},{2,3},{3,2},{4,5},{5,4},{6,7},{7,6},{8,9},{9,8},{10,11... | collective-permute-start | bytes 8847368 | tf_op jit(solution)/shard_map/ppermute | solution.py:540
  238.0 139.9 %collective-permute-start.9 = (bf16[2,256,768]{2,1,0:T(8,128)(2,1)}, bf16[2,256,768]{2,1,0:T(8,128)(2,1)}, u32[]{:S(2)}, u32[]{:S(2)}) collective-permute-start(bf16[2,256,768]{2,1,0:T(8,128)(2,1)} %get-tuple-element.134), channel_id=1, source_target_pairs={{0,2},{1,3},{2,0},{3,1},{4,6},{5,7},{6,4},{7,5},{8,10},{9,11},{10,... | collective-permute-start | bytes 2359304 | tf_op jit(solution)/shard_map/ppermute | solution.py:540
  238.3 140.1 %collective-permute-start.8 = (bf16[2,256,768]{2,1,0:T(8,128)(2,1)}, bf16[2,256,768]{2,1,0:T(8,128)(2,1)}, u32[]{:S(2)}, u32[]{:S(2)}) collective-permute-start(bf16[2,256,768]{2,1,0:T(8,128)(2,1)} %get-tuple-element.133), channel_id=1, source_target_pairs={{0,2},{1,3},{2,0},{3,1},{4,6},{5,7},{6,4},{7,5},{8,10},{9,11},{10,... | collective-permute-start | bytes 2359304 | tf_op jit(solution)/shard_map/ppermute | solution.py:540
  240.2 15.2 %collective-permute-start.13 = (bf16[2,2,96,768]{3,2,1,0:T(8,128)(2,1)S(1)}, bf16[2,2,96,768]{3,2,1,0:T(8,128)(2,1)S(1)}, u32[]{:S(2)}, u32[]{:S(2)}) collective-permute-start(bf16[2,2,96,768]{3,2,1,0:T(8,128)(2,1)S(1)} %get-tuple-element.209.rest_0_), channel_id=1, source_target_pairs={{0,8},{4,12},{8,0},{12,4},{16,24},{20,28},{24,16},{28,20},{1,9},{5... | collective-permute-start | bytes 1769480 | tf_op jit(solution)/shard_map/ppermute | solution.py:540
  243.2 32.4 %copy-start.37 = (bf16[16,128,768]{2,1,0:T(8,128)(2,1)}, bf16[16,128,768]{2,1,0:T(8,128)(2,1)S(1)}, u32[]{:S(2)}) copy-start(bf16[16,128,768]{2,1,0:T(8,128)(2,1)S(1)} %get-tuple-element.217) | copy-start | bytes 9437188
  245.9 14.2 %copy-start.2 = (bf16[4,512,768]{2,1,0:T(8,128)(2,1)S(1)}, bf16[4,512,768]{2,1,0:T(8,128)(2,1)}, u32[]{:S(2)}) copy-start(bf16[4,512,768]{2,1,0:T(8,128)(2,1)} %get-tuple-element.152.g_ref.gone_ref) | copy-start | bytes 9437188
  245.9 14.2 %copy-start.5 = (bf16[4,768,512]{2,1,0:T(8,128)(2,1)S(1)}, bf16[4,768,512]{2,1,0:T(8,128)(2,1)}, u32[]{:S(2)}) copy-start(bf16[4,768,512]{2,1,0:T(8,128)(2,1)} %get-tuple-element.150.do_ref) | copy-start | bytes 9437188
  257.4 27.2 %copy-start.43 = (bf16[1,2,96,768]{3,2,1,0:T(8,128)(2,1)}, bf16[1,2,96,768]{3,2,1,0:T(8,128)(2,1)S(1)}, u32[]{:S(2)}) copy-start(bf16[1,2,96,768]{3,2,1,0:T(8,128)(2,1)S(1)} %get-tuple-element.230) | copy-start | bytes 884740
  257.4 20.2 %collective-permute-start.14 = (bf16[2,96,768]{2,1,0:T(8,128)(2,1)S(1)}, bf16[2,96,768]{2,1,0:T(8,128)(2,1)S(1)}, u32[]{:S(2)}, u32[]{:S(2)}) collective-permute-start(bf16[2,96,768]{2,1,0:T(8,128)(2,1)S(1)} %get-tuple-element.231.rest_0_), channel_id=1, source_target_pairs={{0,16},{4,20},{8,24},{12,28},{16,0},{20,4},{24,8},{28,12},{1,17},{... | collective-permute-start | bytes 884744 | tf_op jit(solution)/shard_map/ppermute | solution.py:540
  282.5 32.1 %collective-permute-start.15 = (bf16[2,2,2,24,1920]{4,3,2,1,0:T(8,128)(2,1)S(1)}, bf16[2,2,2,24,1920]{4,3,2,1,0:T(8,128)(2,1)S(1)}, u32[]{:S(2)}, u32[]{:S(2)}) collective-permute-start(bf16[2,2,2,24,1920]{4,3,2,1,0:T(8,128)(2,1)S(1)} %get-tuple-element.228.rest_1_), channel_id=1, source_target_pairs={{0,4},{4,0},{8,12},{12,8},{16,20},{20,16},{24,28},{28,24},{1,5},{5... | collective-permute-start | bytes 2211848 | tf_op jit(solution)/shard_map/ppermute | solution.py:540
  284.1 32.2 %collective-permute-start.16 = (bf16[2,2,2,24,1920]{4,3,2,1,0:T(8,128)(2,1)S(1)}, bf16[2,2,2,24,1920]{4,3,2,1,0:T(8,128)(2,1)S(1)}, u32[]{:S(2)}, u32[]{:S(2)}) collective-permute-start(bf16[2,2,2,24,1920]{4,3,2,1,0:T(8,128)(2,1)S(1)} %get-tuple-element.229.rest_0_), channel_id=1, source_target_pairs={{0,4},{4,0},{8,12},{12,8},{16,20},{20,16},{24,28},{28,24},{1,5},{5... | collective-permute-start | bytes 2211848 | tf_op jit(solution)/shard_map/ppermute | solution.py:540
  285.3 88.0 %collective-permute-start.34 = (bf16[96,768]{1,0:T(8,128)(2,1)S(1)}, bf16[96,768]{1,0:T(8,128)(2,1)}, u32[]{:S(2)}, u32[]{:S(2)}) collective-permute-start(bf16[96,768]{1,0:T(8,128)(2,1)S(1)} %fusion.44.rest_0_), channel_id=1, source_target_pairs={{0,2},{1,3},{2,0},{3,1},{4,6},{5,7},{6,4},{7,5},{8,10},{9,11},{10,... | collective-permute-start | bytes 442376 | tf_op jit(solution)/shard_map/ppermute | solution.py:540
  314.6 21.9 %collective-permute-start.18 = (bf16[2,256,768]{2,1,0:T(8,128)(2,1)S(1)}, bf16[2,256,768]{2,1,0:T(8,128)(2,1)S(1)}, u32[]{:S(2)}, u32[]{:S(2)}) collective-permute-start(bf16[2,256,768]{2,1,0:T(8,128)(2,1)S(1)} %get-tuple-element.169), channel_id=1, source_target_pairs={{0,2},{1,3},{2,0},{3,1},{4,6},{5,7},{6,4},{7,5},{8,10},{9,11},{10,... | collective-permute-start | bytes 2359304 | tf_op jit(solution)/shard_map/ppermute | solution.py:540
  318.6 18.4 %collective-permute-start.17 = (bf16[2,2,24,3840]{3,2,1,0:T(8,128)(2,1)S(1)}, bf16[2,2,24,3840]{3,2,1,0:T(8,128)(2,1)S(1)}, u32[]{:S(2)}, u32[]{:S(2)}) collective-permute-start(bf16[2,2,24,3840]{3,2,1,0:T(8,128)(2,1)S(1)} %get-tuple-element.205.rest_0_), channel_id=1, source_target_pairs={{0,8},{4,12},{8,0},{12,4},{16,24},{20,28},{24,16},{28,20},{1,9},{5... | collective-permute-start | bytes 2211848 | tf_op jit(solution)/shard_map/ppermute | solution.py:540
  336.5 18.3 %copy-start.34 = (bf16[16,128,768]{2,1,0:T(8,128)(2,1)}, bf16[16,128,768]{2,1,0:T(8,128)(2,1)S(1)}, u32[]{:S(2)}) copy-start(bf16[16,128,768]{2,1,0:T(8,128)(2,1)S(1)} %get-tuple-element.213) | copy-start | bytes 9437188
  336.5 41.8 %collective-permute-start.20 = (bf16[2,256,768]{2,1,0:T(8,128)(2,1)}, bf16[2,256,768]{2,1,0:T(8,128)(2,1)}, u32[]{:S(2)}, u32[]{:S(2)}) collective-permute-start(bf16[2,256,768]{2,1,0:T(8,128)(2,1)} %get-tuple-element.173), channel_id=1, source_target_pairs={{0,2},{1,3},{2,0},{3,1},{4,6},{5,7},{6,4},{7,5},{8,10},{9,11},{10,... | collective-permute-start | bytes 2359304 | tf_op jit(solution)/shard_map/ppermute | solution.py:540
  339.9 43.7 %collective-permute-start.32 = (bf16[2,24,3840]{2,1,0:T(8,128)(2,1)S(1)}, bf16[2,24,3840]{2,1,0:T(8,128)(2,1)}, u32[]{:S(2)}, u32[]{:S(2)}) collective-permute-start(bf16[2,24,3840]{2,1,0:T(8,128)(2,1)S(1)} %get-tuple-element.227.rest_0_), channel_id=1, source_target_pairs={{0,16},{4,20},{8,24},{12,28},{16,0},{20,4},{24,8},{28,12},{1,17},{... | collective-permute-start | bytes 1105928 | tf_op jit(solution)/shard_map/ppermute | solution.py:540
  340.2 15.9 %copy-start.22 = (f32[8,768]{1,0:T(8,128)S(1)}, f32[8,768]{1,0:T(8,128)}, u32[]{:S(2)}) copy-start(f32[8,768]{1,0:T(8,128)} %copy-done.21) | copy-start | bytes 73732
  373.3 13.1 %collective-permute-start.22 = (bf16[2,2,2,2,24,1152]{5,4,3,1,0,2:T(8,128)(2,1)}, bf16[2,2,2,2,24,1152]{5,4,3,1,0,2:T(8,128)(2,1)S(1)}, u32[]{:S(2)}, u32[]{:S(2)}) collective-permute-start(bf16[2,2,2,2,24,1152]{5,4,3,1,0,2:T(8,128)(2,1)} %copy_bitcast_fusion.3), channel_id=1, source_target_pairs={{0,1},{1,0},{2,3},{3,2},{4,5},{5,4},{6,7},{7,6},{8,9},{9,8},{10,11... | collective-permute-start | bytes 2654216 | tf_op jit(solution)/shard_map/ppermute | solution.py:540
  377.9 10.3 %collective-permute-start.27 = (bf16[2,2,2,2,24,1280]{5,4,0,3,2,1:T(8,128)(2,1)S(1)}, bf16[2,2,2,2,24,1280]{5,4,0,3,2,1:T(8,128)(2,1)S(1)}, u32[]{:S(2)}, u32[]{:S(2)}) collective-permute-start(bf16[2,2,2,2,24,1280]{5,4,0,3,2,1:T(8,128)(2,1)S(1)} %copy_bitcast_fusion.2), channel_id=1, source_target_pairs={{0,1},{1,0},{2,3},{3,2},{4,5},{5,4},{6,7},{7,6},{8,9},{9,8},{10,11... | collective-permute-start | bytes 2949128 | tf_op jit(solution)/shard_map/ppermute | solution.py:540
  381.8 27.0 %collective-permute-start.21 = (bf16[2,4,128,768]{3,2,1,0:T(8,128)(2,1)S(1)}, bf16[2,4,128,768]{3,2,1,0:T(8,128)(2,1)S(1)}, u32[]{:S(2)}, u32[]{:S(2)}) collective-permute-start(bf16[2,4,128,768]{3,2,1,0:T(8,128)(2,1)S(1)} %pad_maximum_fusion.2), channel_id=1, source_target_pairs={{0,1},{1,0},{2,3},{3,2},{4,5},{5,4},{6,7},{7,6},{8,9},{9,8},{10,11... | collective-permute-start | bytes 4718600 | tf_op jit(solution)/shard_map/ppermute | solution.py:540
  383.3 25.7 %collective-permute-start.19 = (bf16[2,4,128,768]{3,2,1,0:T(8,128)(2,1)S(1)}, bf16[2,4,128,768]{3,2,1,0:T(8,128)(2,1)S(1)}, u32[]{:S(2)}, u32[]{:S(2)}) collective-permute-start(bf16[2,4,128,768]{3,2,1,0:T(8,128)(2,1)S(1)} %pad_maximum_fusion.1), channel_id=1, source_target_pairs={{0,1},{1,0},{2,3},{3,2},{4,5},{5,4},{6,7},{7,6},{8,9},{9,8},{10,11... | collective-permute-start | bytes 4718600 | tf_op jit(solution)/shard_map/ppermute | solution.py:540
  384.8 6.9 %collective-permute-start.33 = (bf16[24,3840]{1,0:T(8,128)(2,1)S(1)}, bf16[24,3840]{1,0:T(8,128)(2,1)S(1)}, u32[]{:S(2)}, u32[]{:S(2)}) collective-permute-start(bf16[24,3840]{1,0:T(8,128)(2,1)S(1)} %fusion.43), channel_id=1, source_target_pairs={{0,2},{1,3},{2,0},{3,1},{4,6},{5,7},{6,4},{7,5},{8,10},{9,11},{10,... | collective-permute-start | bytes 552968 | tf_op jit(solution)/shard_map/ppermute | solution.py:540
  386.6 12.2 %collective-permute-start.23 = (bf16[2,2,2,24,1152]{4,3,2,1,0:T(8,128)(2,1)S(1)}, bf16[2,2,2,24,1152]{4,3,2,1,0:T(8,128)(2,1)S(1)}, u32[]{:S(2)}, u32[]{:S(2)}) collective-permute-start(bf16[2,2,2,24,1152]{4,3,2,1,0:T(8,128)(2,1)S(1)} %get-tuple-element.207), channel_id=1, source_target_pairs={{0,4},{4,0},{8,12},{12,8},{16,20},{20,16},{24,28},{28,24},{1,5},{5... | collective-permute-start | bytes 1327112 | tf_op jit(solution)/shard_map/ppermute | solution.py:540
  388.4 13.5 %collective-permute-start.28 = (bf16[2,2,2,24,1280]{4,3,0,2,1:T(8,128)(2,1)S(1)}, bf16[2,2,2,24,1280]{4,3,0,2,1:T(8,128)(2,1)S(1)}, u32[]{:S(2)}, u32[]{:S(2)}) collective-permute-start(bf16[2,2,2,24,1280]{4,3,0,2,1:T(8,128)(2,1)S(1)} %get-tuple-element.235), channel_id=1, source_target_pairs={{0,8},{4,12},{8,0},{12,4},{16,24},{20,28},{24,16},{28,20},{1,9},{5... | collective-permute-start | bytes 1474568 | tf_op jit(solution)/shard_map/ppermute | solution.py:540
  398.9 7.2 %collective-permute-start.24 = (bf16[2,2,24,1152]{3,2,1,0:T(8,128)(2,1)S(1)}, bf16[2,2,24,1152]{3,2,1,0:T(8,128)(2,1)S(1)}, u32[]{:S(2)}, u32[]{:S(2)}) collective-permute-start(bf16[2,2,24,1152]{3,2,1,0:T(8,128)(2,1)S(1)} %get-tuple-element.237), channel_id=1, source_target_pairs={{0,8},{4,12},{8,0},{12,4},{16,24},{20,28},{24,16},{28,20},{1,9},{5... | collective-permute-start | bytes 663560 | tf_op jit(solution)/shard_map/ppermute | solution.py:540
  402.1 7.1 %collective-permute-start.29 = (bf16[2,2,24,1280]{3,2,1,0:T(8,128)(2,1)S(1)}, bf16[2,2,24,1280]{3,2,1,0:T(8,128)(2,1)S(1)}, u32[]{:S(2)}, u32[]{:S(2)}) collective-permute-start(bf16[2,2,24,1280]{3,2,1,0:T(8,128)(2,1)S(1)} %copy.107), channel_id=1, source_target_pairs={{0,4},{4,0},{8,12},{12,8},{16,20},{20,16},{24,28},{28,24},{1,5},{5... | collective-permute-start | bytes 737288 | tf_op jit(solution)/shard_map/ppermute | solution.py:540
  406.1 7.1 %collective-permute-start.25 = (bf16[2,24,1152]{2,1,0:T(8,128)(2,1)S(1)}, bf16[2,24,1152]{2,1,0:T(8,128)(2,1)S(1)}, u32[]{:S(2)}, u32[]{:S(2)}) collective-permute-start(bf16[2,24,1152]{2,1,0:T(8,128)(2,1)S(1)} %get-tuple-element.241), channel_id=1, source_target_pairs={{0,16},{4,20},{8,24},{12,28},{16,0},{20,4},{24,8},{28,12},{1,17},{... | collective-permute-start | bytes 331784 | tf_op jit(solution)/shard_map/ppermute | solution.py:540
  409.2 4.9 %collective-permute-start.30 = (bf16[2,24,1280]{2,1,0:T(8,128)(2,1)S(1)}, bf16[2,24,1280]{2,1,0:T(8,128)(2,1)S(1)}, u32[]{:S(2)}, u32[]{:S(2)}) collective-permute-start(bf16[2,24,1280]{2,1,0:T(8,128)(2,1)S(1)} %get-tuple-element.239), channel_id=1, source_target_pairs={{0,2},{1,3},{2,0},{3,1},{4,6},{5,7},{6,4},{7,5},{8,10},{9,11},{10,... | collective-permute-start | bytes 368648 | tf_op jit(solution)/shard_map/ppermute | solution.py:540
  413.2 4.2 collective-permute-start.26
  414.2 5.8 %collective-permute-start.31 = (bf16[24,1280]{1,0:T(8,128)(2,1)S(1)}, bf16[24,1280]{1,0:T(8,128)(2,1)S(1)}, u32[]{:S(2)}, u32[]{:S(2)}) collective-permute-start(bf16[24,1280]{1,0:T(8,128)(2,1)S(1)} %fusion.53), channel_id=1, source_target_pairs={{0,16},{4,20},{8,24},{12,28},{16,0},{20,4},{24,8},{28,12},{1,17},{... | collective-permute-start | bytes 184328 | tf_op jit(solution)/shard_map/ppermute | solution.py:540
  (40 other events, 134.7 us)

commit v3 on v2

--- a/solution.py
+++ b/solution.py
@@ -19,11 +19,11 @@
 NT = (((1,), (1,)), ((), ()))
 TN = (((0,), (0,)), ((), ()))
 MIB = 2**20
-VMEM = 48 * MIB
-ATTEND_VMEM = 40 * MIB
-FFN_VMEM = 48 * MIB
-BACK_VMEM = 48 * MIB
-ATTEND_BACK_VMEM = 40 * MIB
+VMEM = 32 * MIB
+ATTEND_VMEM = 32 * MIB
+FFN_VMEM = 44 * MIB
+BACK_VMEM = 44 * MIB
+ATTEND_BACK_VMEM = 32 * MIB
 WHOLE = pl.BlockSpec(memory_space=pltpu.VMEM)
 TICK = jax.ShapeDtypeStruct((1, 1), jnp.float32)
 TICK1 = pl.BlockSpec((1, 1), lambda i: (0, 0))
@@ -36,6 +36,10 @@
     return lax.dot_general(a, b, dims, preferred_element_type=F32)
 
 
+def far(*arrays):
+    return [pltpu.with_memory_space_constraint(v, pltpu.HBM) for v in arrays]
+
+
 def whole(shape):
     return pl.BlockSpec(shape, lambda i: (0,) * len(shape), pipeline_mode=pl.Buffered(1))
 
@@ -49,7 +53,7 @@
 
 
 def shape_of(shape, dtype):
-    return jax.ShapeDtypeStruct(shape, dtype)
+    return pltpu.HBM(shape, dtype)
 
 
 def params(limit=VMEM):
@@ -164,8 +168,8 @@
     wt_ref, bt_ref, code_ref = rest[-3:]
     wt_ref[...] = w_ref[...].T
     bt_ref[...] = b_ref[...].T
-    R, heads, L = perm_ref.shape
-    group = code_ref.shape[2]
+    heads, _, L = perm_ref.shape
+    R, _, group = code_ref.shape[:3]
     me = me_ref[0]
     block = L // seq
     high = lax.broadcasted_iota(jnp.int32, (8, L), 0)
@@ -178,7 +182,7 @@
             turned = jnp.concatenate([blocks[i ^ (1 << bit)] for i in range(seq)], 1)
             seg = jnp.where(((me >> bit) & 1) == 1, turned, seg)
         for h in range(heads):
-            place = perm_ref[r, h : h + 1, :] ^ (me * block)
+            place = perm_ref[h, pl.ds(me * R + r, 1), :] ^ (me * block)
             a = jnp.where((place >> 7) == high, member, 0.0).astype(BF16)
             b = ((place & 127) == low).astype(BF16)
             table = mm(a, b, NT)
@@ -187,7 +191,7 @@
 
 
 def prepare(me, seq, w, b, perm, segs, group, deps):
-    rows, heads, L = perm.shape
+    heads, rows, L = perm.shape
     R = rows // seq
     D, D3 = w.shape
     full = lambda shape: pl.BlockSpec(shape, lambda i, me: (0,) * len(shape))
@@ -198,32 +202,19 @@
             num_scalar_prefetch=1,
             grid=(1,),
             in_specs=[
-                full((D, D3)), full((8, D3)), pl.BlockSpec((R, heads, L), lambda i, me: (me[0], 0, 0)),
+                full((D, D3)), full((8, D3)), full(perm.shape),
                 full(segs.shape),
             ] + [ANY] * len(deps),
             out_specs=[full((D3, D)), full((D3, 8)), full(codes)],
         ),
-        out_shape=[shape_of((D3, D), BF16), shape_of((D3, 8), F32), shape_of(codes, jnp.int32)],
+        out_shape=[
+            jax.ShapeDtypeStruct((D3, D), BF16), jax.ShapeDtypeStruct((D3, 8), F32),
+            jax.ShapeDtypeStruct(codes, jnp.int32),
+        ],
         compiler_params=params(32 * MIB),
         cost_estimate=cost(4e9, 8e6),
         name="prepare",
     )(me, w, b, perm, segs, *deps)
-
-
-def join_kernel(*refs):
-    refs[-1][...] = jnp.zeros_like(refs[-1])
-
-
-def join(*after):
-    return pl.pallas_call(
-        join_kernel,
-        in_specs=[ANY] * len(after),
-        out_specs=WHOLE,
-        out_shape=TICK,
-        compiler_params=params(4 * MIB),
-        cost_estimate=cost(1, 1),
-        name="join",
-    )(*after)
 
 
 def ffn_kernel(me_ref, *refs, nparts, nio):
@@ -289,26 +280,78 @@
         compiler_params=params(FFN_VMEM),
         cost_estimate=cost(4 * r * L * D * FF * 1.3, 4 * r * L * FF + 4 * D * FF),
         name="ffn",
-    )(me, *arrays_of(parts), first, wu, bu, wd, vec, *deps, *held)
-
-
-def down_grad_kernel(act_ref, g_ref, o_ref):
-    o_ref[...] = mm(act_ref[...], g_ref[...], TN).astype(BF16)
-
-
-def down_grad(act, g, tile):
+    )(me, *arrays_of(parts), *far(first), wu, bu, wd, vec, *deps, *held)
+
+
+def by_core(total, place):
+    rows, width = total.shape
+    bits = len(place) + 1
+    cube = total.reshape((2,) * bits + (rows >> bits, width))
+    cube = cube.transpose((bits - 1,) + tuple(place) + (bits, bits + 1))
+    return cube[0].reshape(rows // 2, width), cube[1].reshape(rows // 2, width)
+
+
+def put_halves(me_ref, total, place, send_ref, keep_ref):
+    even, odd = by_core(total, place)
+    mine = me_ref[0] % 2 == 0
+    send_ref[...] = jnp.where(mine, odd, even).astype(BF16)
+    keep_ref[...] = jnp.where(mine, even, odd).astype(BF16)
+
+
+def halves_of(me, total, place):
+    even, odd = by_core(total, place)
+    mine = me[0] % 2 == 0
+    return jnp.where(mine, odd, even), jnp.where(mine, even, odd)
+
+
+def places(dp, seq, order):
+    names = [("dp", b) for b in reversed(bits_of(dp))] + [("seq", b) for b in reversed(bits_of(seq))]
+    return [names.index(item) for item in order]
+
+
+def splits(rows, n):
+    return (rows // n) % 8 == 0
+
+
+def down_grad_kernel(me_ref, act_ref, g_ref, *rest, place, ndep):
+    outs = rest[ndep:]
+    total = mm(act_ref[...], g_ref[...], TN)
+    if len(outs) == 2:
+        put_halves(me_ref, total, place, *outs)
+    else:
+        outs[0][...] = total.astype(BF16)
+
+
+def down_grad(me, dp, seq, order, act, g, deps):
     T, FF = act.shape
     D = g.shape[1]
-    return pl.pallas_call(
-        down_grad_kernel,
-        grid=(FF // tile,),
-        in_specs=[pl.BlockSpec((T, tile), lambda i: (0, i)), whole((T, D))],
-        out_specs=rows_of(tile, D),
-        out_shape=shape_of((FF, D), BF16),
+    n = dp * seq
+    inside = splits(FF, n) and FF // dp % 128 == 0
+    steps = dp if inside else 8
+    tile = FF // steps
+    place = places(dp, seq, order)
+    inner = [p - len(bits_of(dp)) for p in place if p >= len(bits_of(dp))]
+    turns = [bit for name, bit in order if name == "dp"]
+
+    def at(i):
+        where = 0
+        for bit in turns:
+            where = 2 * where + ((i >> bit) & 1)
+        return (where, 0)
+
+    res = pl.pallas_call(
+        functools.partial(down_grad_kernel, place=inner, ndep=len(deps)),
+        grid=(steps,),
+        in_specs=[
+            pl.BlockSpec(memory_space=pltpu.SMEM), pl.BlockSpec((T, tile), lambda i: (0, i)), whole((T, D)),
+        ] + [ANY] * len(deps),
+        out_specs=[pl.BlockSpec((tile // 2, D), at)] * 2 if inside else [rows_of(tile, D)],
+        out_shape=[jax.ShapeDtypeStruct((FF // 2, D), BF16)] * 2 if inside else [shape_of((FF, D), BF16)],
         compiler_params=params(),
         cost_estimate=cost(2 * T * D * FF * 1.3, 2 * T * FF + 2 * D * FF),
         name="down_grad",
-    )(act, g)
+    )(me, *far(act, g), *deps)
+    return res if inside else halves_of(me, res[0], place)
 
 
 def ffn_back_kernel(
@@ -330,11 +373,13 @@
     gbr_ref[0] = gl
     da = mm(wo_ref[...], gl, NT)
     for h in range(heads):
-        il = il_ref[0, h : h + 1, :]
+        group = il_ref.shape[2]
+        i, j = h // group, h % group
+        il = il_ref[0, i, j : j + 1, :]
         piece = da[h * hs : (h + 1) * hs, :] * il
         do_ref[0, h * hs : (h + 1) * hs, :] = piece.astype(BF16)
         att = att_ref[0, h * hs : (h + 1) * hs, :].astype(F32)
-        de_ref[0, h : h + 1, :] = jnp.sum(piece * att, axis=0, keepdims=True)
+        de_ref[0, i, j : j + 1, :] = jnp.sum(piece * att, axis=0, keepdims=True)
 
     @pl.when(pl.program_id(0) == 0)
     def _():
@@ -359,71 +404,71 @@
         grid=(r,),
         in_specs=[
             flat(D), flat(FF), WHOLE, WHOLE, WHOLE, here((L, D)), here((L, 128)), WHOLE,
-            here((D, L)), here((heads, L)),
+            here((D, L)), here(il.shape[1:]),
         ] + [ANY] * len(extra),
         out_specs=[
-            flat(FF), here((L, D)), here((D, L)), here((heads, L)),
+            flat(FF), here((L, D)), here((D, L)), here(il.shape[1:]),
             pl.BlockSpec((8, D), lambda i: (0, 0)), pl.BlockSpec((8, FF), lambda i: (0, 0)),
             TICK1,
         ],
         out_shape=[
             shape_of((T, FF), BF16), shape_of((R, L, D), BF16), shape_of((R, D, L), BF16),
-            shape_of((R, heads, L), F32), shape_of((8, D), F32), shape_of((8, FF), F32),
+            shape_of(il.shape, F32), shape_of((8, D), F32), shape_of((8, FF), F32),
             TICK,
         ],
         input_output_aliases={10 + len(deps) + i: i for i in range(len(held))},
         compiler_params=params(BACK_VMEM),
         cost_estimate=cost(4 * r * L * D * FF * 1.5, 4 * r * L * FF + 4 * D * FF),
         name="ffn_back",
-    )(g, slope, wu, wd, wo, n1, s1, vec, att, il, *extra)
-
-
-def up_grad_kernel(x_ref, g_ref, *rest):
-    o_ref, tick_ref = rest[-2:]
+    )(*far(g, slope), wu, wd, wo, *far(n1, s1), vec, *far(att, il), *extra)
+
+
+def up_out_grad_kernel(me_ref, x_ref, g_ref, att_ref, gbr_ref, *rest, place, ndep):
+    outs, tick_ref = rest[ndep:-1], rest[-1]
     tick_ref[...] = jnp.zeros_like(tick_ref)
-    o_ref[...] = mm(x_ref[...], g_ref[...], TN).astype(BF16)
-
-
-def up_grad(x, g, tile, deps):
+    last = pl.num_programs(0) - 1
+
+    def put(total):
+        if len(outs) == 2:
+            put_halves(me_ref, total, place, *outs)
+        else:
+            outs[0][...] = total.astype(BF16)
+
+    @pl.when(pl.program_id(0) < last)
+    def _():
+        put(mm(x_ref[...], g_ref[...], TN))
+
+    @pl.when(pl.program_id(0) == last)
+    def _():
+        total = mm(att_ref[0], gbr_ref[0])
+        for r in range(1, att_ref.shape[0]):
+            total = total + mm(att_ref[r], gbr_ref[r])
+        put(total)
+
+
+def up_out_grad(me, dp, seq, order, x, g, att, gbr, deps):
     T, D = x.shape
     FF = g.shape[1]
-    return pl.pallas_call(
-        up_grad_kernel,
-        grid=(FF // tile,),
-        in_specs=[whole((T, D)), pl.BlockSpec((T, tile), lambda i: (0, i))] + [ANY] * len(deps),
-        out_specs=[pl.BlockSpec((D, tile), lambda i: (0, i)), TICK1],
-        out_shape=[shape_of((D, FF + D), BF16), TICK],
+    R, _, L = att.shape
+    place = places(dp, seq, order)
+    inside = splits(D, dp * seq)
+    rows, count = (D // 2, 2) if inside else (D, 1)
+    steps = FF // D
+    *res, tick = pl.pallas_call(
+        functools.partial(up_out_grad_kernel, place=place, ndep=len(deps)),
+        grid=(steps + 1,),
+        in_specs=[
+            pl.BlockSpec(memory_space=pltpu.SMEM), whole((T, D)),
+            pl.BlockSpec((T, D), lambda i: (0, jnp.minimum(i, steps - 1))), whole((R, D, L)),
+            whole((R, L, D)),
+        ] + [ANY] * len(deps),
+        out_specs=[pl.BlockSpec((rows, D), lambda i: (0, i))] * count + [TICK1],
+        out_shape=[jax.ShapeDtypeStruct((rows, FF + D), BF16)] * count + [TICK],
         compiler_params=params(),
-        cost_estimate=cost(2 * T * D * FF * 1.3, 2 * T * FF + 2 * D * FF),
-        name="up_grad",
-    )(x, g, *deps)
-
-
-def out_grad_kernel(att_ref, g_ref, *rest):
-    o_ref, tick_ref = rest[-2:]
-    tick_ref[...] = jnp.zeros_like(tick_ref)
-    total = mm(att_ref[0], g_ref[0])
-    for r in range(1, att_ref.shape[0]):
-        total = total + mm(att_ref[r], g_ref[r])
-    o_ref[...] = total.astype(BF16)
-
-
-def out_grad(att, g, deps, held):
-    R, D, L = att.shape
-    tile = D // 3
-    last = held.shape[1] // D - 1
-    return pl.pallas_call(
-        out_grad_kernel,
-        grid=(3,),
-        in_specs=[pl.BlockSpec((R, tile, L), lambda i: (0, i, 0)), whole((R, L, D))]
-        + [ANY] * (len(deps) + 1),
-        out_specs=[pl.BlockSpec((tile, D), lambda i: (i, last)), TICK1],
-        out_shape=[shape_of(held.shape, BF16), TICK],
-        input_output_aliases={2 + len(deps): 0},
-        compiler_params=params(),
-        cost_estimate=cost(2 * R * L * D * D * 1.3, 4 * R * L * D),
-        name="out_grad",
-    )(att, g, *deps, held)
+        cost_estimate=cost(2 * T * D * (FF + D) * 1.3, 2 * T * FF + 2 * D * FF),
+        name="up_out_grad",
+    )(me, *far(x, g, att, gbr), *deps)
+    return (res if inside else halves_of(me, res[0], place)), tick
 
 
 def attend_back_kernel(
@@ -492,44 +537,102 @@
         compiler_params=params(ATTEND_BACK_VMEM),
         cost_estimate=cost(r * (6 * L * D * D + 4 * 8 * heads * L * L * hs), r * 2 * heads * L * L),
         name="attend_back",
-    )(qkv, p, do, de, gone, wt, *extra)
-
-
-def qkv_grad_kernel(x_ref, g_ref, *rest):
-    o_refs, tick_ref = rest[-3:-1], rest[-1]
-    tick_ref[...] = jnp.zeros_like(tick_ref)
-    total = mm(x_ref[0], g_ref[0], (((0,), (1,)), ((), ())))
-    for r in range(1, x_ref.shape[0]):
-        total = total + mm(x_ref[r], g_ref[r], (((0,), (1,)), ((), ())))
-    half = pl.num_programs(0) // 2
-
-    @pl.when(pl.program_id(0) < half)
+    )(*far(qkv, p, do, de, gone), wt, *extra)
+
+
+def pack(sums, n, lanes):
+    total, at = jnp.zeros((n, lanes), F32), 0
+    for terms in sums:
+        v = functools.reduce(jnp.add, terms)
+        W = v.shape[1]
+        width = W // n
+        owner = lax.broadcasted_iota(jnp.int32, (n, W), 0)
+        place = lax.broadcasted_iota(jnp.int32, (n, W), 1)
+        a = jnp.where((place >= owner * width) & (place < (owner + 1) * width), v, 0.0).astype(BF16)
+        index = lax.broadcasted_iota(jnp.int32, (W, lanes), 0)
+        start = ((index.astype(F32) + 0.5) * (1.0 / width)).astype(jnp.int32) * width
+        b = (lax.broadcasted_iota(jnp.int32, (W, lanes), 1) == index - start + at).astype(BF16)
+        total = total + mm(a, b)
+        at += width
+    return total
+
+
+def qkv_grad_kernel(me_ref, x_ref, g_ref, *rest, spans, nsum, ndep, n, count, first, place):
+    sums_refs, outs, pack_ref = rest[:nsum], rest[nsum + ndep : -2], rest[-1]
+    rest[-2][...] = jnp.zeros_like(rest[-2])
+    step, steps = pl.program_id(0), pl.num_programs(0)
+
+    def put(total, which):
+        refs = outs[which * count : (which + 1) * count]
+        if count == 2:
+            put_halves(me_ref, total, place[which], *refs)
+        else:
+            refs[0][...] = total.astype(BF16)
+
+    @pl.when(step == 0)
     def _():
-        o_refs[0][...] = total.astype(BF16)
-
-    @pl.when(pl.program_id(0) >= half)
+        sums = [
+            [jnp.concatenate([sums_refs[i][row : row + 1, lo:hi] for lo, hi in cols], 1) for i in terms]
+            for terms, row, cols in spans
+        ]
+        pack_ref[...] = pack(sums, n, pack_ref.shape[1])
+
+    @pl.when(step < steps - 1)
     def _():
-        o_refs[1][...] = total.astype(BF16)
-
-
-def qkv_grad(x, g, deps):
+        total = mm(x_ref[0], g_ref[0], (((0,), (1,)), ((), ())))
+        for r in range(1, x_ref.shape[0]):
+            total = total + mm(x_ref[r], g_ref[r], (((0,), (1,)), ((), ())))
+
+        @pl.when(step < first)
+        def _():
+            put(total, 0)
+
+        @pl.when(step >= first)
+        def _():
+            put(total, 1)
+
+    @pl.when(step == steps - 1)
+    def _():
+        D = x_ref.shape[2]
+        lanes = pack_ref.shape[1]
+        row = lax.broadcasted_iota(jnp.int32, (n, D // n, lanes), 1)
+        total = jnp.where(row == 0, pack_ref[...][:, None, :], 0.0)
+        put(total.reshape(D, lanes), 1)
+
+
+def qkv_grad(me, dp, seq, orders, x, g, sums, spans, deps):
     R, L, D = x.shape
     D3 = g.shape[1]
-    tile = 384
-    half = D3 // 2 // tile
-    return pl.pallas_call(
-        qkv_grad_kernel,
-        grid=(2 * half,),
-        in_specs=[whole((R, L, D)), pl.BlockSpec((R, tile, L), lambda i: (0, i, 0))] + [ANY] * len(deps),
-        out_specs=[
-            pl.BlockSpec((D, tile), lambda i: (0, jnp.minimum(i, half - 1))),
-            pl.BlockSpec((D, tile), lambda i: (0, jnp.maximum(i - half, 0))), TICK1,
-        ],
-        out_shape=[shape_of((D, D3 // 2), BF16), shape_of((D, D3 // 2), BF16), TICK],
+    n = dp * seq
+    place = [places(dp, seq, order) for order in orders]
+    tile = D // 2
+    real = D3 // tile
+    first = (real + 2) // 2
+    inside = splits(D, n)
+    rows, count = (D // 2, 2) if inside else (D, 1)
+    widths = (first * tile, (real + 1 - first) * tile)
+    *res, tick = pl.pallas_call(
+        functools.partial(
+            qkv_grad_kernel, spans=spans, nsum=len(sums), ndep=len(deps), n=n, count=count,
+            first=first, place=place,
+        ),
+        grid=(real + 1,),
+        in_specs=[
+            pl.BlockSpec(memory_space=pltpu.SMEM), whole((R, L, D)),
+            pl.BlockSpec((R, tile, L), lambda i: (0, jnp.minimum(i, real - 1), 0)),
+        ] + [whole(v.shape) for v in sums] + [ANY] * len(deps),
+        out_specs=[pl.BlockSpec((rows, tile), lambda i: (0, jnp.minimum(i, first - 1)))] * count
+        + [pl.BlockSpec((rows, tile), lambda i: (0, jnp.maximum(i - first, 0)))] * count + [TICK1],
+        out_shape=[
+            jax.ShapeDtypeStruct((rows, width), BF16) for width in widths for _ in range(count)
+        ] + [TICK],
+        scratch_shapes=[pltpu.VMEM((n, tile), F32)],
         compiler_params=params(),
         cost_estimate=cost(2 * R * L * D * D3 * 1.3, 2 * R * L * (D + D3)),
         name="qkv_grad",
-    )(x, g, *deps)
+    )(me, *far(x, g), *sums, *deps)
+    pieces = [res[:count], res[count:]]
+    return [piece if inside else halves_of(me, piece[0], at) for piece, at in zip(pieces, place)], tick
 
 
 def bits_of(size):
@@ -550,46 +653,83 @@
 
 def late(x, tick):
     return x if tick is None else x + tick.reshape(()).astype(x.dtype)
+
+
+def move_kernel(me_ref, *refs, count, ndep, copies):
+    srcs, outs, sems = refs[:count], refs[count + ndep : -1], refs[-1]
+    me = me_ref[0]
+    started = []
+    for i, (src, at, out, to) in enumerate(copies):
+        copy = pltpu.make_async_copy(srcs[src].at[at(me)], outs[out].at[to(me)], sems.at[i])
+        copy.start()
+        started.append(copy)
+    for copy in started:
+        copy.wait()
+
+
+def move(me, srcs, shapes, copies, deps=()):
+    return pl.pallas_call(
+        functools.partial(move_kernel, count=len(srcs), ndep=len(deps), copies=copies),
+        in_specs=[pl.BlockSpec(memory_space=pltpu.SMEM)] + [ANY] * (len(srcs) + len(deps)),
+        out_specs=[ANY] * len(shapes),
+        out_shape=[jax.ShapeDtypeStruct(shape, BF16) for shape in shapes],
+        scratch_shapes=[pltpu.SemaphoreType.DMA((len(copies),))],
+        compiler_params=params(4 * MIB),
+        cost_estimate=cost(1, 1),
+        name="move",
+    )(me, *srcs, *deps)
 
 
 class Rows:
     def __init__(self, x, axis, size):
         self.x, self.axis, self.size = x, axis, size
         self.bits = bits_of(size)
-        self.R = x.shape[0] // size
+        self.R, self.B, self.D = x.shape[0] // size, x.shape[1], x.shape[2]
         self.came = [[] for _ in self.bits]
-        self.sent = []
-
-    def own(self, bit, start, stop):
-        cut = self.x.reshape((2,) * len(self.bits) + (self.R,) + self.x.shape[1:])[..., start:stop, :, :]
-        held = [cut]
-        for done in range(bit):
-            mine = my_bit(self.axis, done)
-            held = [pick(v, mine, v.ndim - 4) for v in held]
-            got, base = self.find(done, start)
-            held.append(got[..., start - base : stop - base, :, :])
-        return held
 
     def find(self, bit, start):
         return [(v, base) for v, base in self.came[bit] if base <= start][-1]
 
-    def come(self, bit, start, stop):
-        held = self.own(bit, start, stop)
-        mine = my_bit(self.axis, bit)
-        send = [pick(v, 1 - mine, v.ndim - 4) for v in held]
-        send = send[0] if len(send) == 1 else jnp.concatenate(send, -2)
+    def plan(self, bit, start, stop, srcs, copies, out):
+        r, B, R = stop - start, self.B, self.R
+        lead = 1 << (len(self.bits) - 1 - bit)
+        for high in range(lead):
+            def owner(me, high=high):
+                return (high << (bit + 1)) + (me ^ (1 << bit)) % (1 << (bit + 1))
+
+            def own(me, owner=owner):
+                return (pl.ds(owner(me) * R + start, r),)
+
+            def place(lo, hi, high=high):
+                return lambda me: (high, slice(None), pl.ds(lo, hi - lo))
+
+            copies.append((len(srcs), own, out, place(0, B)))
+            for done in range(bit):
+                got, base = self.find(done, start)
+
+                def theirs(me, owner=owner, done=done, base=base):
+                    return (owner(me) >> (done + 1), pl.ds(start - base, r))
+
+                copies.append((len(srcs) + 1 + done, theirs, out, place(B << done, B << (done + 1))))
+        srcs.append(self.x)
+        srcs.extend(self.find(done, start)[0] for done in range(bit))
+        return (lead, r, B << bit, self.D)
+
+    def send(self, bit, start, send):
         self.came[bit].append((flip(send, self.axis, self.size, bit), start))
-        return send
-
-    def all_high(self, start, stop):
-        return [self.come(bit, start, stop) for bit in self.bits[1:]]
 
     def parts(self, start):
-        out = [self.x]
-        for bit in self.bits:
-            got, base = self.find(bit, start)
-            out.append((got.reshape((-1,) + got.shape[-3:]), base))
-        return out
+        return [self.x] + [self.find(bit, start) for bit in self.bits]
+
+
+def exchange(me, jobs, deps=()):
+    srcs, copies, shapes = [], [], []
+    for out, (rows, bit, start, stop) in enumerate(jobs):
+        shapes.append(rows.plan(bit, start, stop, srcs, copies, out))
+    sends = move(me, srcs, shapes, copies, deps)
+    for (rows, bit, start, stop), send in zip(jobs, sends):
+        rows.send(bit, start, send)
+    return sends
 
 
 class Blocks:
@@ -599,60 +739,123 @@
     def send(self, lo, hi):
         self.chunks.append((lo, flip(hi, self.axis, self.size, bits_of(self.size)[-1])))
 
+    def turn(self, me, tick):
+        bits, axis, size = bits_of(self.size), self.axis, self.size
+        half, D = self.chunks[0][0].shape[1:]
+        self.R = R = sum(lo.shape[0] for lo, _ in self.chunks)
+        self.pieces = pieces = {0: [], 1 << bits[-1]: []}
+        at = 0
+        for chunk in self.chunks:
+            for name, v in zip(pieces, chunk):
+                pieces[name].append((v, (), at, v.shape[0], 0))
+            at += chunk[0].shape[0]
+        for bit in reversed(bits[:-1]):
+            half //= 2
+            names = list(pieces)
+            join = lambda vs: vs[0] if len(vs) == 1 else jnp.concatenate(vs, 0)
+            send = jnp.stack([
+                join([v[front + (slice(None), slice(token + half, token + 2 * half))] for v, front, _, _, token in pieces[name]])
+                for name in names
+            ], 0)
+            send = late(send, tick)
+            self.came = flip(send, axis, size, bit)
+            for i, name in enumerate(names):
+                pieces[name | (1 << bit)] = [(self.came, (i,), 0, R, 0)]
+        self.shape = (size * R, half, D)
+
+    def result(self, tick):
+        half = self.shape[1]
+        me = lax.axis_index(self.axis)
+        out = jnp.zeros(self.shape, BF16)
+        for name, sources in self.pieces.items():
+            for v, front, row, rows, token in sources:
+                piece = v[front + (slice(None), slice(token, token + half))]
+                out = lax.dynamic_update_slice_in_dim(out, late(piece, tick), (me ^ name) * self.R + row, 0)
+        return out
+
+
+class Sum:
+    def __init__(self, halves, dp, seq, order):
+        self.sizes = {"dp": dp, "seq": seq}
+        self.order = list(order)
+        self.send, self.keep = halves
+
+    def begin(self, send=None):
+        self.go("seq", 0, [self.send if send is None else send])
+
+    def go(self, name, bit, sends):
+        self.came = [flip(v, name, self.sizes[name], bit) for v in sends]
+
     def result(self, tick=None):
-        bits = bits_of(self.size)
-        axis, size = self.axis, self.size
-        join = lambda vs: jnp.concatenate(vs, 0) if len(vs) > 1 else vs[0]
-        pieces = {0: join([lo for lo, _ in self.chunks]), 1 << bits[-1]: late(join([hi for _, hi in self.chunks]), tick)}
-        for bit in reversed(bits[:-1]):
-            names = list(pieces)
-            half = pieces[0].shape[1] // 2
-            came = flip(jnp.stack([pieces[name][:, half:] for name in names], 0), axis, size, bit)
-            for i, name in enumerate(names):
-                pieces[name | (1 << bit)] = came[i]
-                pieces[name] = pieces[name][:, :half]
-        R, B, D = pieces[0].shape
-        me = lax.axis_index(axis)
-        out = jnp.zeros((size * R, B, D), BF16)
-        for name, piece in pieces.items():
-            out = lax.dynamic_update_slice_in_dim(out, piece, (me ^ name) * R, 0)
-        return out
-
-
-class Sum:
-    def __init__(self, x, dp, seq, order):
-        self.sizes = {"dp": dp, "seq": seq}
-        self.left = [("dp", b) for b in reversed(bits_of(dp))] + [("seq", b) for b in reversed(bits_of(seq))]
-        self.order = list(order)
-        self.terms = [x.reshape((2,) * len(self.left) + (x.shape[0] // (dp * seq),) + x.shape[1:])]
-        self.came = []
-
-    def total(self, terms, tick):
-        if len(terms) == 1:
-            return terms[0]
-        sum_ = terms[0].astype(F32) + terms[1].astype(F32)
-        return (sum_ if tick is None else sum_ + tick.reshape(())).astype(BF16)
-
-    def step(self, tick=None, split=1):
-        name, bit = self.order.pop(0)
-        axis = self.left.index((name, bit))
-        self.left.pop(axis)
-        mine = my_bit(name, bit)
-        terms = self.terms
-        if self.came:
-            terms = terms + [self.came[0] if len(self.came) == 1 else jnp.concatenate(self.came, -1)]
-        send = self.total([pick(term, 1 - mine, axis) for term in terms], tick)
-        self.terms = [self.total([pick(term, mine, axis) for term in terms], tick)]
-        width = send.shape[-1] // split
-        sends = [send[..., i * width : (i + 1) * width] for i in range(split)] if split > 1 else [send]
-        self.came = [flip(v, name, self.sizes[name], bit) for v in sends]
-        return sends
-
-    def result(self, tick=None):
-        while self.order:
-            self.step(tick)
-        out = self.terms[0].astype(F32) + self.came[0].astype(F32)
-        return out if tick is None else out + tick.reshape(())
+        came = self.came[0] if len(self.came) == 1 else jnp.concatenate(self.came, -1)
+        return late(self.keep.astype(F32) + came.astype(F32), tick)
+
+
+def fold_kernel(me_ref, *refs, shapes, ndep, nthrough):
+    nin = sum(2 + 2 * took for took, _ in shapes)
+    ins, outs = refs[:nin], refs[nin + ndep + nthrough : len(refs) - nthrough]
+    outs[-1][...] = jnp.zeros_like(outs[-1])
+    for took, gave in shapes:
+        keep, came, ins = ins[:2], (ins[2 : 2 + took], ins[2 + took : 2 + 2 * took]), ins[2 + 2 * took :]
+        send_refs, keep_ref, outs = outs[:gave], outs[gave], outs[gave + 1 :]
+        sums = []
+        for base, parts in zip(keep, came):
+            part = jnp.concatenate([ref[0] for ref in parts], 1) if took > 1 else parts[0][0]
+            sums.append((base[0].astype(F32) + part.astype(F32)).astype(BF16))
+        width = sums[0].shape[1] // gave
+        for i, ref in enumerate(send_refs):
+            ref[...] = sums[0][:, i * width : (i + 1) * width]
+        keep_ref[...] = sums[1]
+
+
+def fold(me, chains, deps=(), split=1, through=()):
+    items = [chain.order.pop(0) for chain in chains]
+    rows = [chain.keep.shape[0] // 2 for chain in chains]
+    steps = max(s for s in (4, 2, 1) if s == 1 or all(r % (16 * s) == 0 for r in rows))
+    ins, in_specs, out_specs, out_shape, shapes = [], [], [], [], []
+    for chain, (name, bit), r in zip(chains, items, rows):
+        tile, width = r // steps, chain.keep.shape[1]
+        row = 0 if name == "dp" else 1
+        gave = split if chain is chains[-1] else 1
+
+        def half(other, width, row=row, bit=bit, tile=tile):
+            return pl.BlockSpec(
+                (1, tile, width), lambda i, me: (((me[row] >> bit) & 1) ^ other, i, 0)
+            )
+
+        view = lambda v, r=r: v.reshape(2, r, v.shape[1])
+        ins += [view(chain.keep)] * 2 + [view(v) for v in chain.came] * 2
+        in_specs += [half(1, width), half(0, width)]
+        in_specs += [half(other, v.shape[1]) for other in (1, 0) for v in chain.came]
+        out_specs += [pl.BlockSpec((tile, width // gave), lambda i, me: (i, 0))] * gave
+        out_specs += [pl.BlockSpec((tile, width), lambda i, me: (i, 0))]
+        out_shape += [jax.ShapeDtypeStruct((r, width // gave), BF16)] * gave
+        out_shape += [jax.ShapeDtypeStruct((r, width), BF16)]
+        shapes.append((len(chain.came), gave))
+    res = pl.pallas_call(
+        functools.partial(fold_kernel, shapes=shapes, ndep=len(deps), nthrough=len(through)),
+        grid_spec=pltpu.PrefetchScalarGridSpec(
+            num_scalar_prefetch=1,
+            grid=(steps,),
+            in_specs=in_specs + [ANY] * (len(deps) + len(through)),
+            out_specs=out_specs + [pl.BlockSpec((1, 1), lambda i, me: (0, 0))] + [ANY] * len(through),
+        ),
+        out_shape=out_shape + [TICK] + [jax.ShapeDtypeStruct(v.shape, v.dtype) for v in through],
+        input_output_aliases={
+            1 + len(ins) + len(deps) + i: len(out_shape) + 1 + i for i in range(len(through))
+        },
+        compiler_params=params(16 * MIB),
+        cost_estimate=cost(1, 1),
+        name="fold",
+    )(me, *ins, *deps, *through)
+    tick, on = res[len(out_shape)], res[len(out_shape) + 1 :]
+    sends = []
+    for chain, (name, bit), (_, gave) in zip(chains, items, shapes):
+        chain.go(name, bit, res[:gave])
+        chain.keep = res[gave]
+        sends += res[:gave]
+        res = res[gave + 1 :]
+    return (sends, tick, on) if through else (sends, tick)
 
 
 def chunks_of(count, sizes):
@@ -680,39 +883,43 @@
     scale = 1.0 / math.sqrt(hs)
     mine = lax.axis_index("seq")
     me = mine.reshape(1).astype(jnp.int32)
+    both = jnp.stack([lax.axis_index("dp"), mine]).astype(jnp.int32)
 
     hidden, gout = Rows(hidden_in, "seq", seq), Rows(grad_out, "seq", seq)
     halves = chunks_of(R, (R // 2,))
-    hidden.come(0, 0, R)
-    sent = [hidden.all_high(row, row + 1) for row in range(R)]
-    gout_core = gout.come(0, 0, R)
-    gout_sent = [gout.all_high(*half) for half in halves]
+    bits = bits_of(seq)
+    exchange(me, [(hidden, 0, 0, 1)])
+    for bit in bits[1:]:
+        first_sent = exchange(me, [(hidden, bit, 0, 1)])
+    rest = [(hidden, 0, 1, R)] if R > 1 else []
+    exchange(me, rest + [(gout, 0, 0, R)], first_sent)
 
     bias = jnp.concatenate([bias_qv[:D], jnp.zeros((D,), F32), bias_qv[D:]])
     bias = jnp.broadcast_to(bias, (8, 3 * D))
     none = jnp.zeros((D,), F32)
     vec = jnp.stack([bias_out, gain_attn, shift_attn, bias_down, gain_ffn, shift_ffn, none, none])
-    wt, bt, code = prepare(me, seq, w_qkv, bias, cluster_perm, segment_ids, group, sent[0])
-
-    held = ()
+    wt, bt, code = prepare(me, seq, w_qkv, bias, cluster_perm.transpose(1, 0, 2), segment_ids, group, first_sent)
+
+    held, tick = (), None
     for row in range(R):
-        deps = sent[row + 1] if row + 1 < R else []
-        if row == min(1, R - 1):
-            deps = deps + [gout_core]
-        if row >= R - 2:
-            deps = deps + gout_sent[min(row - R + 2, len(halves) - 1)]
+        jobs = [(hidden, row + 1, row + 2)] if row + 1 < R else [(gout, *halves[0])]
+        deps = first_sent if tick is None else [tick]
+        for bit in bits[1:]:
+            deps = exchange(me, [(rows, bit, start, stop) for rows, start, stop in jobs], deps)
         *held, tick = attend(
             me, hidden.parts(row), row, 1, R, code, wt, bt, w_out, vec, heads, hs, scale, group, deps, held
         )
     x, qkv, p, il, att, first, n1, s1 = held
-    il = il.reshape(R, heads, L)
     first = first.reshape(T, D)
 
     held, out_blocks, sums_ffn = (), Blocks("seq", seq), []
-    for start, stop in halves:
+    for i, (start, stop) in enumerate(halves):
+        deps = [tick]
+        for bit in bits[1:] if i + 1 < len(halves) else []:
+            deps = exchange(me, [(gout, bit, *halves[i + 1])], deps)
         lo, hi, *held, sums, tick = ffn(
             me, first, gout.parts(start), start, stop - start, R, w_up, bias_up.reshape(1, -1), w_down,
-            vec, [], held,
+            vec, deps, held,
         )
         out_blocks.send(lo, hi)
         sums_ffn.append(sums)
@@ -720,44 +927,37 @@
 
     low = [("dp", b) for b in bits_of(dp)]
     high = [("seq", b) for b in bits_of(seq)[1:]]
-    core = [("seq", 0)]
     turned = low[1:2] + low[:1] + high + low[2:]
 
-    d_down = down_grad(act, gffn, 512)
-    down = Sum(d_down, dp, seq, core + low + high)
-    tick, held, sums_attn, sums_up = None, (), [], []
+    n = dp * seq
+    came_out = [v for _, v in out_blocks.chunks]
+    down = Sum(down_grad(me, dp, seq, low + high, act, gffn, came_out[:1]), dp, seq, low + high)
+    down.begin()
+    held, sums_attn, sums_up, deps = (), [], [], []
     for i, (start, stop) in enumerate(halves):
-        deps = down.step(tick)
         *held, sums1, sums2, tick = ffn_back(
             start, stop - start, gffn, slope, w_up, w_down, w_out, n1, s1, vec, att, il, heads, hs,
             deps, held,
         )
-        tick = join(tick, *down.came)
         sums_attn.append(sums1)
         sums_up.append(sums2)
+        deps, _ = fold(both, [down], [tick] + (came_out[1:] if i == 0 else []))
     gpre, gbr, do, de = held
-    deps = down.step(tick)
-    d_up, tick = up_grad(first, gpre, 512, deps)
-    d_up, tick = out_grad(att, gbr, [], d_up)
-    up = Sum(d_up, dp, seq, core + low + high)
-    tick = join(tick, *down.came)
-    deps = down.step(tick) + up.step()
-    de = de.reshape(R, heads // group, group, L)
+    d_up, tick = up_out_grad(me, dp, seq, low + high, first, gpre, att, gbr, deps)
+    up = Sum(d_up, dp, seq, low + high)
+    deps, _, (send,) = fold(both, [down], [tick], 1, [up.send])
+    up.begin(send)
     g, in_blocks, sums_qkv = None, Blocks("seq", seq), []
     for start, stop in halves:
         lo = hi = None
         for row in range(start, stop):
             if row == 1:
-                tick = join(tick, *down.came, *up.came)
-                last = down.step(tick) if len(down.order) == 1 else []
-                sends = up.step(tick, 2)
-                deps = last + sends[:1]
+                sends, _ = fold(both, [down, up] if down.order else [up], [tick], 2)
+                deps = sends[:-1]
             elif row == 2:
-                tick = join(tick, *down.came, up.came[0])
-                deps = sends[1:]
+                deps = [sends[-1], up.came[0]]
             elif row == 3:
-                tick = join(tick, *up.came)
-                deps = up.step(tick)
+                deps, _ = fold(both, [up], [tick])
             elif row:
                 deps = []
             g, lo, hi, sums, tick = attend_back(
@@ -766,40 +966,49 @@
             )
             sums_qkv.append(sums)
         in_blocks.send(lo, hi)
-    if R > 3:
-        tick = join(tick, *up.came, *[came for _, came in in_blocks.chunks[:1]])
-    d_qkv0, d_qkv1, tick = qkv_grad(x, g, up.step(tick))
-    qkv0 = Sum(d_qkv0, dp, seq, core + low + high)
-
-    n = dp * seq
-    add = lambda vs: late(functools.reduce(jnp.add, vs), tick)
-    sums_qkv, sums_attn, sums_up, sums_ffn = add(sums_qkv), add(sums_attn), add(sums_up), add(sums_ffn)
-    small = [
-        jnp.concatenate([sums_qkv[0, :D], sums_qkv[0, 2 * D :]]),
-        sums_attn[0], sums_attn[1], sums_attn[2], sums_up[0], sums_ffn[0], sums_ffn[1], sums_ffn[2],
+    deps, _ = fold(both, [up], [tick, in_blocks.chunks[0][1]])
+
+    sums = sums_qkv + sums_attn + sums_up + sums_ffn
+    kinds = [sums_qkv, sums_attn, sums_up, sums_ffn]
+    firsts = [sum(len(v) for v in kinds[:i]) for i in range(4)]
+    span = lambda kind, row, *cols: (range(firsts[kind], firsts[kind] + len(kinds[kind])), row, cols)
+    spans = [
+        span(0, 0, (0, D), (2 * D, 3 * D)), span(1, 0, (0, D)), span(1, 1, (0, D)), span(1, 2, (0, D)),
+        span(2, 0, (0, FF)), span(3, 0, (0, D)), span(3, 1, (0, D)), span(3, 2, (0, D)),
     ]
-    per = [v.size // n for v in small]
-    packed = jnp.concatenate([v.reshape(n, -1) for v in small], -1)
-    lanes = 128 * -(-packed.shape[1] // (128 * (D // n)))
-    packed = jnp.pad(packed, ((0, 0), (0, lanes * (D // n) - packed.shape[1])))
-    packed = packed.reshape(D, lanes).astype(BF16)
-
-    qkv1 = Sum(jnp.concatenate([d_qkv1, packed], 1), dp, seq, core + turned)
-    while qkv0.order or qkv1.order or up.order:
-        for s in (qkv0, qkv1, up):
-            if s.order:
-                s.step()
-    grad_in = in_blocks.result(tick)
-    out_hidden = out_blocks.result(tick)
-    r_down, r_up, r_qkv0, r_qkv1 = down.result(tick), up.result(tick), qkv0.result(), qkv1.result()
-    vec = r_qkv1[:, 3 * D // 2 :].reshape(-1)
+    per = [sum(hi - lo for lo, hi in cols) // n for _, _, cols in spans]
+    (d_qkv0, d_qkv1), tick = qkv_grad(me, dp, seq, [low + high, turned], x, g, sums, spans, deps)
+    qkv0 = Sum(d_qkv0, dp, seq, low + high)
+    qkv1 = Sum(d_qkv1, dp, seq, turned)
+    while len(up.order) > 1:
+        _, tick = fold(both, [up], [tick])
+    _, tick, sends = fold(both, [up], [tick], 1, [qkv0.send, qkv1.send])
+    qkv0.begin(sends[0])
+    qkv1.begin(sends[1])
+    while down.order:
+        _, tick = fold(both, [down], [tick])
+    out_blocks.turn(me, tick)
+    stage = 0
+    while qkv0.order:
+        _, tick = fold(both, [qkv0, qkv1], [tick])
+        if stage == 0:
+            in_blocks.turn(me, tick)
+            out_hidden = out_blocks.result(tick)
+            r_down = down.result(tick)
+        if stage == 1:
+            grad_in = in_blocks.result(tick)
+            r_up = up.result(tick)
+        stage += 1
+    r_qkv0, r_qkv1 = qkv0.result(), qkv1.result()
+    split = 3 * D - r_qkv0.shape[1]
+    vec = r_qkv1[0, split:]
     cuts, at = [], 0
     for width in per:
         cuts.append(vec[at : at + width])
         at += width
     b_qv, b_out, g_attn, s_attn, b_up, b_down, g_ffn, s_ffn = cuts
     return (
-        out_hidden, grad_in, jnp.concatenate([r_qkv0, r_qkv1[:, : 3 * D // 2]], 1), b_qv,
+        out_hidden, grad_in, jnp.concatenate([r_qkv0, r_qkv1[:, :split]], 1), b_qv,
         r_up[:, FF:], b_out, g_attn, s_attn, r_up[:, :FF], b_up, r_down, b_down, g_ffn, s_ffn,
     )
 

time: 428 us -> 404 us (0.944)
  local copies, waits for them, and re-layouts: 53 us -> 24.6 us
  Pallas kernels: 270 us -> 296 us
  other arithmetic: 30.3 us -> 13.9 us
  waiting for transfers between devices: 31 us -> 21.2 us
    pallas_call x10 -> x22, Pallas kernels: 55.1 us -> 87.5 us  [the longest x11 25.8 us: fold(): pl.pallas_call(functools.partial(fold_kernel, shapes=shapes, ndep=len(dep...]
    squeeze x20 -> x0, local copies, waits for them, and re-layouts: 14.5 us -> none  [pick(): return lax.dynamic_index_in_dim(x, index, axis, keepdims=False)]
    convert_element_type x16 -> x0, other arithmetic: 13.7 us -> none  [total(): return (sum_ if tick is None else sum_ + tick.reshape(())).astype(BF16)]
    ppermute x35 -> x36, waiting for transfers between devices: 31 us -> 21.2 us  [flip(): return lax.ppermute(x, axis, [(i, i ^ 1 << bit) for i in range(size)])]
    another operation x13 -> x2, local copies, waits for them, and re-layouts: 6.62 us -> 0.61 us  [the longest x7 3.65 us: shards(): packed = jnp.concatenate([v.reshape(n, -1) for v in small], -1)]
    add x4 -> x2, other arithmetic: 4.88 us -> 0.03 us  [result(): return late(self.keep.astype(F32) + came.astype(F32), tick)]
    dynamic_update_slice x0 -> x4, other arithmetic: none -> 4.61 us  [result(): lax.dynamic_update_slice_in_dim(out, late(piece, tick), (me ^ name) * sel...]
    slice x9 -> x1, local copies, waits for them, and re-layouts: 4.33 us -> 0.01 us  [shards(): r_qkv1[:, :split]]
  transfers between devices with their start and end apart: 35 -> 36, of which waited for: 10 -> 13; matrix products, arithmetic and copies ran while one was open for 12% -> 5% of each run, Pallas kernels for 50% -> 67%
where the time goes in v3:
time: 404 us; the launch traced here: 396 us
  Pallas kernels  296 us (73%)
  starting transfers between devices  37.2 us (9%)
  local copies, waits for them, and re-layouts  24.6 us (6%)
  waiting for transfers between devices  21.2 us (5%)
  other arithmetic  13.9 us (3%)
    pallas_call x4, Pallas kernels, attend_back(): pl.pallas_call(functools.partial(attend_back_kernel, heads=heads, hs=hs,...  60.5 us
    pallas_call x4, Pallas kernels, attend(): pl.pallas_call(functools.partial(attend_kernel, nparts=np_, heads=heads,...  59.1 us
    pallas_call x2, Pallas kernels, ffn_back(): pl.pallas_call(functools.partial(ffn_back_kernel, heads=heads, hs=hs), gr...  45.7 us
    pallas_call x2, Pallas kernels, ffn(): pl.pallas_call(functools.partial(ffn_kernel, nparts=np_, nio=nio), grid_s...  41.3 us
    ppermute x36, starting transfers between devices, flip(): return lax.ppermute(x, axis, [(i, i ^ 1 << bit) for i in range(size)])  37.2 us
    pallas_call x11, Pallas kernels, fold(): pl.pallas_call(functools.partial(fold_kernel, shapes=shapes, ndep=len(dep...  25.8 us
    ppermute x36, waiting for transfers between devices, flip(): return lax.ppermute(x, axis, [(i, i ^ 1 << bit) for i in range(size)])  21.2 us
    unnamed x108, local copies, waits for them, and re-layouts  20.2 us
  transfers between devices with their start and end apart: 36, of which 13 were waited for; matrix products, arithmetic and copies ran while one was open for 5% of the time, Pallas kernels for 67%

profile of v3, /device:TPU:0, one launch (start us, length us, event | category | flops | bytes accessed | tf_op | source)
XLA Modules:
  0.0 396.5 jit_solution(11413202405477384676)
XLA Ops:
  0.7 1.9 copy-done
  7.9 2.6 collective-permute-start.3
  11.4 2.0 copy-done.27
  15.2 1.8 prepare.1
  20.5 14.6 %attend.4 = (bf16[4,512,768]{2,1,0:T(8,128)(2,1)}, bf16[4,2304,512]{2,1,0:T(8,128)(2,1)}, bf16[4,12,512,512]{3,2,1,0:T(8,128)(2,1)}, f32[4,3,4,512]{3,2,1,0:T(4,...) custom-call(s32[1]{0:T(128)} %bitcast.me_ref, ...), custom_call_target="tpu_custom_call" | custom-call | flops 5637144576 | bytes 6291456 | tf_op jit(solution)/shard_map/attend/pallas_call | solution.py:142
  35.1 1.9 move.12.refs_8_
  36.9 2.1 collective-permute-start.4
  39.0 14.8 %attend.5 = (bf16[4,512,768]{2,1,0:T(8,128)(2,1)}, bf16[4,2304,512]{2,1,0:T(8,128)(2,1)}, bf16[4,12,512,512]{3,2,1,0:T(8,128)(2,1)}, f32[4,3,4,512]{3,2,1,0:T(4,...) custom-call(s32[1]{0:T(128)} %bitcast.me_ref, ...), custom_call_target="tpu_custom_call", output_to_operand_aliasing={{0}: (10, {}), {1}: (11, {}), {2}: (12, {}), {3}: (13, {}),... | custom-call | flops 5637144576 | bytes 6291456 | tf_op jit(solution)/shard_map/attend/pallas_call | solution.py:142
  53.8 1.9 move.13.refs_8_
  55.8 14.7 %attend.6 = (bf16[4,512,768]{2,1,0:T(8,128)(2,1)}, bf16[4,2304,512]{2,1,0:T(8,128)(2,1)}, bf16[4,12,512,512]{3,2,1,0:T(8,128)(2,1)}, f32[4,3,4,512]{3,2,1,0:T(4,...) custom-call(s32[1]{0:T(128)} %bitcast.me_ref, ...), custom_call_target="tpu_custom_call", output_to_operand_aliasing={{0}: (10, {}), {1}: (11, {}), {2}: (12, {}), {3}: (13, {}),... | custom-call | flops 5637144576 | bytes 6291456 | tf_op jit(solution)/shard_map/attend/pallas_call | solution.py:142
  71.4 2.0 collective-permute-start.6
  73.5 15.0 %attend.7 = (bf16[4,512,768]{2,1,0:T(8,128)(2,1)}, bf16[4,2304,512]{2,1,0:T(8,128)(2,1)}, bf16[4,12,512,512]{3,2,1,0:T(8,128)(2,1)}, f32[4,3,4,512]{3,2,1,0:T(4,...) custom-call(s32[1]{0:T(128)} %bitcast.me_ref, ...), custom_call_target="tpu_custom_call", output_to_operand_aliasing={{0}: (10, {}), {1}: (11, {}), {2}: (12, {}), {3}: (13, {}),... | custom-call | flops 5637144576 | bytes 6291456 | tf_op jit(solution)/shard_map/attend/pallas_call | solution.py:142
  90.1 20.8 %ffn.2 = (bf16[2,256,768]{2,1,0:T(8,128)(2,1)}, bf16[2,256,768]{2,1,0:T(8,128)(2,1)}, bf16[2048,768]{1,0:T(8,128)(2,1)}, bf16[2048,3072]{1,0:T(8,128)(2,1)}, bf1...) custom-call(s32[1]{0:T(128)} %bitcast.me_ref, bf16[16,128,768]{2,1,0:T(8,128)(2,1)S(1)} %copy-done.3, ...), custom_call_target="tpu_custom_call" | custom-call | flops 12562779136 | bytes 22020096 | tf_op jit(solution)/shard_map/ffn/pallas_call | solution.py:261
  111.0 2.1 collective-permute-start.9
  113.1 2.3 copy-done.8
  115.5 20.5 %ffn.3 = (bf16[2,256,768]{2,1,0:T(8,128)(2,1)}, bf16[2,256,768]{2,1,0:T(8,128)(2,1)}, bf16[2048,768]{1,0:T(8,128)(2,1)}, bf16[2048,3072]{1,0:T(8,128)(2,1)}, bf1...) custom-call(s32[1]{0:T(128)} %bitcast.me_ref, ...), custom_call_target="tpu_custom_call", output_to_operand_aliasing={{2}: (10, {}), {3}: (11, {}), {4}: (12, {})} | custom-call | flops 12562779136 | bytes 22020096 | tf_op jit(solution)/shard_map/ffn/pallas_call | solution.py:261
  135.9 15.2 %down_grad.1 = (bf16[1536,768]{1,0:T(8,128)(2,1)}, bf16[1536,768]{1,0:T(8,128)(2,1)S(1)}) custom-call(s32[1]{0:T(128)} %bitcast.me_ref, bf16[2048,3072]{1,0:T(8,128)(2,1)} %get-tuple-element.199.act_ref, bf16[2048,768]{1,0:T(8,128)(2,1)} %get-tuple-element.193.g_ref, bf16[2,256,768]{2,1,0:T(8,128)(2,1)S(1)} %collective-permute-done.9.rest_0_), custom_call_target="tpu_custom_call" | custom-call | flops 12562779136 | bytes 17301504 | tf_op jit(solution)/shard_map/down_grad/pallas_call | solution.py:342
  154.0 2.3 copy-done.9
  157.1 22.8 %ffn_back.2 = (bf16[2048,3072]{1,0:T(8,128)(2,1)}, bf16[4,512,768]{2,1,0:T(8,128)(2,1)}, bf16[4,768,512]{2,1,0:T(8,128)(2,1)}, f32[4,3,4,512]{3,2,1,0:T(4,128)},...) custom-call(bf16[2048,768]{1,0:T(8,128)(2,1)} %get-tuple-element.193.g_ref, ...), custom_call_target="tpu_custom_call" | custom-call | flops 14495514624 | bytes 22020096 | tf_op jit(solution)/shard_map/ffn_back/pallas_call | solution.py:402
  179.9 4.3 %fold.11 = (bf16[768,768]{1,0:T(8,128)(2,1)S(1)}, bf16[768,768]{1,0:T(8,128)(2,1)S(1)}, f32[1,1]{1,0:T(1,128)}) custom-call(s32[2]{0:T(128)S(1)} %pad_add_fusion.me_ref, bf16[2,768,768]{2,1,0:T(8,128)(2,1)S(1)} %bitcast.85, bf16[2,768,768]{2,1,0:T(8,128)(2,1)S(1)} %bitcast.86, bf16[2,768,768]{2,1,0:T(8,128)(2,1)} %bitcast.6.refs_2_.refs_3_, ...), custom_call_target="tpu_custom_call" | custom-call | flops 1 | bytes 1 | tf_op jit(solution)/shard_map/fold/pallas_call | solution.py:835
  185.7 22.9 %ffn_back.3 = (bf16[2048,3072]{1,0:T(8,128)(2,1)}, bf16[4,512,768]{2,1,0:T(8,128)(2,1)}, bf16[4,768,512]{2,1,0:T(8,128)(2,1)}, f32[4,3,4,512]{3,2,1,0:T(4,128)},...) custom-call(bf16[2048,768]{1,0:T(8,128)(2,1)} %get-tuple-element.193, ...), custom_call_target="tpu_custom_call", output_to_operand_aliasing={{0}: (11, {}), {1}: (12, {}), {2}: (13, {}), {3}: (14, {})} | custom-call | flops 14495514624 | bytes 22020096 | tf_op jit(solution)/shard_map/ffn_back/pallas_call | solution.py:402
  208.6 4.0 %collective-permute-done.12 = bf16[768,768]{1,0:T(8,128)(2,1)S(1)} collective-permute-done((bf16[768,768]{1,0:T(8,128)(2,1)S(1)}, bf16[768,768]{1,0:T(8,128)(2,1)S(1)}, u32[]{:S(2)}, u32[]{:S(2)}) %collective-permute-start.12) | collective-permute-done | bytes 1179680 | tf_op jit(solution)/shard_map/ppermute | solution.py:643
  212.6 2.0 fold.12
  216.1 18.9 %up_out_grad.1 = (bf16[384,3840]{1,0:T(8,128)(2,1)S(1)}, bf16[384,3840]{1,0:T(8,128)(2,1)S(1)}, f32[1,1]{1,0:T(1,128)}) custom-call(s32[1]{0:T(128)} %bitcast.me_ref, bf16[2048,768]{1,0:T(8,128)(2,1)} %bitcast.148, bf16[2048,3072]{1,0:T(8,128)(2,1)} %get-tuple-element.217.g_ref, bf16[4,768,512]{2,1,0:T(8,128)(2,1)} %get-tuple-element.197.att_ref, ...), custom_call_target="tpu_custom_call" | custom-call | flops 15703474176 | bytes 17301504 | tf_op jit(solution)/shard_map/up_out_grad/pallas_call | solution.py:457
  235.1 1.9 fold.13
  236.9 2.6 collective-permute-start.14
  239.5 15.4 %attend_back.4 = (bf16[4,2304,512]{2,1,0:T(8,128)(2,1)}, bf16[2,256,768]{2,1,0:T(8,128)(2,1)}, bf16[2,256,768]{2,1,0:T(8,128)(2,1)}, f32[8,2304]{1,0:T(8,128)}, f32[1,1]{1,0:T(1,128)}) custom-call(bf16[4,2304,512]{2,1,0:T(8,128)(2,1)} %get-tuple-element.187.qkv_ref, bf16[4,12,512,512]{3,2,1,0:T(8,128)(2,1)} %get-tuple-element.188.p_ref, ...), custom_call_target="tpu_custom_call" | custom-call | flops 8254390272 | bytes 6291456 | tf_op jit(solution)/shard_map/attend_back/pallas_call | solution.py:520
  254.9 2.2 fold.14
  259.8 15.0 %attend_back.5 = (bf16[4,2304,512]{2,1,0:T(8,128)(2,1)}, bf16[2,256,768]{2,1,0:T(8,128)(2,1)}, bf16[2,256,768]{2,1,0:T(8,128)(2,1)}, f32[8,2304]{1,0:T(8,128)}, f32[1,1]{1,0:T(1,128)}) custom-call(bf16[4,2304,512]{2,1,0:T(8,128)(2,1)} %get-tuple-element.187.qkv_ref, ...), custom_call_target="tpu_custom_call", output_to_operand_aliasing={{0}: (8, {}), {1}: (9, {}), {2}: (10, {})} | custom-call | flops 8254390272 | bytes 6291456 | tf_op jit(solution)/shard_map/attend_back/pallas_call | solution.py:520
  274.8 1.8 collective-permute-start.19
  277.1 15.0 %attend_back.6 = (bf16[4,2304,512]{2,1,0:T(8,128)(2,1)}, bf16[2,256,768]{2,1,0:T(8,128)(2,1)}, bf16[2,256,768]{2,1,0:T(8,128)(2,1)}, f32[8,2304]{1,0:T(8,128)}, f32[1,1]{1,0:T(1,128)}) custom-call(bf16[4,2304,512]{2,1,0:T(8,128)(2,1)} %get-tuple-element.187.qkv_ref, ...), custom_call_target="tpu_custom_call", output_to_operand_aliasing={{0}: (8, {})} | custom-call | flops 8254390272 | bytes 6291456 | tf_op jit(solution)/shard_map/attend_back/pallas_call | solution.py:520
  292.3 2.0 fold.15
  294.7 15.2 %attend_back.7 = (bf16[4,2304,512]{2,1,0:T(8,128)(2,1)}, bf16[2,256,768]{2,1,0:T(8,128)(2,1)}, bf16[2,256,768]{2,1,0:T(8,128)(2,1)}, f32[8,2304]{1,0:T(8,128)}, f32[1,1]{1,0:T(1,128)}) custom-call(bf16[4,2304,512]{2,1,0:T(8,128)(2,1)} %get-tuple-element.187.qkv_ref, ...), custom_call_target="tpu_custom_call", output_to_operand_aliasing={{0}: (7, {}), {1}: (8, {}), {2}: (9, {})} | custom-call | flops 8254390272 | bytes 6291456 | tf_op jit(solution)/shard_map/attend_back/pallas_call | solution.py:520
  310.0 2.1 collective-permute-done.18
  314.2 17.8 %qkv_grad.1 = (bf16[384,1536]{1,0:T(8,128)(2,1)}, bf16[384,1536]{1,0:T(8,128)(2,1)S(1)}, bf16[384,1152]{1,0:T(8,128)(2,1)}, bf16[384,1152]{1,0:T(8,128)(2,1)S(1)}, f32[1,1]{1,0:T(1,128)}) custom-call(s32[1]{0:T(128)} %bitcast.me_ref, bf16[4,512,768]{2,1,0:T(8,128)(2,1)} %get-tuple-element.186.x_ref, bf16[4,2304,512]{2,1,0:T(8,128)(2,1)} %get-tuple-element.238.g_ref, ...), custom_call_target="tpu_custom_call" | custom-call | flops 9422084096 | bytes 12582912 | tf_op jit(solution)/shard_map/qkv_grad/pallas_call | solution.py:614
  334.8 1.7 collective-permute-start.35
  336.8 1.7 collective-permute-start.34
  339.3 4.6 %fold.18 = (bf16[192,1536]{1,0:T(8,128)(2,1)}, bf16[192,1536]{1,0:T(8,128)(2,1)S(1)}, bf16[192,1152]{1,0:T(8,128)(2,1)}, bf16[192,1152]{1,0:T(8,128)(2,1)S(1)}, f32[1,1]{1,0:T(1,128)}) custom-call(s32[2]{0:T(128)S(1)} %pad_add_fusion.me_ref, bf16[2,192,1536]{2,1,0:T(8,128)(2,1)S(1)} %bitcast.91, bf16[2,192,1536]{2,1,0:T(8,128)(2,1)S(1)} %bitcast.92, ...), custom_call_target="tpu_custom_call" | custom-call | flops 1 | bytes 1 | tf_op jit(solution)/shard_map/fold/pallas_call | solution.py:835
  351.7 2.3 add_add_fusion.1
  354.0 4.5 %collective-permute-done.25 = bf16[192,1152]{1,0:T(8,128)(2,1)S(1)} collective-permute-done((bf16[192,1152]{1,0:T(8,128)(2,1)}, bf16[192,1152]{1,0:T(8,128)(2,1)S(1)}, u32[]{:S(2)}, u32[]{:S(2)}) %collective-permute-start.25) | collective-permute-done | bytes 442400 | tf_op jit(solution)/shard_map/ppermute | solution.py:643
  358.5 1.9 collective-permute-done.24
  360.4 2.1 fold.19
  371.9 2.6 collective-permute-start.30
  374.5 2.4 collective-permute-start.31
  377.1 2.6 collective-permute-done.31
  383.9 2.4 collective-permute-start.32
  390.0 2.1 fusion.7
  392.1 2.1 fusion.5
  (209 shorter events, 55.3 us)
Async XLA Ops:
  3.1 1.9 collective-permute-start
  5.8 4.8 %copy-start.49 = (f32[768]{0:T(1024)S(1)}, f32[768]{0:T(1024)}, u32[]{:S(2)}) copy-start(f32[768]{0:T(1024)} %param.23) | copy-start | bytes 9220
  5.8 4.8 %copy-start.50 = (f32[768]{0:T(1024)S(1)}, f32[768]{0:T(1024)}, u32[]{:S(2)}) copy-start(f32[768]{0:T(1024)} %param.24) | copy-start | bytes 9220
  5.8 4.8 %copy-start.51 = (f32[768]{0:T(1024)S(1)}, f32[768]{0:T(1024)}, u32[]{:S(2)}) copy-start(f32[768]{0:T(1024)} %param.28) | copy-start | bytes 9220
  5.8 4.8 %copy-start.52 = (f32[768]{0:T(1024)S(1)}, f32[768]{0:T(1024)}, u32[]{:S(2)}) copy-start(f32[768]{0:T(1024)} %param.29) | copy-start | bytes 9220
  5.8 4.8 %copy-start.53 = (f32[768]{0:T(1024)S(1)}, f32[768]{0:T(1024)}, u32[]{:S(2)}) copy-start(f32[768]{0:T(1024)} %param.30) | copy-start | bytes 9220
  7.4 9.6 %collective-permute-start.2 = (bf16[2,3,128,768]{3,2,1,0:T(8,128)(2,1)}, bf16[2,3,128,768]{3,2,1,0:T(8,128)(2,1)}, u32[]{:S(2)}, u32[]{:S(2)}) collective-permute-start(bf16[2,3,128,768]{3,2,1,0:T(8,128)(2,1)} %get-tuple-element.152), channel_id=1, source_target_pairs={{0,1},{1,0},{2,3},{3,2},{4,5},{5,4},{6,7},{7,6},{8,9},{9,8},{10,11... | collective-permute-start | bytes 3538952 | tf_op jit(solution)/shard_map/ppermute | solution.py:643
  7.9 12.6 %collective-permute-start.3 = (bf16[1,1,256,768]{3,2,1,0:T(8,128)(2,1)}, bf16[1,1,256,768]{3,2,1,0:T(8,128)(2,1)}, u32[]{:S(2)}, u32[]{:S(2)}) collective-permute-start(bf16[1,1,256,768]{3,2,1,0:T(8,128)(2,1)} %move.9.refs_2_.rest_0_), channel_id=1, source_target_pairs={{0,2},{1,3},{2,0},{3,1},{4,6},{5,7},{6,4},{7,5},{8,10},{9,11},{10,... | collective-permute-start | bytes 1179656 | tf_op jit(solution)/shard_map/ppermute | solution.py:643
  11.3 59.2 %collective-permute-start.1 = (bf16[2,4,128,768]{3,2,1,0:T(8,128)(2,1)}, bf16[2,4,128,768]{3,2,1,0:T(8,128)(2,1)S(1)}, u32[]{:S(2)}, u32[]{:S(2)}) collective-permute-start(bf16[2,4,128,768]{3,2,1,0:T(8,128)(2,1)} %get-tuple-element.151), channel_id=1, source_target_pairs={{0,1},{1,0},{2,3},{3,2},{4,5},{5,4},{6,7},{7,6},{8,9},{9,8},{10,11... | collective-permute-start | bytes 4718600 | tf_op jit(solution)/shard_map/ppermute | solution.py:643
  18.4 20.6 %collective-permute-start.5 = (bf16[1,1,256,768]{3,2,1,0:T(8,128)(2,1)S(1)}, bf16[1,1,256,768]{3,2,1,0:T(8,128)(2,1)S(1)}, u32[]{:S(2)}, u32[]{:S(2)}) collective-permute-start(bf16[1,1,256,768]{3,2,1,0:T(8,128)(2,1)S(1)} %move.11.refs_8_), channel_id=1, source_target_pairs={{0,2},{1,3},{2,0},{3,1},{4,6},{5,7},{6,4},{7,5},{8,10},{9,11},{10,... | collective-permute-start | bytes 1179656 | tf_op jit(solution)/shard_map/ppermute | solution.py:643
  36.9 18.8 %collective-permute-start.4 = (bf16[1,1,256,768]{3,2,1,0:T(8,128)(2,1)S(1)}, bf16[1,1,256,768]{3,2,1,0:T(8,128)(2,1)S(1)}, u32[]{:S(2)}, u32[]{:S(2)}) collective-permute-start(bf16[1,1,256,768]{3,2,1,0:T(8,128)(2,1)S(1)} %move.12.refs_8_), channel_id=1, source_target_pairs={{0,2},{1,3},{2,0},{3,1},{4,6},{5,7},{6,4},{7,5},{8,10},{9,11},{10,... | collective-permute-start | bytes 1179656 | tf_op jit(solution)/shard_map/ppermute | solution.py:643
  55.7 17.8 %collective-permute-start.7 = (bf16[1,1,256,768]{3,2,1,0:T(8,128)(2,1)S(1)}, bf16[1,1,256,768]{3,2,1,0:T(8,128)(2,1)S(1)}, u32[]{:S(2)}, u32[]{:S(2)}) collective-permute-start(bf16[1,1,256,768]{3,2,1,0:T(8,128)(2,1)S(1)} %move.13.refs_8_), channel_id=1, source_target_pairs={{0,2},{1,3},{2,0},{3,1},{4,6},{5,7},{6,4},{7,5},{8,10},{9,11},{10,... | collective-permute-start | bytes 1179656 | tf_op jit(solution)/shard_map/ppermute | solution.py:643
  55.8 14.8 %copy-start.3 = (bf16[16,128,768]{2,1,0:T(8,128)(2,1)S(1)}, bf16[16,128,768]{2,1,0:T(8,128)(2,1)}, u32[]{:S(2)}) copy-start(bf16[16,128,768]{2,1,0:T(8,128)(2,1)} %refs_0_.27) | copy-start | bytes 9437188
  71.4 18.7 %collective-permute-start.6 = (bf16[1,2,256,768]{3,2,1,0:T(8,128)(2,1)S(1)}, bf16[1,2,256,768]{3,2,1,0:T(8,128)(2,1)S(1)}, u32[]{:S(2)}, u32[]{:S(2)}) collective-permute-start(bf16[1,2,256,768]{3,2,1,0:T(8,128)(2,1)S(1)} %move.14.refs_8_), channel_id=1, source_target_pairs={{0,2},{1,3},{2,0},{3,1},{4,6},{5,7},{6,4},{7,5},{8,10},{9,11},{10,... | collective-permute-start | bytes 2359304 | tf_op jit(solution)/shard_map/ppermute | solution.py:643
  89.4 23.7 %collective-permute-start.8 = (bf16[1,2,256,768]{3,2,1,0:T(8,128)(2,1)S(1)}, bf16[1,2,256,768]{3,2,1,0:T(8,128)(2,1)S(1)}, u32[]{:S(2)}, u32[]{:S(2)}) collective-permute-start(bf16[1,2,256,768]{3,2,1,0:T(8,128)(2,1)S(1)} %move.15.refs_8_), channel_id=1, source_target_pairs={{0,2},{1,3},{2,0},{3,1},{4,6},{5,7},{6,4},{7,5},{8,10},{9,11},{10,... | collective-permute-start | bytes 2359304 | tf_op jit(solution)/shard_map/ppermute | solution.py:643
  111.0 24.9 %collective-permute-start.9 = (bf16[2,256,768]{2,1,0:T(8,128)(2,1)}, bf16[2,256,768]{2,1,0:T(8,128)(2,1)S(1)}, u32[]{:S(2)}, u32[]{:S(2)}) collective-permute-start(bf16[2,256,768]{2,1,0:T(8,128)(2,1)} %get-tuple-element.200), channel_id=1, source_target_pairs={{0,2},{1,3},{2,0},{3,1},{4,6},{5,7},{6,4},{7,5},{8,10},{9,11},{10,... | collective-permute-start | bytes 2359304 | tf_op jit(solution)/shard_map/ppermute | solution.py:643
  135.9 15.2 %copy-start.18 = (bf16[2,256,768]{2,1,0:T(8,128)(2,1)}, bf16[2,256,768]{2,1,0:T(8,128)(2,1)S(1)}, u32[]{:S(2)}) copy-start(bf16[2,256,768]{2,1,0:T(8,128)(2,1)S(1)} %collective-permute-done.9.rest_0_) | copy-start | bytes 2359300
  152.6 27.3 %collective-permute-start.10 = (bf16[1536,768]{1,0:T(8,128)(2,1)}, bf16[1536,768]{1,0:T(8,128)(2,1)}, u32[]{:S(2)}, u32[]{:S(2)}) collective-permute-start(bf16[1536,768]{1,0:T(8,128)(2,1)} %get-tuple-element.202), channel_id=1, source_target_pairs={{0,1},{1,0},{2,3},{3,2},{4,5},{5,4},{6,7},{7,6},{8,9},{9,8},{10,11... | collective-permute-start | bytes 7077896 | tf_op jit(solution)/shard_map/ppermute | solution.py:643
  152.7 27.2 %collective-permute-start.11 = (bf16[2,256,768]{2,1,0:T(8,128)(2,1)}, bf16[2,256,768]{2,1,0:T(8,128)(2,1)S(1)}, u32[]{:S(2)}, u32[]{:S(2)}) collective-permute-start(bf16[2,256,768]{2,1,0:T(8,128)(2,1)} %get-tuple-element.204), channel_id=1, source_target_pairs={{0,2},{1,3},{2,0},{3,1},{4,6},{5,7},{6,4},{7,5},{8,10},{9,11},{10,... | collective-permute-start | bytes 2359304 | tf_op jit(solution)/shard_map/ppermute | solution.py:643
  157.1 22.8 %copy-start.7 = (bf16[1536,768]{1,0:T(8,128)(2,1)S(1)}, bf16[1536,768]{1,0:T(8,128)(2,1)}, u32[]{:S(2)}) copy-start(bf16[1536,768]{1,0:T(8,128)(2,1)} %copy-done.6) | copy-start | bytes 7077892
  184.2 28.4 %collective-permute-start.12 = (bf16[768,768]{1,0:T(8,128)(2,1)S(1)}, bf16[768,768]{1,0:T(8,128)(2,1)S(1)}, u32[]{:S(2)}, u32[]{:S(2)}) collective-permute-start(bf16[768,768]{1,0:T(8,128)(2,1)S(1)} %get-tuple-element.205.rest_0_), channel_id=1, source_target_pairs={{0,4},{4,0},{8,12},{12,8},{16,20},{20,16},{24,28},{28,24},{1,5},{5... | collective-permute-start | bytes 3538952 | tf_op jit(solution)/shard_map/ppermute | solution.py:643
  214.6 20.5 %collective-permute-start.13 = (bf16[384,768]{1,0:T(8,128)(2,1)S(1)}, bf16[384,768]{1,0:T(8,128)(2,1)S(1)}, u32[]{:S(2)}, u32[]{:S(2)}) collective-permute-start(bf16[384,768]{1,0:T(8,128)(2,1)S(1)} %get-tuple-element.216.rest_0_), channel_id=1, source_target_pairs={{0,8},{4,12},{8,0},{12,4},{16,24},{20,28},{24,16},{28,20},{1,9},{5... | collective-permute-start | bytes 1769480 | tf_op jit(solution)/shard_map/ppermute | solution.py:643
  236.9 18.0 %collective-permute-start.15 = (bf16[384,3840]{1,0:T(8,128)(2,1)S(1)}, bf16[384,3840]{1,0:T(8,128)(2,1)S(1)}, u32[]{:S(2)}, u32[]{:S(2)}) collective-permute-start(bf16[384,3840]{1,0:T(8,128)(2,1)S(1)} %get-tuple-element.223), channel_id=1, source_target_pairs={{0,1},{1,0},{2,3},{3,2},{4,5},{5,4},{6,7},{7,6},{8,9},{9,8},{10,11... | collective-permute-start | bytes 8847368 | tf_op jit(solution)/shard_map/ppermute | solution.py:643
  236.9 18.0 %collective-permute-start.14 = (bf16[192,768]{1,0:T(8,128)(2,1)S(1)}, bf16[192,768]{1,0:T(8,128)(2,1)S(1)}, u32[]{:S(2)}, u32[]{:S(2)}) collective-permute-start(bf16[192,768]{1,0:T(8,128)(2,1)S(1)} %get-tuple-element.221.rest_0_), channel_id=1, source_target_pairs={{0,16},{4,20},{8,24},{12,28},{16,0},{20,4},{24,8},{28,12},{1,17},{... | collective-permute-start | bytes 884744 | tf_op jit(solution)/shard_map/ppermute | solution.py:643
  257.8 17.0 %copy-start.26 = (bf16[96,768]{1,0:T(8,128)(2,1)}, bf16[96,768]{1,0:T(8,128)(2,1)S(1)}, u32[]{:S(2)}) copy-start(bf16[96,768]{1,0:T(8,128)(2,1)S(1)} %get-tuple-element.228.rest_0_) | copy-start | bytes 442372
  257.8 19.3 %collective-permute-start.16 = (bf16[192,1920]{1,0:T(8,128)(2,1)S(1)}, bf16[192,1920]{1,0:T(8,128)(2,1)S(1)}, u32[]{:S(2)}, u32[]{:S(2)}) collective-permute-start(bf16[192,1920]{1,0:T(8,128)(2,1)S(1)} %get-tuple-element.226.rest_1_), channel_id=1, source_target_pairs={{0,4},{4,0},{8,12},{12,8},{16,20},{20,16},{24,28},{28,24},{1,5},{5... | collective-permute-start | bytes 2211848 | tf_op jit(solution)/shard_map/ppermute | solution.py:643
  259.4 32.9 %collective-permute-start.17 = (bf16[192,1920]{1,0:T(8,128)(2,1)S(1)}, bf16[192,1920]{1,0:T(8,128)(2,1)S(1)}, u32[]{:S(2)}, u32[]{:S(2)}) collective-permute-start(bf16[192,1920]{1,0:T(8,128)(2,1)S(1)} %get-tuple-element.227.rest_0_), channel_id=1, source_target_pairs={{0,4},{4,0},{8,12},{12,8},{16,20},{20,16},{24,28},{28,24},{1,5},{5... | collective-permute-start | bytes 2211848 | tf_op jit(solution)/shard_map/ppermute | solution.py:643
  274.8 35.1 %collective-permute-start.19 = (bf16[2,256,768]{2,1,0:T(8,128)(2,1)}, bf16[2,256,768]{2,1,0:T(8,128)(2,1)S(1)}, u32[]{:S(2)}, u32[]{:S(2)}) collective-permute-start(bf16[2,256,768]{2,1,0:T(8,128)(2,1)} %get-tuple-element.251), channel_id=1, source_target_pairs={{0,2},{1,3},{2,0},{3,1},{4,6},{5,7},{6,4},{7,5},{8,10},{9,11},{10,... | collective-permute-start | bytes 2359304 | tf_op jit(solution)/shard_map/ppermute | solution.py:643
  294.3 17.8 %collective-permute-start.18 = (bf16[96,3840]{1,0:T(8,128)(2,1)S(1)}, bf16[96,3840]{1,0:T(8,128)(2,1)S(1)}, u32[]{:S(2)}, u32[]{:S(2)}) collective-permute-start(bf16[96,3840]{1,0:T(8,128)(2,1)S(1)} %get-tuple-element.234.rest_0_), channel_id=1, source_target_pairs={{0,8},{4,12},{8,0},{12,4},{16,24},{20,28},{24,16},{28,20},{1,9},{5... | collective-permute-start | bytes 2211848 | tf_op jit(solution)/shard_map/ppermute | solution.py:643
  313.8 18.2 %collective-permute-start.20 = (bf16[48,3840]{1,0:T(8,128)(2,1)S(1)}, bf16[48,3840]{1,0:T(8,128)(2,1)S(1)}, u32[]{:S(2)}, u32[]{:S(2)}) collective-permute-start(bf16[48,3840]{1,0:T(8,128)(2,1)S(1)} %get-tuple-element.252.rest_10_), channel_id=1, source_target_pairs={{0,16},{4,20},{8,24},{12,28},{16,0},{20,4},{24,8},{28,12},{1,17},{... | collective-permute-start | bytes 1105928 | tf_op jit(solution)/shard_map/ppermute | solution.py:643
  334.3 4.9 %collective-permute-start.21 = (bf16[384,1536]{1,0:T(8,128)(2,1)}, bf16[384,1536]{1,0:T(8,128)(2,1)S(1)}, u32[]{:S(2)}, u32[]{:S(2)}) collective-permute-start(bf16[384,1536]{1,0:T(8,128)(2,1)} %get-tuple-element.258), channel_id=1, source_target_pairs={{0,1},{1,0},{2,3},{3,2},{4,5},{5,4},{6,7},{7,6},{8,9},{9,8},{10,11... | collective-permute-start | bytes 3538952 | tf_op jit(solution)/shard_map/ppermute | solution.py:643
  334.3 4.9 %collective-permute-start.22 = (bf16[384,1152]{1,0:T(8,128)(2,1)}, bf16[384,1152]{1,0:T(8,128)(2,1)}, u32[]{:S(2)}, u32[]{:S(2)}) collective-permute-start(bf16[384,1152]{1,0:T(8,128)(2,1)} %get-tuple-element.260), channel_id=1, source_target_pairs={{0,1},{1,0},{2,3},{3,2},{4,5},{5,4},{6,7},{7,6},{8,9},{9,8},{10,11... | collective-permute-start | bytes 2654216 | tf_op jit(solution)/shard_map/ppermute | solution.py:643
  334.8 16.9 %collective-permute-start.35 = (bf16[96,768]{1,0:T(8,128)(2,1)}, bf16[96,768]{1,0:T(8,128)(2,1)}, u32[]{:S(2)}, u32[]{:S(2)}) collective-permute-start(bf16[96,768]{1,0:T(8,128)(2,1)} %copy-done.26), channel_id=1, source_target_pairs={{0,2},{1,3},{2,0},{3,1},{4,6},{5,7},{6,4},{7,5},{8,10},{9,11},{10,... | collective-permute-start | bytes 442376 | tf_op jit(solution)/shard_map/ppermute | solution.py:643
  336.5 31.8 %collective-permute-start.26 = (bf16[2,256,768]{2,1,0:T(8,128)(2,1)}, bf16[2,256,768]{2,1,0:T(8,128)(2,1)}, u32[]{:S(2)}, u32[]{:S(2)}) collective-permute-start(bf16[2,256,768]{2,1,0:T(8,128)(2,1)} %get-tuple-element.271), channel_id=1, source_target_pairs={{0,2},{1,3},{2,0},{3,1},{4,6},{5,7},{6,4},{7,5},{8,10},{9,11},{10,... | collective-permute-start | bytes 2359304 | tf_op jit(solution)/shard_map/ppermute | solution.py:643
  336.8 27.5 %collective-permute-start.34 = (bf16[24,3840]{1,0:T(8,128)(2,1)}, bf16[24,3840]{1,0:T(8,128)(2,1)}, u32[]{:S(2)}, u32[]{:S(2)}) collective-permute-start(bf16[24,3840]{1,0:T(8,128)(2,1)} %copy-done.29), channel_id=1, source_target_pairs={{0,2},{1,3},{2,0},{3,1},{4,6},{5,7},{6,4},{7,5},{8,10},{9,11},{10,... | collective-permute-start | bytes 552968 | tf_op jit(solution)/shard_map/ppermute | solution.py:643
  345.5 15.0 %collective-permute-start.24 = (bf16[192,1536]{1,0:T(8,128)(2,1)}, bf16[192,1536]{1,0:T(8,128)(2,1)S(1)}, u32[]{:S(2)}, u32[]{:S(2)}) collective-permute-start(bf16[192,1536]{1,0:T(8,128)(2,1)} %get-tuple-element.266), channel_id=1, source_target_pairs={{0,4},{4,0},{8,12},{12,8},{16,20},{20,16},{24,28},{28,24},{1,5},{5... | collective-permute-start | bytes 1769480 | tf_op jit(solution)/shard_map/ppermute | solution.py:643
  347.0 11.5 %collective-permute-start.25 = (bf16[192,1152]{1,0:T(8,128)(2,1)}, bf16[192,1152]{1,0:T(8,128)(2,1)S(1)}, u32[]{:S(2)}, u32[]{:S(2)}) collective-permute-start(bf16[192,1152]{1,0:T(8,128)(2,1)} %get-tuple-element.268), channel_id=1, source_target_pairs={{0,8},{4,12},{8,0},{12,4},{16,24},{20,28},{24,16},{28,20},{1,9},{5... | collective-permute-start | bytes 1327112 | tf_op jit(solution)/shard_map/ppermute | solution.py:643
  349.5 10.9 %copy-start.15 = (bf16[192,1536]{1,0:T(8,128)(2,1)S(1)}, bf16[192,1536]{1,0:T(8,128)(2,1)}, u32[]{:S(2)}) copy-start(bf16[192,1536]{1,0:T(8,128)(2,1)} %copy-done.14) | copy-start | bytes 1769476
  349.6 10.9 %copy-start.17 = (bf16[192,1152]{1,0:T(8,128)(2,1)S(1)}, bf16[192,1152]{1,0:T(8,128)(2,1)}, u32[]{:S(2)}) copy-start(bf16[192,1152]{1,0:T(8,128)(2,1)} %copy-done.16) | copy-start | bytes 1327108
  351.7 38.3 %collective-permute-start.23 = (bf16[2,4,128,768]{3,2,1,0:T(8,128)(2,1)}, bf16[2,4,128,768]{3,2,1,0:T(8,128)(2,1)}, u32[]{:S(2)}, u32[]{:S(2)}) collective-permute-start(bf16[2,4,128,768]{3,2,1,0:T(8,128)(2,1)} %maximum_add_fusion), channel_id=1, source_target_pairs={{0,1},{1,0},{2,3},{3,2},{4,5},{5,4},{6,7},{7,6},{8,9},{9,8},{10,11... | collective-permute-start | bytes 4718600 | tf_op jit(solution)/shard_map/ppermute | solution.py:643
  362.5 5.7 %copy-start.42 = (bf16[2,256,768]{2,1,0:T(8,128)(2,1)S(1)}, bf16[2,256,768]{2,1,0:T(8,128)(2,1)}, u32[]{:S(2)}) copy-start(bf16[2,256,768]{2,1,0:T(8,128)(2,1)} %get-tuple-element.270) | copy-start | bytes 2359300
  362.5 7.7 %collective-permute-start.28 = (bf16[96,1536]{1,0:T(8,128)(2,1)S(1)}, bf16[96,1536]{1,0:T(8,128)(2,1)S(1)}, u32[]{:S(2)}, u32[]{:S(2)}) collective-permute-start(bf16[96,1536]{1,0:T(8,128)(2,1)S(1)} %get-tuple-element.273), channel_id=1, source_target_pairs={{0,8},{4,12},{8,0},{12,4},{16,24},{20,28},{24,16},{28,20},{1,9},{5... | collective-permute-start | bytes 884744 | tf_op jit(solution)/shard_map/ppermute | solution.py:643
  362.9 6.7 %collective-permute-start.29 = (bf16[96,1152]{1,0:T(8,128)(2,1)S(1)}, bf16[96,1152]{1,0:T(8,128)(2,1)S(1)}, u32[]{:S(2)}, u32[]{:S(2)}) collective-permute-start(bf16[96,1152]{1,0:T(8,128)(2,1)S(1)} %get-tuple-element.275), channel_id=1, source_target_pairs={{0,4},{4,0},{8,12},{12,8},{16,20},{20,16},{24,28},{28,24},{1,5},{5... | collective-permute-start | bytes 663560 | tf_op jit(solution)/shard_map/ppermute | solution.py:643
  371.9 7.8 %collective-permute-start.30 = (bf16[48,1536]{1,0:T(8,128)(2,1)S(1)}, bf16[48,1536]{1,0:T(8,128)(2,1)S(1)}, u32[]{:S(2)}, u32[]{:S(2)}) collective-permute-start(bf16[48,1536]{1,0:T(8,128)(2,1)S(1)} %get-tuple-element.277), channel_id=1, source_target_pairs={{0,16},{4,20},{8,24},{12,28},{16,0},{20,4},{24,8},{28,12},{1,17},{... | collective-permute-start | bytes 442376 | tf_op jit(solution)/shard_map/ppermute | solution.py:643
  374.5 5.2 %collective-permute-start.31 = (bf16[48,1152]{1,0:T(8,128)(2,1)S(1)}, bf16[48,1152]{1,0:T(8,128)(2,1)S(1)}, u32[]{:S(2)}, u32[]{:S(2)}) collective-permute-start(bf16[48,1152]{1,0:T(8,128)(2,1)S(1)} %get-tuple-element.279), channel_id=1, source_target_pairs={{0,2},{1,3},{2,0},{3,1},{4,6},{5,7},{6,4},{7,5},{8,10},{9,11},{10,... | collective-permute-start | bytes 331784 | tf_op jit(solution)/shard_map/ppermute | solution.py:643
  381.4 5.6 %collective-permute-start.33 = (bf16[24,1152]{1,0:T(8,128)(2,1)S(1)}, bf16[24,1152]{1,0:T(8,128)(2,1)S(1)}, u32[]{:S(2)}, u32[]{:S(2)}) collective-permute-start(bf16[24,1152]{1,0:T(8,128)(2,1)S(1)} %get-tuple-element.284), channel_id=1, source_target_pairs={{0,16},{4,20},{8,24},{12,28},{16,0},{20,4},{24,8},{28,12},{1,17},{... | collective-permute-start | bytes 165896 | tf_op jit(solution)/shard_map/ppermute | solution.py:643
  383.9 10.4 %collective-permute-start.27 = (bf16[2,4,128,768]{3,2,1,0:T(8,128)(2,1)S(1)}, bf16[2,4,128,768]{3,2,1,0:T(8,128)(2,1)S(1)}, u32[]{:S(2)}, u32[]{:S(2)}) collective-permute-start(bf16[2,4,128,768]{3,2,1,0:T(8,128)(2,1)S(1)} %maximum_add_fusion.1), channel_id=1, source_target_pairs={{0,1},{1,0},{2,3},{3,2},{4,5},{5,4},{6,7},{7,6},{8,9},{9,8},{10,11... | collective-permute-start | bytes 4718600 | tf_op jit(solution)/shard_map/ppermute | solution.py:643
  383.9 5.4 %collective-permute-start.32 = (bf16[24,1536]{1,0:T(8,128)(2,1)S(1)}, bf16[24,1536]{1,0:T(8,128)(2,1)S(1)}, u32[]{:S(2)}, u32[]{:S(2)}) collective-permute-start(bf16[24,1536]{1,0:T(8,128)(2,1)S(1)} %get-tuple-element.282), channel_id=1, source_target_pairs={{0,2},{1,3},{2,0},{3,1},{4,6},{5,7},{6,4},{7,5},{8,10},{9,11},{10,... | collective-permute-start | bytes 221192 | tf_op jit(solution)/shard_map/ppermute | solution.py:643
  (42 other events, 109.4 us)
